TPU v7x, 256 devices: a whole 4x4x8 slice. The times are simulated.
256 devices in a mesh: gx: 32 (over y, x, core), gy: 8 (over z).
Axes of the slice: x: 4, y: 4, z: 8, core: 2. Of those that a mesh axis runs over, the one named last changes fastest.
Arguments:
- edge_embed: bfloat16 [524288, 512], P(('gx', 'gy')), may hold values from -6 to 6
- cotangent: bfloat16 [524288, 512], P(('gx', 'gy')), may hold values from -6 to 6
- w_down: bfloat16 [512, 64], replicated, may hold values from -0.25 to 0.25
- w_bilinear: bfloat16 [512, 64], replicated, may hold values from -0.25 to 0.25
- w_up: bfloat16 [64, 512], replicated, may hold values from -0.75 to 0.75
- in_index: int32 [2304, 768], P(('gx', 'gy')), may hold values from 0 to 2047
- out_index: int32 [2304, 768], P(('gx', 'gy')), may hold values from 0 to 2047
- triplet_cos: float32 [2304, 768], P(('gx', 'gy')), may hold values from -1 to 1
- block_counts: int32 [2304, 12], P(('gx', 'gy')), may hold values from 1 to 64, as said below
Outputs:
- updated: bfloat16 [524288, 512], P(('gx', 'gy'))
- grad_embed: bfloat16 [524288, 512], P(('gx', 'gy'))
- grad_down: float32 [512, 64], replicated
- grad_bilinear: float32 [512, 64], replicated
- grad_up: float32 [64, 512], replicated
Inputs may be any that keep to these rules, and one draw needn't show every extreme that they name: `block_counts`: each group of nine rows (one grid block) has at least one entry equal to 64; loads differ from block to block.
All inputs are finite; a program needn't handle non-finite values.
Results may differ from a plain program's by a relative error of at most 0.007.
Values may be sent and summed in bfloat16 or wider, within the bound.
No kernel may reach another device: no remote copies, remote signals or barrier semaphores. Data moves between devices by JAX's collectives and lax.ppermute only.
A program may use at most 128 MiB of HBM per device.

v0:
```python
import jax
import jax.numpy as jnp
from jax import lax
from jax.sharding import PartitionSpec as P

L = 8
TB = 64
SLOTS = 768


def with_halo(shard, sides, width):
    for axis, dim in sides:
        devices, length = (lax.axis_size(axis), shard.shape[dim])
        up = [(i, (i + 1) % devices) for i in range(devices)]
        down = [(j, i) for i, j in up]
        last = lax.slice_in_dim(shard, length - width, length, axis=dim)
        initial = lax.slice_in_dim(shard, 0, width, axis=dim)
        before = lax.ppermute(last, axis, up)
        after = lax.ppermute(initial, axis, down)
        shard = jnp.concatenate([before, shard, after], axis=dim)
    return shard


def legendre(cosine):
    terms = [jnp.ones_like(cosine), cosine]
    for order in range(1, L - 1):
        terms.append(
            ((2 * order + 1) * cosine * terms[order] - order * terms[order - 1]) / (order + 1)
        )
    return jnp.stack(terms[:L], axis=-1)


def silu_grad(value):
    sig = jax.nn.sigmoid(value)
    return sig * (1.0 + value * (1.0 - sig))


def slot_mask(counts):
    position = jnp.arange(SLOTS, dtype=jnp.int32) % TB
    return (position < jnp.repeat(counts, TB, total_repeat_length=SLOTS)).astype(jnp.float32)


def one_hot_rows(index, count, dtype):
    return (index[:, None] == jnp.arange(count, dtype=jnp.int32)[None, :]).astype(dtype)


def pick_rows(table, index):
    selector = one_hot_rows(index, table.shape[0], table.dtype)
    return jnp.dot(selector, table, preferred_element_type=jnp.float32)


def collect_rows(values, index, count):
    selector = one_hot_rows(index, count, jnp.float32)
    return lax.dot_general(
        selector,
        values,
        (((0,), (0,)), ((), ())),
        precision=lax.Precision.HIGHEST,
        preferred_element_type=jnp.float32,
    )


def lift(source, in_idx, cosine):
    feat = pick_rows(source, in_idx)
    basis = legendre(cosine)
    lifted = (basis[:, :, None] * feat[:, None, :]).astype(jnp.bfloat16)
    return (lifted.reshape(SLOTS, -1), basis)


def pair_forward(source, in_idx, out_idx, cosine, counts, w_bil):
    lifted, basis = lift(source, in_idx, cosine)
    message = (
        jnp.dot(lifted, w_bil, preferred_element_type=jnp.float32) * slot_mask(counts)[:, None]
    )
    return collect_rows(message, out_idx, source.shape[0])


def masked_backward(source, in_idx, out_idx, cosine, valid, w_bil, d_trip):
    lifted, basis = lift(source, in_idx, cosine)
    picked = pick_rows(d_trip, out_idx).astype(jnp.bfloat16)
    d_message = picked * valid.astype(jnp.bfloat16)[:, None]
    grad_bil = jnp.dot(lifted.T, d_message, preferred_element_type=jnp.float32)
    d_lifted = jnp.dot(d_message, w_bil.T, preferred_element_type=jnp.float32)
    d_lifted = d_lifted.reshape(SLOTS, basis.shape[1], -1)
    d_feat = jnp.sum(basis[:, :, None] * d_lifted, axis=1)
    d_source = collect_rows(d_feat, in_idx, source.shape[0])
    return (d_source, grad_bil)


def shards(
    edge_embed, cotangent, w_down, w_bilinear, w_up, in_index, out_index, triplet_cos, block_counts
):
    edges = edge_embed.shape[0]
    width_t = w_down.shape[1]
    pre_down = jnp.dot(edge_embed, w_down, preferred_element_type=jnp.float32)
    down = jax.nn.silu(pre_down).astype(jnp.bfloat16)
    rim_down = with_halo(down[None, None], (("gx", 0), ("gy", 1)), 1)
    sources = rim_down.reshape(9, edges, width_t)

    def forward_step(total, pieces):
        source, in_idx, out_idx, cosine, counts = pieces
        return (total + pair_forward(source, in_idx, out_idx, cosine, counts, w_bilinear), None)

    trip, unused = lax.scan(
        forward_step,
        jnp.zeros((edges, width_t), jnp.float32),
        (sources, in_index, out_index, triplet_cos, block_counts),
    )
    trip_b = trip.astype(jnp.bfloat16)
    up_act = jnp.dot(trip_b, w_up, preferred_element_type=jnp.float32)
    updated = (edge_embed.astype(jnp.float32) + jax.nn.silu(up_act)).astype(jnp.bfloat16)
    cot_f = cotangent.astype(jnp.float32)
    d_act = (cot_f * silu_grad(up_act)).astype(jnp.bfloat16)
    grad_up_local = jnp.dot(trip_b.T, d_act, preferred_element_type=jnp.float32)
    d_trip = jnp.dot(d_act, w_up.T, preferred_element_type=jnp.float32).astype(jnp.bfloat16)
    valid_rows = jax.vmap(slot_mask)(block_counts)

    def backward_step(carry, pieces):
        source, in_idx, out_idx, cosine, valid = pieces
        d_source, g_bil = masked_backward(
            source, in_idx, out_idx, cosine, valid, w_bilinear, d_trip
        )
        return (carry + g_bil, d_source)

    grad_bil_local, d_sources = lax.scan(
        backward_step,
        jnp.zeros(w_bilinear.shape, jnp.float32),
        (sources, in_index, out_index, triplet_cos, valid_rows),
    )
    d_grid = d_sources.reshape(3, 3, edges, width_t)
    row_terms = jnp.stack([d_grid[:, 0], d_grid[:, 2]], axis=1)
    rim_rows = with_halo(row_terms, (("gy", 1),), 1)
    partial_sum = d_grid[:, 1] + rim_rows[:, 0] + rim_rows[:, 3]
    col_terms = jnp.stack([partial_sum[0], partial_sum[2]], axis=0)
    rim_cols = with_halo(col_terms, (("gx", 0),), 1)
    d_down = partial_sum[1] + rim_cols[0] + rim_cols[3]
    d_pre = (d_down * silu_grad(pre_down)).astype(jnp.bfloat16)
    grad_down_local = jnp.dot(edge_embed.T, d_pre, preferred_element_type=jnp.float32)
    grad_embed = (cot_f + jnp.dot(d_pre, w_down.T, preferred_element_type=jnp.float32)).astype(
        jnp.bfloat16
    )
    grad_down, grad_bil, grad_up = lax.psum(
        (grad_down_local, grad_bil_local, grad_up_local), ("gx", "gy")
    )
    scale = float(edges * lax.axis_size("gx") * lax.axis_size("gy")) ** (-0.5)
    return (updated, grad_embed, grad_down * scale, grad_bil * scale, grad_up * scale)


def solution(mesh):
    in_specs = (
        P(("gx", "gy"), None),
        P(("gx", "gy"), None),
        P(),
        P(),
        P(),
        P(("gx", "gy"), None),
        P(("gx", "gy"), None),
        P(("gx", "gy"), None),
        P(("gx", "gy"), None),
    )
    out_specs = (P(("gx", "gy"), None), P(("gx", "gy"), None), P(), P(), P())
    return jax.shard_map(shards, mesh=mesh, in_specs=in_specs, out_specs=out_specs, check_vma=False)
```

profile of v0, /device:TPU:1, one launch (start us, length us, event | category | flops | bytes accessed | tf_op | source)
XLA Modules:
  0.0 620.5 jit_solution(16415845239614318720)
XLA Ops:
  9.7 3.3 collective-permute-start.1
  13.3 3.2 collective-permute-done.1
  17.1 5.7 collective-permute-start.3
  26.5 5.1 collective-permute-done.3
  36.6 4.0 copy.25
  40.6 150.0 %while.34 = (s32[]{:T(128)}, f32[2048,64]{0,1:T(8,128)}, s32[9,768]{1,0:T(8,128)}, f32[9,768]{1,0:T(8,128)}, s32[9,768]{1,0:T(8,128)}, /*index=5*/bf16[9,2048,64...) while((s32[]{:T(128)}, f32[2048,64]{0,1:T(8,128)}, ...), condition=%wide.region_1.2_spmd.clone, body=%wide.region_0.1_spmd.clone.sunk | while | flops 1463922688 | bytes 8378379 | solution.py:104
  41.4 4.6 fusion.111
  58.1 4.6 fusion.111
  74.7 4.6 fusion.111
  91.4 4.6 fusion.111
  108.1 4.6 fusion.111
  124.7 4.6 fusion.111
  141.4 4.6 fusion.111
  158.1 4.6 fusion.111
  162.7 3.2 fusion.112
  174.7 4.6 fusion.111
  190.6 5.1 fusion.36
  198.8 99.9 %while.35 = (s32[]{:T(128)}, f32[512,64]{0,1:T(8,128)S(1)}, f32[9,2048,64]{1,2,0:T(8,128)}, f32[9,768]{1,0:T(8,128)}, s32[9,768]{1,0:T(8,128)}, /*index=5*/bf16[...) while((s32[]{:T(128)}, f32[512,64]{0,1:T(8,128)S(1)}, ...), condition=%wide.region_4.5_spmd.clone, body=%wide.region_2.4_spmd.clone.sunk | while | flops 1717709824 | bytes 7587495 | solution.py:125
  206.5 3.3 fusion.124
  217.6 3.3 fusion.124
  228.7 3.3 fusion.124
  239.8 3.3 fusion.124
  250.9 3.3 fusion.124
  262.0 3.3 fusion.124
  273.1 3.4 fusion.124
  284.2 3.4 fusion.124
  295.3 3.4 fusion.124
  303.6 24.9 %collective-permute-done.4 = f32[3,1,2048,64]{2,3,1,0:T(8,128)S(1)} collective-permute-done((f32[3,1,2048,64]{2,3,1,0:T(8,128)S(1)}, f32[3,1,2048,64]{2,3,1,0:T(8,128)S(1)}, u32[]{:S(2)}, u32[]{:S(2)}) %collective-permute-start.4) | collective-permute-done | bytes 1572896 | tf_op jit(solution)/shard_map/ppermute | solution.py:18
  330.4 18.9 %collective-permute-start.6 = (f32[1,2048,64]{1,2,0:T(8,128)S(1)}, f32[1,2048,64]{1,2,0:T(8,128)S(1)}, u32[]{:S(2)}, u32[]{:S(2)}) collective-permute-start(f32[1,2048,64]{1,2,0:T(8,128)S(1)} %get-tuple-element.597), channel_id=1, source_target_pairs={{0,8},{8,16},{16,24},{24,32},{32,40},{40,48},{48,56},{56,64},{64,7... | collective-permute-start | bytes 1572872 | tf_op jit(solution)/shard_map/ppermute | solution.py:18
  350.4 5.0 collective-permute-done.6
  359.6 3.7 fusion.37
  363.3 247.1 %all-reduce.3.cloned.1.call-done = (f32[512,64]{0,1:T(8,128)}, f32[512,64]{0,1:T(8,128)}, f32[64,512]{1,0:T(8,128)}) async-done(((f32[512,64]{0,1:T(8,128)}, f32[512,64]{0,1:T(8,128)}, f32[64,512]{1,0:T(8,128)}), (f32[512,64]{0,1:T(8,128)}, f32[512,64]{0,1:T(8,128)}, f32[64,512]{1,0:T(8,128)})) %all-reduce.3.cloned.1.call-update) | async-done | bytes 393232 | tf_op jit(solution)/shard_map/psum | solution.py:142
  (351 shorter events, 204.7 us)
Async XLA Ops:
  7.2 183.4 %copy-start = (bf16[64,512]{1,0:T(8,128)(2,1)S(1)}, bf16[64,512]{1,0:T(8,128)(2,1)}, u32[]{:S(2)}) copy-start(bf16[64,512]{1,0:T(8,128)(2,1)} %param.21) | copy-start | bytes 196612
  7.2 6.0 copy-start.9
  7.2 5.9 copy-start.14
  7.2 603.1 %all-reduce.3.cloned.1.call-start = ((), (), s32[]{:S(2)}) async-start(), calls=%async_computation | async-start | bytes 786432 | tf_op jit(solution)/shard_map/psum | solution.py:142
  9.7 6.7 %collective-permute-start.1 = (bf16[1,1,2048,64]{2,3,1,0:T(8,128)(2,1)S(1)}, bf16[1,1,2048,64]{2,3,1,0:T(8,128)(2,1)S(1)}, u32[]{:S(2)}, u32[]{:S(2)}) collective-permute-start(bf16[1,1,2048,64]{2,3,1,0:T(8,128)(2,1)S(1)} %fusion.44), channel_id=1, source_target_pairs={{8,0},{16,8},{24,16},{32,24},{40,32},{48,40},{56,48},{64,56},{72,6... | collective-permute-start | bytes 786440 | tf_op jit(solution)/shard_map/ppermute | solution.py:19
  13.1 3.9 collective-permute-start
  16.5 15.2 %copy-start.6 = (bf16[1,1,2048,64]{2,3,1,0:T(8,128)(2,1)}, bf16[1,1,2048,64]{2,3,1,0:T(8,128)(2,1)S(1)}, u32[]{:S(2)}) copy-start(bf16[1,1,2048,64]{2,3,1,0:T(8,128)(2,1)S(1)} %collective-permute-done.1) | copy-start | bytes 786436
  17.0 14.7 %copy-start.7 = (bf16[1,1,2048,64]{2,3,1,0:T(8,128)(2,1)}, bf16[1,1,2048,64]{2,3,1,0:T(8,128)(2,1)S(1)}, u32[]{:S(2)}) copy-start(bf16[1,1,2048,64]{2,3,1,0:T(8,128)(2,1)S(1)} %collective-permute-done) | copy-start | bytes 786436
  17.1 14.6 %collective-permute-start.3 = (bf16[3,1,2048,64]{2,3,1,0:T(8,128)(2,1)S(1)}, bf16[3,1,2048,64]{2,3,1,0:T(8,128)(2,1)S(1)}, u32[]{:S(2)}, u32[]{:S(2)}) collective-permute-start(bf16[3,1,2048,64]{2,3,1,0:T(8,128)(2,1)S(1)} %pad_maximum_fusion.1), channel_id=1, source_target_pairs={{1,0},{2,1},{3,2},{4,3},{5,4},{6,5},{7,6},{0,7},{9,8},{10,9},{11,1... | collective-permute-start | bytes 2359304 | tf_op jit(solution)/shard_map/ppermute | solution.py:19
  22.8 12.2 %collective-permute-start.2 = (bf16[3,1,2048,64]{2,3,1,0:T(8,128)(2,1)S(1)}, bf16[3,1,2048,64]{2,3,1,0:T(8,128)(2,1)}, u32[]{:S(2)}, u32[]{:S(2)}) collective-permute-start(bf16[3,1,2048,64]{2,3,1,0:T(8,128)(2,1)S(1)} %pad_maximum_fusion.1), channel_id=1, source_target_pairs={{0,1},{1,2},{2,3},{3,4},{4,5},{5,6},{6,7},{7,0},{8,9},{9,10},{10,1... | collective-permute-start | bytes 2359304 | tf_op jit(solution)/shard_map/ppermute | solution.py:18
  31.7 0.9 copy-start.8
  36.6 4.0 copy-start.4
  40.6 150.0 %copy-start.1 = (bf16[2048,512]{1,0:T(8,128)(2,1)S(1)}, bf16[2048,512]{1,0:T(8,128)(2,1)}, u32[]{:S(2)}) copy-start(bf16[2048,512]{1,0:T(8,128)(2,1)} %param.17) | copy-start | bytes 6291460
  50.9 3.0 copy-start.10
  56.5 0.8 copy-start.11
  67.6 3.0 copy-start.10
  84.2 3.0 copy-start.10
  100.9 3.0 copy-start.10
  117.6 3.0 copy-start.10
  134.2 3.0 copy-start.10
  150.9 3.0 copy-start.10
  167.6 3.0 copy-start.10
  184.2 3.0 copy-start.10
  195.7 1.3 copy-start.2
  298.7 2.1 copy-start.5
  300.8 27.7 %collective-permute-start.4 = (f32[3,1,2048,64]{2,3,1,0:T(8,128)S(1)}, f32[3,1,2048,64]{2,3,1,0:T(8,128)S(1)}, u32[]{:S(2)}, u32[]{:S(2)}) collective-permute-start(f32[3,1,2048,64]{2,3,1,0:T(8,128)S(1)} %get-tuple-element.593), channel_id=1, source_target_pairs={{0,1},{1,2},{2,3},{3,4},{4,5},{5,6},{6,7},{7,0},{8,9},{9,10},{10,1... | collective-permute-start | bytes 4718600 | tf_op jit(solution)/shard_map/ppermute | solution.py:18
  300.9 27.6 %collective-permute-start.5 = (f32[3,1,2048,64]{2,3,1,0:T(8,128)S(1)}, f32[3,1,2048,64]{2,3,1,0:T(8,128)S(1)}, u32[]{:S(2)}, u32[]{:S(2)}) collective-permute-start(f32[3,1,2048,64]{2,3,1,0:T(8,128)S(1)} %get-tuple-element.594), channel_id=1, source_target_pairs={{1,0},{2,1},{3,2},{4,3},{5,4},{6,5},{7,6},{0,7},{9,8},{10,9},{11,1... | collective-permute-start | bytes 4718600 | tf_op jit(solution)/shard_map/ppermute | solution.py:19
  328.5 20.8 %copy-start.12 = (f32[2048,64]{0,1:T(8,128)S(1)}, f32[2048,64]{0,1:T(8,128)}, u32[]{:S(2)}) copy-start(f32[2048,64]{0,1:T(8,128)} %get-tuple-element.390) | copy-start | bytes 1572868
  330.3 19.0 %copy-start.3 = (bf16[2048,512]{1,0:T(8,128)(2,1)S(1)}, bf16[2048,512]{1,0:T(8,128)(2,1)}, u32[]{:S(2)}) copy-start(bf16[2048,512]{1,0:T(8,128)(2,1)} %copy-done.2) | copy-start | bytes 6291460
  330.4 25.0 %collective-permute-start.6 = (f32[1,2048,64]{1,2,0:T(8,128)S(1)}, f32[1,2048,64]{1,2,0:T(8,128)S(1)}, u32[]{:S(2)}, u32[]{:S(2)}) collective-permute-start(f32[1,2048,64]{1,2,0:T(8,128)S(1)} %get-tuple-element.597), channel_id=1, source_target_pairs={{0,8},{8,16},{16,24},{24,32},{32,40},{40,48},{48,56},{56,64},{64,7... | collective-permute-start | bytes 1572872 | tf_op jit(solution)/shard_map/ppermute | solution.py:18
  349.3 8.9 %collective-permute-start.7 = (f32[1,2048,64]{1,2,0:T(8,128)S(1)}, f32[1,2048,64]{1,2,0:T(8,128)S(1)}, u32[]{:S(2)}, u32[]{:S(2)}) collective-permute-start(f32[1,2048,64]{1,2,0:T(8,128)S(1)} %get-tuple-element.598), channel_id=1, source_target_pairs={{8,0},{16,8},{24,16},{32,24},{40,32},{48,40},{56,48},{64,56},{72,6... | collective-permute-start | bytes 1572872 | tf_op jit(solution)/shard_map/ppermute | solution.py:19
  350.4 9.2 %copy-start.13 = (bf16[512,64]{0,1:T(8,128)(2,1)S(1)}, bf16[512,64]{0,1:T(8,128)(2,1)}, u32[]{:S(2)}) copy-start(bf16[512,64]{0,1:T(8,128)(2,1)} %param.19) | copy-start | bytes 196612
  (8 other events, 6.3 us)
Sparse Core Ops, SparseCore 0:
  359.7 250.5 all-reduce.2
where the time goes:
time: 625 us; the launch traced here: 620 us
  waiting for transfers between devices  291 us (47%)
  matrix products  146 us (23%)
  other arithmetic  97.1 us (16%)
  local copies, waits for them, and re-layouts  40.6 us (6%)
  starting transfers between devices  30.7 us (5%)
  between operations  14.2 us (2%)
    psum x1, waiting for transfers between devices, shards(): lax.psum((grad_down_local, grad_bil_local, grad_up_local), ('gx', 'gy'))  247 us
    dot_general x27, matrix products, pick_rows(): return jnp.dot(selector, table, preferred_element_type=jnp.float32)  68.6 us
    dot_general x18, matrix products, collect_rows(): lax.dot_general(selector, values, (((0,), (0,)), ((), ())), precision=lax...  53.6 us
    gather x19, other arithmetic, slot_mask(): jnp.repeat(counts, TB, total_repeat_length=SLOTS)  41.7 us
    ppermute x4, waiting for transfers between devices, with_halo(): before = lax.ppermute(last, axis, up)  32.7 us
    convert_element_type x10, other arithmetic, slot_mask(): (position < jnp.repeat(counts, TB, total_repeat_length=SLOTS)).astype(jnp...  30 us
    ppermute x4, starting transfers between devices, with_halo(): before = lax.ppermute(last, axis, up)  19 us
    div x54, other arithmetic, legendre(): ((2 * order + 1) * cosine * terms[order] - order * terms[order - 1]) / (o...  14.4 us
  transfers between devices with their start and end apart: 9, of which 8 were waited for; matrix products, arithmetic and copies ran while one was open for 1% of the time, Pallas kernels for 0%

commit v1 on v0

v1 whole, which is shorter than its diff:
```python
import functools

import jax
import jax.numpy as jnp
from jax import lax
from jax.experimental import pallas as pl
from jax.experimental.pallas import tpu as pltpu
from jax.sharding import PartitionSpec as P

L = 8
DT = 64
TB = 64
SLOTS = 768
Q = 256
F32 = jnp.float32
BF16 = jnp.bfloat16
VMEM_LIMIT = 48 * 2**20

NN = (((1,), (0,)), ((), ()))
NT = (((1,), (1,)), ((), ()))
TN = (((0,), (0,)), ((), ()))


def dot(a, b, dims):
    return lax.dot_general(a, b, dims, preferred_element_type=F32)


def sigmoid(value):
    return 0.5 * jnp.tanh(0.5 * value) + 0.5


def legendre(cosine):
    terms = [jnp.ones_like(cosine), cosine]
    for order in range(1, L - 1):
        terms.append(
            ((2 * order + 1) * cosine * terms[order] - order * terms[order - 1])
            * (1.0 / (order + 1))
        )
    return terms


def valid_row(counts_ref, k):
    lane = lax.broadcasted_iota(jnp.int32, (1, 2 * TB), 1)
    rows = []
    for t in range(SLOTS // (2 * TB)):
        count = jnp.where(lane < TB, counts_ref[k, 2 * t], counts_ref[k, 2 * t + 1])
        rows.append(((lane & (TB - 1)) < count).astype(F32))
    return jnp.concatenate(rows, axis=1)


def one_hot(index):
    low = (index & (Q - 1)).astype(F32).astype(BF16)
    row = lax.broadcasted_iota(jnp.int32, (Q, 128), 0).astype(F32).astype(BF16)
    row = jnp.concatenate([row] * (SLOTS // 128), axis=1)
    return jnp.where(row == low, jnp.ones((), BF16), jnp.zeros((), BF16))


def stacked(table):
    parts = table.shape[1] // Q
    return jnp.concatenate([table[:, r * Q : (r + 1) * Q] for r in range(parts)], axis=0)


def pick(table, hot, high):
    parts = table.shape[1] // Q
    found = dot(stacked(table), hot, NN)
    total = found[:DT]
    for r in range(1, parts):
        total = jnp.where(high == r, found[r * DT : (r + 1) * DT], total)
    return total


def collect(values, hot, high, parts):
    low = values.astype(BF16)
    zero = jnp.zeros((), BF16)
    rows = [jnp.where(high == r, low, zero) for r in range(parts)]
    return dot(jnp.concatenate(rows, axis=0), hot, NT)


def expand(basis, values):
    return jnp.concatenate([(row * values).astype(BF16) for row in basis], axis=0)


def down_kernel(edge_ref, w_ref, down_ref, slope_ref):
    pre = dot(w_ref[...], edge_ref[...], (((0,), (1,)), ((), ())))
    sig = sigmoid(pre)
    down_ref[...] = (pre * sig).astype(BF16)
    slope_ref[...] = sig * (1.0 + pre * (1.0 - sig))


def forward_kernel(pairs, base, counts_ref, in_ref, out_ref, cos_ref, w_ref, *refs):
    n = len(pairs)
    sources = refs[:n]
    total_ref = refs[n] if base else None
    trip_ref, feat_ref = refs[-2:]
    w_t = w_ref[...].T
    parts = sources[0].shape[1] // Q
    for i, k in enumerate(pairs):
        in_idx = in_ref[k : k + 1, :]
        out_idx = out_ref[k : k + 1, :]
        feat = pick(sources[i][...], one_hot(in_idx), in_idx // Q)
        feat_ref[i * DT : (i + 1) * DT, :] = feat.astype(BF16)
        lifted = expand(legendre(cos_ref[k : k + 1, :]), feat)
        message = dot(w_t, lifted, NN) * valid_row(counts_ref, k)
        part = collect(message, one_hot(out_idx), out_idx // Q, parts)
        if i == 0:
            trip_ref[...] = part + total_ref[...] if base else part
        else:
            trip_ref[...] += part


def middle_kernel(edge_ref, cot_ref, trip_ref, w_ref, updated_ref, d_trip_ref, grad_ref):
    trip = trip_ref[...].astype(BF16)
    up_act = dot(trip, w_ref[...], TN)
    sig = sigmoid(up_act)
    silu = up_act * sig
    updated_ref[...] = (edge_ref[...].astype(F32) + silu).astype(BF16)
    slope = sig * (1.0 + up_act - silu)
    d_act = (cot_ref[...].astype(F32) * slope).astype(BF16)
    d_trip_ref[...] = dot(w_ref[...], d_act, NT).astype(BF16)
    part = dot(trip, d_act, NN)

    @pl.when(pl.program_id(0) == 0)
    def _():
        grad_ref[...] = part

    @pl.when(pl.program_id(0) > 0)
    def _():
        grad_ref[...] += part


def backward_kernel(pairs, base, counts_ref, in_ref, out_ref, cos_ref, w_ref, d_trip_ref, *refs):
    feat_refs = refs[: len(pairs)]
    grad_base = refs[len(pairs)] if base else None
    d_ref, grad_ref = refs[-2:]
    w = w_ref[...]
    w_rows = jnp.concatenate([w[l * DT : (l + 1) * DT] for l in range(L)], axis=1)
    d_trip = d_trip_ref[...]
    parts = d_trip.shape[1] // Q
    for i, k in enumerate(pairs):
        in_idx = in_ref[k : k + 1, :]
        out_idx = out_ref[k : k + 1, :]
        d_message = pick(d_trip, one_hot(out_idx), out_idx // Q) * valid_row(counts_ref, k)
        spread = expand(legendre(cos_ref[k : k + 1, :]), d_message)
        part = dot(feat_refs[i][...], spread, NT)
        if i == 0:
            grad_ref[...] = part + grad_base[...] if base else part
        else:
            grad_ref[...] += part
        d_feat = dot(w_rows, spread, NN)
        d_source = collect(d_feat, one_hot(in_idx), in_idx // Q, parts).astype(d_ref.dtype)
        for r in range(parts):
            d_ref[i, :, r * Q : (r + 1) * Q] = d_source[r * DT : (r + 1) * DT]


def final_kernel(edge_ref, slope_ref, *refs):
    terms = refs[:-2]
    d_pre_ref, grad_ref = refs[-2:]
    d_down = terms[0][...].astype(F32)
    for term in terms[1:]:
        d_down = d_down + term[...].astype(F32)
    d_pre = (d_down * slope_ref[...]).astype(BF16)
    d_pre_ref[...] = d_pre
    grad_ref[...] = dot(d_pre, edge_ref[...], NN)


def embed_kernel(cot_ref, d_pre_ref, w_ref, grad_ref):
    part = dot(d_pre_ref[...], w_ref[...], (((0,), (1,)), ((), ())))
    grad_ref[...] = (cot_ref[...].astype(F32) + part).astype(BF16)


def finish_kernel(scale, down_ref, bil_ref, up_ref, out_down, out_bil, out_up):
    out_down[...] = down_ref[...].T * scale
    for l in range(L):
        out_bil[l * DT : (l + 1) * DT, :] = bil_ref[:, l * DT : (l + 1) * DT] * scale
    out_up[...] = up_ref[...] * scale


def call(kernel, outs, args, us, smem=()):
    vmem = pl.BlockSpec(memory_space=pltpu.VMEM)
    scalar = pl.BlockSpec(memory_space=pltpu.SMEM)
    return pl.pallas_call(
        kernel,
        out_shape=outs,
        in_specs=[scalar if i in smem else vmem for i in range(len(args))],
        out_specs=jax.tree.map(lambda _: vmem, outs),
        compiler_params=pltpu.CompilerParams(vmem_limit_bytes=VMEM_LIMIT),
        cost_estimate=pl.CostEstimate(
            flops=int(us * 1.0e9), bytes_accessed=int(us * 3.0e6), transcendentals=0
        ),
    )(*args)


def shift(x, axis, step):
    n = lax.axis_size(axis)
    return lax.ppermute(x, axis, [(i, (i + step) % n) for i in range(n)])


def all_sum(x):
    nx, ny = lax.axis_size("gx"), lax.axis_size("gy")
    core = lax.rem(lax.axis_index("gx"), 2)
    half = x.shape[0] // 2

    def swap(value, axis, partner):
        n = lax.axis_size(axis)
        return lax.ppermute(value, axis, [(i, partner(i)) for i in range(n)])

    low, high = x[:half], x[half:]
    mine = jnp.where(core == 0, low, high)
    total = mine + swap(jnp.where(core == 0, high, low), "gx", lambda i: i ^ 1)
    side = 4
    steps = []
    for unit in (2, 2 * side):
        steps.append(("gx", lambda i, u=unit: i ^ u))
        steps.append(
            ("gx", lambda i, u=unit: i + (side - 1 - 2 * (i // u % side)) * u)
        )
    bit = 1
    while bit < ny:
        steps.append(("gy", lambda i, b=bit: i ^ b))
        bit *= 2
    for axis, partner in steps:
        total = total + swap(total, axis, partner)
    other = swap(total, "gx", lambda i: i ^ 1)
    first = jnp.where(core == 0, total, other)
    second = jnp.where(core == 0, other, total)
    return jnp.concatenate([first, second], axis=0)


def shards(
    edge_embed, cotangent, w_down, w_bilinear, w_up, in_index, out_index, triplet_cos, block_counts
):
    edges, width = edge_embed.shape
    struct = jax.ShapeDtypeStruct
    table = struct((DT, edges), BF16)
    stack = struct((edges // Q * DT, Q), F32)
    wide = struct((DT, width), F32)
    slots = (block_counts, in_index, out_index, triplet_cos, w_bilinear)

    down, slope = call(
        down_kernel, (table, struct((DT, edges), F32)), (edge_embed, w_down), 3
    )
    source = {4: down}
    source[3] = shift(down, "gy", 1)
    source[5] = shift(down, "gy", -1)
    source[1] = shift(down, "gx", 1)
    source[7] = shift(down, "gx", -1)
    source[0] = shift(source[3], "gx", 1)
    source[2] = shift(source[5], "gx", 1)
    source[6] = shift(source[3], "gx", -1)
    source[8] = shift(source[5], "gx", -1)

    feats = {}
    trip = None
    for pairs in ((4,), (3, 5, 1, 7), (0, 2, 6, 8)):
        n = len(pairs)
        base = trip is not None
        args = slots + tuple(source[k] for k in pairs) + ((trip,) if base else ())
        trip, feat = call(
            functools.partial(forward_kernel, pairs, base),
            (stack, struct((n * DT, SLOTS), BF16)),
            args,
            n,
            smem=(0,),
        )
        for i, k in enumerate(pairs):
            feats[k] = feat[i * DT : (i + 1) * DT]

    steps = edges // Q
    updated, d_trip, grad_up = pl.pallas_call(
        middle_kernel,
        grid=(steps,),
        out_shape=(struct((edges, width), BF16), table, wide),
        in_specs=[
            pl.BlockSpec((Q, width), lambda r: (r, 0)),
            pl.BlockSpec((Q, width), lambda r: (r, 0)),
            pl.BlockSpec((DT, Q), lambda r: (r, 0)),
            pl.BlockSpec((DT, width), lambda r: (0, 0)),
        ],
        out_specs=(
            pl.BlockSpec((Q, width), lambda r: (r, 0)),
            pl.BlockSpec((DT, Q), lambda r: (0, r)),
            pl.BlockSpec((DT, width), lambda r: (0, 0)),
        ),
        compiler_params=pltpu.CompilerParams(vmem_limit_bytes=VMEM_LIMIT),
        cost_estimate=pl.CostEstimate(
            flops=5_000_000_000, bytes_accessed=15_000_000, transcendentals=0
        ),
    )(edge_embed, cotangent, trip, w_up)

    d_source = {}
    grad_bil = None
    for pairs in ((0, 1, 2), (6, 7, 8), (3, 4, 5)):
        n = len(pairs)
        base = grad_bil is not None
        args = slots + (d_trip,) + tuple(feats[k] for k in pairs) + ((grad_bil,) if base else ())
        out, grad_bil = call(
            functools.partial(backward_kernel, pairs, base),
            (struct((n, DT, edges), BF16), wide),
            args,
            n,
            smem=(0,),
        )
        d_source[pairs[0] // 3] = out
    before = shift(d_source[2], "gx", 1)
    after = shift(d_source[0], "gx", -1)
    rows = d_source[1].astype(F32) + before.astype(F32) + after.astype(F32)
    below = shift(rows[2].astype(BF16), "gy", 1)
    above = shift(rows[0].astype(BF16), "gy", -1)

    d_pre, grad_down = call(
        final_kernel, (table, wide), (edge_embed, slope, rows[1], below, above), 3
    )
    grad_embed = pl.pallas_call(
        embed_kernel,
        grid=(steps,),
        out_shape=struct((edges, width), BF16),
        in_specs=[
            pl.BlockSpec((Q, width), lambda r: (r, 0)),
            pl.BlockSpec((DT, Q), lambda r: (0, r)),
            pl.BlockSpec((width, DT), lambda r: (0, 0)),
        ],
        out_specs=pl.BlockSpec((Q, width), lambda r: (r, 0)),
        compiler_params=pltpu.CompilerParams(vmem_limit_bytes=VMEM_LIMIT),
        cost_estimate=pl.CostEstimate(
            flops=3_000_000_000, bytes_accessed=9_000_000, transcendentals=0
        ),
    )(cotangent, d_pre, w_down)

    early = all_sum(jnp.concatenate([grad_bil, grad_up], axis=0))
    late = all_sum(grad_down)
    scale = float(edges * lax.axis_size("gx") * lax.axis_size("gy")) ** (-0.5)
    grad_down, grad_bil, grad_up = call(
        functools.partial(finish_kernel, scale),
        (struct((width, DT), F32), struct((L * DT, DT), F32), wide),
        (late, early[:DT], early[DT:]),
        2,
    )
    return (updated, grad_embed, grad_down, grad_bil, grad_up)


def solution(mesh):
    both = P(("gx", "gy"), None)
    in_specs = (both, both, P(), P(), P(), both, both, both, both)
    out_specs = (both, both, P(), P(), P())
    return jax.shard_map(shards, mesh=mesh, in_specs=in_specs, out_specs=out_specs, check_vma=False)
```

time: 625 us -> 136 us (0.22)
  waiting for transfers between devices: 291 us -> 36.5 us
  matrix products: 146 us -> 0 us
  other arithmetic: 97.1 us -> 0.74 us
  local copies, waits for them, and re-layouts: 40.6 us -> 5.12 us
  Pallas kernels: 0 us -> 32.5 us
  starting transfers between devices: 30.7 us -> 60.3 us
  between operations: 14.2 us -> 1.04 us
    psum x1 -> x0, waiting for transfers between devices: 247 us -> none  [shards(): lax.psum((grad_down_local, grad_bil_local, grad_up_local), ('gx', 'gy'))]
    dot_general x78 -> x0, matrix products: 146 us -> none  [the longest x27 68.6 us: pick_rows(): return jnp.dot(selector, table, preferred_element_type=jnp.float32)]
    gather x19 -> x0, other arithmetic: 41.7 us -> none  [slot_mask(): jnp.repeat(counts, TB, total_repeat_length=SLOTS)]
    pallas_call x0 -> x11, Pallas kernels: none -> 32.5 us  [the longest x9 22.5 us: call(): pl.pallas_call(kernel, out_shape=outs, in_specs=[scalar if i in smem else...]
    convert_element_type x20 -> x0, other arithmetic: 31.2 us -> none  [the longest x10 30 us: slot_mask(): (position < jnp.repeat(counts, TB, total_repeat_length=SLOTS)).astype(jnp...]
    ppermute x8 -> x30, starting transfers between devices: 30.6 us -> 60.3 us  [the longest x18 36 us: swap(): return lax.ppermute(value, axis, [(i, partner(i)) for i in range(n)])]
    div x54 -> x0, other arithmetic: 14.4 us -> none  [legendre(): ((2 * order + 1) * cosine * terms[order] - order * terms[order - 1]) / (o...]
    dynamic_slice x27 -> x0, local copies, waits for them, and re-layouts: 14.1 us -> none  [shards(): lax.scan(forward_step, jnp.zeros((edges, width_t), jnp.float32), (sources...]
  transfers between devices with their start and end apart: 9 -> 30, of which waited for: 8 -> 13; matrix products, arithmetic and copies ran while one was open for 1% -> 1% of each run, Pallas kernels for 0% -> 13%
where the time goes in v1:
time: 136 us
  starting transfers between devices  60.3 us (44%)
  waiting for transfers between devices  36.5 us (27%)
  Pallas kernels  32.5 us (24%)
  local copies, waits for them, and re-layouts  5.12 us (4%)
    ppermute x18, starting transfers between devices, swap(): return lax.ppermute(value, axis, [(i, partner(i)) for i in range(n)])  36 us
    ppermute x18, waiting for transfers between devices, swap(): return lax.ppermute(value, axis, [(i, partner(i)) for i in range(n)])  30.9 us
    ppermute x12, starting transfers between devices, shift(): return lax.ppermute(x, axis, [(i, (i + step) % n) for i in range(n)])  24.3 us
    pallas_call x9, Pallas kernels, call(): pl.pallas_call(kernel, out_shape=outs, in_specs=[scalar if i in smem else...  22.5 us
    pallas_call x1, Pallas kernels, shards(): pl.pallas_call(middle_kernel, grid=(steps,), out_shape=(struct((edges, wi...  5.91 us
    ppermute x12, waiting for transfers between devices, shift(): return lax.ppermute(x, axis, [(i, (i + step) % n) for i in range(n)])  5.65 us
    unnamed x22, local copies, waits for them, and re-layouts  4.99 us
    pallas_call x1, Pallas kernels, shards(): pl.pallas_call(embed_kernel, grid=(steps,), out_shape=struct((edges, widt...  4.11 us
  transfers between devices with their start and end apart: 30, of which 13 were waited for; matrix products, arithmetic and copies ran while one was open for 1% of the time, Pallas kernels for 13%

profile of v1, /device:TPU:1, one launch (start us, length us, event | category | flops | bytes accessed | tf_op | source)
XLA Modules:
  0.0 136.2 jit_solution(1624100032606876151)
XLA Ops:
  4.0 2.5 %collective-permute-start = (bf16[64,2048]{1,0:T(8,128)(2,1)S(1)}, bf16[64,2048]{1,0:T(8,128)(2,1)S(1)}, u32[]{:S(2)}, u32[]{:S(2)}) collective-permute-start(bf16[64,2048]{1,0:T(8,128)(2,1)S(1)} %get-tuple-element.27.refs_0_), channel_id=1, source_target_pairs={{0,1},{1,2},{2,3},{3,4},{4,5},{5,6},{6,7},{7,0},{8,9},{9,10},{10,1... | collective-permute-start | bytes 786440 | tf_op jit(solution)/shard_map/ppermute | solution.py:195
  6.6 4.0 %collective-permute-start.2 = (bf16[64,2048]{1,0:T(8,128)(2,1)S(1)}, bf16[64,2048]{1,0:T(8,128)(2,1)S(1)}, u32[]{:S(2)}, u32[]{:S(2)}) collective-permute-start(bf16[64,2048]{1,0:T(8,128)(2,1)S(1)} %get-tuple-element.27.refs_0_), channel_id=1, source_target_pairs={{0,7},{1,0},{2,1},{3,2},{4,3},{5,4},{6,5},{7,6},{8,15},{9,8},{10,9... | collective-permute-start | bytes 786440 | tf_op jit(solution)/shard_map/ppermute | solution.py:195
  10.6 2.0 %collective-permute-start.6 = (bf16[64,2048]{1,0:T(8,128)(2,1)S(1)}, bf16[64,2048]{1,0:T(8,128)(2,1)S(1)}, u32[]{:S(2)}, u32[]{:S(2)}) collective-permute-start(bf16[64,2048]{1,0:T(8,128)(2,1)S(1)} %get-tuple-element.27.refs_0_), channel_id=1, source_target_pairs={{0,8},{8,16},{16,24},{24,32},{32,40},{40,48},{48,56},{56,64},{64,7... | collective-permute-start | bytes 786440 | tf_op jit(solution)/shard_map/ppermute | solution.py:195
  16.5 2.3 %collective-permute-start.1 = (bf16[64,2048]{1,0:T(8,128)(2,1)S(1)}, bf16[64,2048]{1,0:T(8,128)(2,1)S(1)}, u32[]{:S(2)}, u32[]{:S(2)}) collective-permute-start(bf16[64,2048]{1,0:T(8,128)(2,1)S(1)} %collective-permute-done.refs_0_), channel_id=1, source_target_pairs={{0,8},{8,16},{16,24},{24,32},{32,40},{40,48},{48,56},{56,64},{64,7... | collective-permute-start | bytes 786440 | tf_op jit(solution)/shard_map/ppermute | solution.py:195
  20.6 3.4 %collective-permute-start.5 = (bf16[64,2048]{1,0:T(8,128)(2,1)S(1)}, bf16[64,2048]{1,0:T(8,128)(2,1)S(1)}, u32[]{:S(2)}, u32[]{:S(2)}) collective-permute-start(bf16[64,2048]{1,0:T(8,128)(2,1)S(1)} %collective-permute-done.2.refs_1_), channel_id=1, source_target_pairs={{0,248},{8,0},{16,8},{24,16},{32,24},{40,32},{48,40},{56,48},{64,5... | collective-permute-start | bytes 786440 | tf_op jit(solution)/shard_map/ppermute | solution.py:195
  24.0 3.7 %shard_map.130 = (f32[512,256]{1,0:T(8,128)S(1)}, bf16[256,768]{1,0:T(8,128)(2,1)S(1)}) custom-call(s32[9,12]{1,0:T(8,128)S(1)} %copy-done.7, s32[9,768]{1,0:T(8,128)S(1)} %copy-done.4, s32[9,768]{1,0:T(8,128)S(1)} %copy-done.5, f32[9,768]{1,0:T(8,128)S(1)} %copy-done.6, bf16[512,64]{1,0:T(8,128)(2,1)S(1)} %copy.17.w_ref, ...), custom_call_target="tpu_custom_call" | custom-call | flops 4000000000 | bytes 12000000 | tf_op jit(solution)/shard_map/pallas_call | solution.py:181
  27.8 3.7 %shard_map.131 = (f32[512,256]{1,0:T(8,128)S(1)}, bf16[256,768]{1,0:T(8,128)(2,1)S(1)}) custom-call(s32[9,12]{1,0:T(8,128)S(1)} %copy-done.7, s32[9,768]{1,0:T(8,128)S(1)} %copy-done.4, s32[9,768]{1,0:T(8,128)S(1)} %copy-done.5, f32[9,768]{1,0:T(8,128)S(1)} %copy-done.6, bf16[512,64]{1,0:T(8,128)(2,1)S(1)} %copy.17.w_ref, ...), custom_call_target="tpu_custom_call" | custom-call | flops 4000000000 | bytes 12000000 | tf_op jit(solution)/shard_map/pallas_call | solution.py:181
  32.4 5.9 %shard_map.132 = (bf16[2048,512]{1,0:T(8,128)(2,1)}, bf16[64,2048]{1,0:T(8,128)(2,1)S(1)}, f32[64,512]{1,0:T(8,128)S(1)}) custom-call(bf16[2048,512]{1,0:T(8,128)(2,1)S(1)} %copy-done.1, bf16[2048,512]{1,0:T(8,128)(2,1)S(1)} %copy-done.2, f32[512,256]{1,0:T(8,128)S(1)} %get-tuple-element.30.trip_ref, bf16[64,512]{1,0:T(8,128)(2,1)S(1)} %copy-done.3), custom_call_target="tpu_custom_call" | custom-call | flops 5000000000 | bytes 15000000 | tf_op jit(solution)/shard_map/pallas_call | solution.py:269
  38.3 3.7 %shard_map.133 = (bf16[3,64,2048]{2,1,0:T(8,128)(2,1)S(1)}, f32[64,512]{1,0:T(8,128)S(1)}) custom-call(s32[9,12]{1,0:T(8,128)S(1)} %copy-done.7, s32[9,768]{1,0:T(8,128)S(1)} %copy-done.4, s32[9,768]{1,0:T(8,128)S(1)} %copy-done.5, f32[9,768]{1,0:T(8,128)S(1)} %copy-done.6, bf16[512,64]{1,0:T(8,128)(2,1)S(1)} %copy.17.w_ref, ...), custom_call_target="tpu_custom_call" | custom-call | flops 3000000000 | bytes 9000000 | tf_op jit(solution)/shard_map/pallas_call | solution.py:181
  42.1 5.1 %collective-permute-start.9 = (bf16[3,64,2048]{2,1,0:T(8,128)(2,1)S(1)}, bf16[3,64,2048]{2,1,0:T(8,128)(2,1)S(1)}, u32[]{:S(2)}, u32[]{:S(2)}) collective-permute-start(bf16[3,64,2048]{2,1,0:T(8,128)(2,1)S(1)} %get-tuple-element.41), channel_id=1, source_target_pairs={{0,248},{8,0},{16,8},{24,16},{32,24},{40,32},{48,40},{56,48},{64,5... | collective-permute-start | bytes 2359304 | tf_op jit(solution)/shard_map/ppermute | solution.py:195
  47.2 3.7 %shard_map.134 = (bf16[3,64,2048]{2,1,0:T(8,128)(2,1)S(1)}, f32[64,512]{1,0:T(8,128)S(1)}) custom-call(s32[9,12]{1,0:T(8,128)S(1)} %copy-done.7, s32[9,768]{1,0:T(8,128)S(1)} %copy-done.4, s32[9,768]{1,0:T(8,128)S(1)} %copy-done.5, f32[9,768]{1,0:T(8,128)S(1)} %copy-done.6, bf16[512,64]{1,0:T(8,128)(2,1)S(1)} %copy.17.w_ref, ...), custom_call_target="tpu_custom_call" | custom-call | flops 3000000000 | bytes 9000000 | tf_op jit(solution)/shard_map/pallas_call | solution.py:181
  51.2 3.7 %shard_map.135 = (bf16[3,64,2048]{2,1,0:T(8,128)(2,1)S(1)}, f32[64,512]{1,0:T(8,128)S(1)}) custom-call(s32[9,12]{1,0:T(8,128)S(1)} %copy-done.7, s32[9,768]{1,0:T(8,128)S(1)} %copy-done.4, s32[9,768]{1,0:T(8,128)S(1)} %copy-done.5, f32[9,768]{1,0:T(8,128)S(1)} %copy-done.6, bf16[512,64]{1,0:T(8,128)(2,1)S(1)} %copy.17.w_ref, ...), custom_call_target="tpu_custom_call" | custom-call | flops 3000000000 | bytes 9000000 | tf_op jit(solution)/shard_map/pallas_call | solution.py:181
  55.0 5.1 %collective-permute-start.21 = (f32[64,512]{1,0:T(8,128)S(1)}, f32[64,512]{1,0:T(8,128)S(1)}, u32[]{:S(2)}, u32[]{:S(2)}) collective-permute-start(f32[64,512]{1,0:T(8,128)S(1)} %broadcast_select_fusion.2), channel_id=1, source_target_pairs={{0,8},{8,0},{16,24},{24,16},{32,40},{40,32},{48,56},{56,48},{64,72... | collective-permute-start | bytes 393224 | tf_op jit(solution)/shard_map/ppermute | solution.py:205
  61.3 4.7 %collective-permute-done.22 = f32[64,512]{1,0:T(8,128)S(1)} collective-permute-done((f32[64,512]{1,0:T(8,128)S(1)}, f32[64,512]{1,0:T(8,128)S(1)}, u32[]{:S(2)}, u32[]{:S(2)}) %collective-permute-start.22) | collective-permute-done | bytes 131104 | tf_op jit(solution)/shard_map/ppermute | solution.py:205
  66.1 5.0 %collective-permute-done.23 = f32[64,512]{1,0:T(8,128)S(1)} collective-permute-done((f32[64,512]{1,0:T(8,128)S(1)}, f32[64,512]{1,0:T(8,128)S(1)}, u32[]{:S(2)}, u32[]{:S(2)}) %collective-permute-start.23) | collective-permute-done | bytes 131104 | tf_op jit(solution)/shard_map/ppermute | solution.py:205
  71.2 3.8 %collective-permute-done.24 = f32[64,512]{1,0:T(8,128)S(1)} collective-permute-done((f32[64,512]{1,0:T(8,128)S(1)}, f32[64,512]{1,0:T(8,128)S(1)}, u32[]{:S(2)}, u32[]{:S(2)}) %collective-permute-start.24) | collective-permute-done | bytes 131104 | tf_op jit(solution)/shard_map/ppermute | solution.py:205
  75.1 3.5 %collective-permute-start.25 = (f32[64,512]{1,0:T(8,128)S(1)}, f32[64,512]{1,0:T(8,128)S(1)}, u32[]{:S(2)}, u32[]{:S(2)}) collective-permute-start(f32[64,512]{1,0:T(8,128)S(1)} %add.67), channel_id=1, source_target_pairs={{0,192},{8,200},{16,208},{24,216},{32,224},{40,232},{48,240},{56,2... | collective-permute-start | bytes 393224 | tf_op jit(solution)/shard_map/ppermute | solution.py:205
  79.1 2.7 %collective-permute-start.11 = (bf16[64,2048]{1,0:T(8,128)(2,1)S(1)}, bf16[64,2048]{1,0:T(8,128)(2,1)S(1)}, u32[]{:S(2)}, u32[]{:S(2)}) collective-permute-start(bf16[64,2048]{1,0:T(8,128)(2,1)S(1)} %get-tuple-element.56), channel_id=1, source_target_pairs={{0,7},{1,0},{2,1},{3,2},{4,3},{5,4},{6,5},{7,6},{8,15},{9,8},{10,9... | collective-permute-start | bytes 786440 | tf_op jit(solution)/shard_map/ppermute | solution.py:195
  81.8 3.7 %collective-permute-done.10.refs_1_ = bf16[64,2048]{1,0:T(8,128)(2,1)S(1)} collective-permute-done((bf16[64,2048]{1,0:T(8,128)(2,1)S(1)}, bf16[64,2048]{1,0:T(8,128)(2,1)S(1)}, u32[]{:S(2)}, u32[]{:S(2)}) %collective-permute-start.10) | collective-permute-done | bytes 262176 | tf_op jit(solution)/shard_map/ppermute | solution.py:195
  86.0 4.2 %collective-permute-start.12 = (f32[32,512]{1,0:T(8,128)S(1)}, f32[32,512]{1,0:T(8,128)S(1)}, u32[]{:S(2)}, u32[]{:S(2)}) collective-permute-start(f32[32,512]{1,0:T(8,128)S(1)} %slice_select_fusion), channel_id=1, source_target_pairs={{0,8},{8,0},{16,24},{24,16},{32,40},{40,32},{48,56},{56,48},{64,72... | collective-permute-start | bytes 196616 | tf_op jit(solution)/shard_map/ppermute | solution.py:205
  91.3 3.4 %collective-permute-done.13 = f32[32,512]{1,0:T(8,128)S(1)} collective-permute-done((f32[32,512]{1,0:T(8,128)S(1)}, f32[32,512]{1,0:T(8,128)S(1)}, u32[]{:S(2)}, u32[]{:S(2)}) %collective-permute-start.13) | collective-permute-done | bytes 65568 | tf_op jit(solution)/shard_map/ppermute | solution.py:205
  94.7 2.8 %collective-permute-start.14 = (f32[32,512]{1,0:T(8,128)S(1)}, f32[32,512]{1,0:T(8,128)S(1)}, u32[]{:S(2)}, u32[]{:S(2)}) collective-permute-start(f32[32,512]{1,0:T(8,128)S(1)} %add.57), channel_id=1, source_target_pairs={{0,48},{8,56},{16,32},{24,40},{32,16},{40,24},{48,0},{56,8},{64,11... | collective-permute-start | bytes 196616 | tf_op jit(solution)/shard_map/ppermute | solution.py:205
  97.5 4.3 %collective-permute-start.27 = (f32[64,512]{1,0:T(8,128)S(1)}, f32[64,512]{1,0:T(8,128)S(1)}, u32[]{:S(2)}, u32[]{:S(2)}) collective-permute-start(f32[64,512]{1,0:T(8,128)S(1)} %add.69), channel_id=1, source_target_pairs={{0,2},{1,3},{2,0},{3,1},{4,6},{5,7},{6,4},{7,5},{8,10},{9,11},{10,... | collective-permute-start | bytes 393224 | tf_op jit(solution)/shard_map/ppermute | solution.py:205
  102.0 3.4 %collective-permute-done.15 = f32[32,512]{1,0:T(8,128)S(1)} collective-permute-done((f32[32,512]{1,0:T(8,128)S(1)}, f32[32,512]{1,0:T(8,128)S(1)}, u32[]{:S(2)}, u32[]{:S(2)}) %collective-permute-start.15) | collective-permute-done | bytes 65568 | tf_op jit(solution)/shard_map/ppermute | solution.py:205
  105.5 2.6 %collective-permute-done.27 = f32[64,512]{1,0:T(8,128)S(1)} collective-permute-done((f32[64,512]{1,0:T(8,128)S(1)}, f32[64,512]{1,0:T(8,128)S(1)}, u32[]{:S(2)}, u32[]{:S(2)}) %collective-permute-start.27) | collective-permute-done | bytes 131104 | tf_op jit(solution)/shard_map/ppermute | solution.py:205
  108.1 2.5 %collective-permute-start.28 = (f32[64,512]{1,0:T(8,128)S(1)}, f32[64,512]{1,0:T(8,128)S(1)}, u32[]{:S(2)}, u32[]{:S(2)}) collective-permute-start(f32[64,512]{1,0:T(8,128)S(1)} %add.70), channel_id=1, source_target_pairs={{0,4},{1,5},{2,6},{3,7},{4,0},{5,1},{6,2},{7,3},{8,12},{9,13},{10,... | collective-permute-start | bytes 393224 | tf_op jit(solution)/shard_map/ppermute | solution.py:205
  110.9 5.1 %collective-permute-done.17 = f32[32,512]{1,0:T(8,128)S(1)} collective-permute-done((f32[32,512]{1,0:T(8,128)S(1)}, f32[32,512]{1,0:T(8,128)S(1)}, u32[]{:S(2)}, u32[]{:S(2)}) %collective-permute-start.17) | collective-permute-done | bytes 65568 | tf_op jit(solution)/shard_map/ppermute | solution.py:205
  116.1 3.5 %collective-permute-start.18 = (f32[32,512]{1,0:T(8,128)S(1)}, f32[32,512]{1,0:T(8,128)S(1)}, u32[]{:S(2)}, u32[]{:S(2)}) collective-permute-start(f32[32,512]{1,0:T(8,128)S(1)} %add.61), channel_id=1, source_target_pairs={{0,2},{1,3},{2,0},{3,1},{4,6},{5,7},{6,4},{7,5},{8,10},{9,11},{10,... | collective-permute-start | bytes 196616 | tf_op jit(solution)/shard_map/ppermute | solution.py:205
  119.6 2.0 %collective-permute-start.29 = (f32[64,512]{1,0:T(8,128)S(1)}, f32[64,512]{1,0:T(8,128)S(1)}, u32[]{:S(2)}, u32[]{:S(2)}) collective-permute-start(f32[64,512]{1,0:T(8,128)S(1)} %add.71), channel_id=1, source_target_pairs={{0,8},{8,0},{16,24},{24,16},{32,40},{40,32},{48,56},{56,48},{64,72... | collective-permute-start | bytes 393224 | tf_op jit(solution)/shard_map/ppermute | solution.py:205
  121.7 2.9 %collective-permute-start.19 = (f32[32,512]{1,0:T(8,128)S(1)}, f32[32,512]{1,0:T(8,128)S(1)}, u32[]{:S(2)}, u32[]{:S(2)}) collective-permute-start(f32[32,512]{1,0:T(8,128)S(1)} %add.62), channel_id=1, source_target_pairs={{0,4},{1,5},{2,6},{3,7},{4,0},{5,1},{6,2},{7,3},{8,12},{9,13},{10,... | collective-permute-start | bytes 196616 | tf_op jit(solution)/shard_map/ppermute | solution.py:205
  124.6 4.1 %shard_map.137 = bf16[2048,512]{1,0:T(8,128)(2,1)} custom-call(bf16[2048,512]{1,0:T(8,128)(2,1)S(1)} %copy-done.2, bf16[64,2048]{1,0:T(8,128)(2,1)S(1)} %get-tuple-element.42.d_pre_ref, bf16[512,64]{1,0:T(8,128)(2,1)S(1)} %copy.14.w_ref), custom_call_target="tpu_custom_call" | custom-call | flops 3000000000 | bytes 9000000 | tf_op jit(solution)/shard_map/pallas_call | solution.py:313
  128.9 4.1 %collective-permute-start.20 = (f32[32,512]{1,0:T(8,128)S(1)}, f32[32,512]{1,0:T(8,128)S(1)}, u32[]{:S(2)}, u32[]{:S(2)}) collective-permute-start(f32[32,512]{1,0:T(8,128)S(1)} %add.63), channel_id=1, source_target_pairs={{0,8},{8,0},{16,24},{24,16},{32,40},{40,32},{48,56},{56,48},{64,72... | collective-permute-start | bytes 196616 | tf_op jit(solution)/shard_map/ppermute | solution.py:205
  (86 shorter events, 17.7 us)
Async XLA Ops:
  3.2 9.6 %copy-start.6 = (f32[9,768]{1,0:T(8,128)S(1)}, f32[9,768]{1,0:T(8,128)}, u32[]{:S(2)}) copy-start(f32[9,768]{1,0:T(8,128)} %cos_ref.11) | copy-start | bytes 82948
  3.2 9.6 %copy-start.7 = (s32[9,12]{1,0:T(8,128)S(1)}, s32[9,12]{1,0:T(8,128)}, u32[]{:S(2)}) copy-start(s32[9,12]{1,0:T(8,128)} %counts_ref.11) | copy-start | bytes 1300
  4.0 12.5 %collective-permute-start = (bf16[64,2048]{1,0:T(8,128)(2,1)S(1)}, bf16[64,2048]{1,0:T(8,128)(2,1)S(1)}, u32[]{:S(2)}, u32[]{:S(2)}) collective-permute-start(bf16[64,2048]{1,0:T(8,128)(2,1)S(1)} %get-tuple-element.27.refs_0_), channel_id=1, source_target_pairs={{0,1},{1,2},{2,3},{3,4},{4,5},{5,6},{6,7},{7,0},{8,9},{9,10},{10,1... | collective-permute-start | bytes 786440 | tf_op jit(solution)/shard_map/ppermute | solution.py:195
  6.6 12.3 %collective-permute-start.2 = (bf16[64,2048]{1,0:T(8,128)(2,1)S(1)}, bf16[64,2048]{1,0:T(8,128)(2,1)S(1)}, u32[]{:S(2)}, u32[]{:S(2)}) collective-permute-start(bf16[64,2048]{1,0:T(8,128)(2,1)S(1)} %get-tuple-element.27.refs_0_), channel_id=1, source_target_pairs={{0,7},{1,0},{2,1},{3,2},{4,3},{5,4},{6,5},{7,6},{8,15},{9,8},{10,9... | collective-permute-start | bytes 786440 | tf_op jit(solution)/shard_map/ppermute | solution.py:195
  10.6 10.0 %collective-permute-start.6 = (bf16[64,2048]{1,0:T(8,128)(2,1)S(1)}, bf16[64,2048]{1,0:T(8,128)(2,1)S(1)}, u32[]{:S(2)}, u32[]{:S(2)}) collective-permute-start(bf16[64,2048]{1,0:T(8,128)(2,1)S(1)} %get-tuple-element.27.refs_0_), channel_id=1, source_target_pairs={{0,8},{8,16},{16,24},{24,32},{32,40},{40,48},{48,56},{56,64},{64,7... | collective-permute-start | bytes 786440 | tf_op jit(solution)/shard_map/ppermute | solution.py:195
  12.6 11.4 %collective-permute-start.7 = (bf16[64,2048]{1,0:T(8,128)(2,1)S(1)}, bf16[64,2048]{1,0:T(8,128)(2,1)S(1)}, u32[]{:S(2)}, u32[]{:S(2)}) collective-permute-start(bf16[64,2048]{1,0:T(8,128)(2,1)S(1)} %get-tuple-element.27.refs_0_), channel_id=1, source_target_pairs={{0,248},{8,0},{16,8},{24,16},{32,24},{40,32},{48,40},{56,48},{64,5... | collective-permute-start | bytes 786440 | tf_op jit(solution)/shard_map/ppermute | solution.py:195
  16.5 11.2 %collective-permute-start.1 = (bf16[64,2048]{1,0:T(8,128)(2,1)S(1)}, bf16[64,2048]{1,0:T(8,128)(2,1)S(1)}, u32[]{:S(2)}, u32[]{:S(2)}) collective-permute-start(bf16[64,2048]{1,0:T(8,128)(2,1)S(1)} %collective-permute-done.refs_0_), channel_id=1, source_target_pairs={{0,8},{8,16},{16,24},{24,32},{32,40},{40,48},{48,56},{56,64},{64,7... | collective-permute-start | bytes 786440 | tf_op jit(solution)/shard_map/ppermute | solution.py:195
  18.9 8.9 %collective-permute-start.4 = (bf16[64,2048]{1,0:T(8,128)(2,1)S(1)}, bf16[64,2048]{1,0:T(8,128)(2,1)S(1)}, u32[]{:S(2)}, u32[]{:S(2)}) collective-permute-start(bf16[64,2048]{1,0:T(8,128)(2,1)S(1)} %collective-permute-done.refs_0_), channel_id=1, source_target_pairs={{0,248},{8,0},{16,8},{24,16},{32,24},{40,32},{48,40},{56,48},{64,5... | collective-permute-start | bytes 786440 | tf_op jit(solution)/shard_map/ppermute | solution.py:195
  18.9 8.9 %collective-permute-start.3 = (bf16[64,2048]{1,0:T(8,128)(2,1)S(1)}, bf16[64,2048]{1,0:T(8,128)(2,1)S(1)}, u32[]{:S(2)}, u32[]{:S(2)}) collective-permute-start(bf16[64,2048]{1,0:T(8,128)(2,1)S(1)} %collective-permute-done.2.refs_1_), channel_id=1, source_target_pairs={{0,8},{8,16},{16,24},{24,32},{32,40},{40,48},{48,56},{56,64},{64,7... | collective-permute-start | bytes 786440 | tf_op jit(solution)/shard_map/ppermute | solution.py:195
  20.6 7.2 %collective-permute-start.5 = (bf16[64,2048]{1,0:T(8,128)(2,1)S(1)}, bf16[64,2048]{1,0:T(8,128)(2,1)S(1)}, u32[]{:S(2)}, u32[]{:S(2)}) collective-permute-start(bf16[64,2048]{1,0:T(8,128)(2,1)S(1)} %collective-permute-done.2.refs_1_), channel_id=1, source_target_pairs={{0,248},{8,0},{16,8},{24,16},{32,24},{40,32},{48,40},{56,48},{64,5... | collective-permute-start | bytes 786440 | tf_op jit(solution)/shard_map/ppermute | solution.py:195
  42.1 36.5 %collective-permute-start.9 = (bf16[3,64,2048]{2,1,0:T(8,128)(2,1)S(1)}, bf16[3,64,2048]{2,1,0:T(8,128)(2,1)S(1)}, u32[]{:S(2)}, u32[]{:S(2)}) collective-permute-start(bf16[3,64,2048]{2,1,0:T(8,128)(2,1)S(1)} %get-tuple-element.41), channel_id=1, source_target_pairs={{0,248},{8,0},{16,8},{24,16},{32,24},{40,32},{48,40},{56,48},{64,5... | collective-permute-start | bytes 2359304 | tf_op jit(solution)/shard_map/ppermute | solution.py:195
  50.9 27.6 %collective-permute-start.8 = (bf16[3,64,2048]{2,1,0:T(8,128)(2,1)S(1)}, bf16[3,64,2048]{2,1,0:T(8,128)(2,1)S(1)}, u32[]{:S(2)}, u32[]{:S(2)}) collective-permute-start(bf16[3,64,2048]{2,1,0:T(8,128)(2,1)S(1)} %get-tuple-element.40), channel_id=1, source_target_pairs={{0,8},{8,16},{16,24},{24,32},{32,40},{40,48},{48,56},{56,64},{64,7... | collective-permute-start | bytes 2359304 | tf_op jit(solution)/shard_map/ppermute | solution.py:195
  55.0 6.1 %collective-permute-start.21 = (f32[64,512]{1,0:T(8,128)S(1)}, f32[64,512]{1,0:T(8,128)S(1)}, u32[]{:S(2)}, u32[]{:S(2)}) collective-permute-start(f32[64,512]{1,0:T(8,128)S(1)} %broadcast_select_fusion.2), channel_id=1, source_target_pairs={{0,8},{8,0},{16,24},{24,16},{32,40},{40,32},{48,56},{56,48},{64,72... | collective-permute-start | bytes 393224 | tf_op jit(solution)/shard_map/ppermute | solution.py:205
  61.2 4.8 %collective-permute-start.22 = (f32[64,512]{1,0:T(8,128)S(1)}, f32[64,512]{1,0:T(8,128)S(1)}, u32[]{:S(2)}, u32[]{:S(2)}) collective-permute-start(f32[64,512]{1,0:T(8,128)S(1)} %select_add_fusion), channel_id=1, source_target_pairs={{0,16},{8,24},{16,0},{24,8},{32,48},{40,56},{48,32},{56,40},{64,80... | collective-permute-start | bytes 393224 | tf_op jit(solution)/shard_map/ppermute | solution.py:205
  66.0 5.1 %collective-permute-start.23 = (f32[64,512]{1,0:T(8,128)S(1)}, f32[64,512]{1,0:T(8,128)S(1)}, u32[]{:S(2)}, u32[]{:S(2)}) collective-permute-start(f32[64,512]{1,0:T(8,128)S(1)} %add.65), channel_id=1, source_target_pairs={{0,48},{8,56},{16,32},{24,40},{32,16},{40,24},{48,0},{56,8},{64,11... | collective-permute-start | bytes 393224 | tf_op jit(solution)/shard_map/ppermute | solution.py:205
  71.1 3.9 %collective-permute-start.24 = (f32[64,512]{1,0:T(8,128)S(1)}, f32[64,512]{1,0:T(8,128)S(1)}, u32[]{:S(2)}, u32[]{:S(2)}) collective-permute-start(f32[64,512]{1,0:T(8,128)S(1)} %add.66), channel_id=1, source_target_pairs={{0,64},{8,72},{16,80},{24,88},{32,96},{40,104},{48,112},{56,120},{... | collective-permute-start | bytes 393224 | tf_op jit(solution)/shard_map/ppermute | solution.py:205
  75.1 15.2 %collective-permute-start.25 = (f32[64,512]{1,0:T(8,128)S(1)}, f32[64,512]{1,0:T(8,128)S(1)}, u32[]{:S(2)}, u32[]{:S(2)}) collective-permute-start(f32[64,512]{1,0:T(8,128)S(1)} %add.67), channel_id=1, source_target_pairs={{0,192},{8,200},{16,208},{24,216},{32,224},{40,232},{48,240},{56,2... | collective-permute-start | bytes 393224 | tf_op jit(solution)/shard_map/ppermute | solution.py:205
  79.0 6.5 %collective-permute-start.10 = (bf16[64,2048]{1,0:T(8,128)(2,1)S(1)}, bf16[64,2048]{1,0:T(8,128)(2,1)S(1)}, u32[]{:S(2)}, u32[]{:S(2)}) collective-permute-start(bf16[64,2048]{1,0:T(8,128)(2,1)S(1)} %get-tuple-element.57), channel_id=1, source_target_pairs={{0,1},{1,2},{2,3},{3,4},{4,5},{5,6},{6,7},{7,0},{8,9},{9,10},{10,1... | collective-permute-start | bytes 786440 | tf_op jit(solution)/shard_map/ppermute | solution.py:195
  79.1 6.4 %collective-permute-start.11 = (bf16[64,2048]{1,0:T(8,128)(2,1)S(1)}, bf16[64,2048]{1,0:T(8,128)(2,1)S(1)}, u32[]{:S(2)}, u32[]{:S(2)}) collective-permute-start(bf16[64,2048]{1,0:T(8,128)(2,1)S(1)} %get-tuple-element.56), channel_id=1, source_target_pairs={{0,7},{1,0},{2,1},{3,2},{4,3},{5,4},{6,5},{7,6},{8,15},{9,8},{10,9... | collective-permute-start | bytes 786440 | tf_op jit(solution)/shard_map/ppermute | solution.py:195
  86.0 5.1 %collective-permute-start.12 = (f32[32,512]{1,0:T(8,128)S(1)}, f32[32,512]{1,0:T(8,128)S(1)}, u32[]{:S(2)}, u32[]{:S(2)}) collective-permute-start(f32[32,512]{1,0:T(8,128)S(1)} %slice_select_fusion), channel_id=1, source_target_pairs={{0,8},{8,0},{16,24},{24,16},{32,40},{40,32},{48,56},{56,48},{64,72... | collective-permute-start | bytes 196616 | tf_op jit(solution)/shard_map/ppermute | solution.py:205
  90.3 7.2 %collective-permute-start.26 = (f32[64,512]{1,0:T(8,128)S(1)}, f32[64,512]{1,0:T(8,128)S(1)}, u32[]{:S(2)}, u32[]{:S(2)}) collective-permute-start(f32[64,512]{1,0:T(8,128)S(1)} %add.68), channel_id=1, source_target_pairs={{0,1},{1,0},{2,3},{3,2},{4,5},{5,4},{6,7},{7,6},{8,9},{9,8},{10,11... | collective-permute-start | bytes 393224 | tf_op jit(solution)/shard_map/ppermute | solution.py:205
  91.2 3.5 %collective-permute-start.13 = (f32[32,512]{1,0:T(8,128)S(1)}, f32[32,512]{1,0:T(8,128)S(1)}, u32[]{:S(2)}, u32[]{:S(2)}) collective-permute-start(f32[32,512]{1,0:T(8,128)S(1)} %select_add_fusion.1), channel_id=1, source_target_pairs={{0,16},{8,24},{16,0},{24,8},{32,48},{40,56},{48,32},{56,40},{64,80... | collective-permute-start | bytes 196616 | tf_op jit(solution)/shard_map/ppermute | solution.py:205
  94.7 7.2 %collective-permute-start.14 = (f32[32,512]{1,0:T(8,128)S(1)}, f32[32,512]{1,0:T(8,128)S(1)}, u32[]{:S(2)}, u32[]{:S(2)}) collective-permute-start(f32[32,512]{1,0:T(8,128)S(1)} %add.57), channel_id=1, source_target_pairs={{0,48},{8,56},{16,32},{24,40},{32,16},{40,24},{48,0},{56,8},{64,11... | collective-permute-start | bytes 196616 | tf_op jit(solution)/shard_map/ppermute | solution.py:205
  97.5 10.5 %collective-permute-start.27 = (f32[64,512]{1,0:T(8,128)S(1)}, f32[64,512]{1,0:T(8,128)S(1)}, u32[]{:S(2)}, u32[]{:S(2)}) collective-permute-start(f32[64,512]{1,0:T(8,128)S(1)} %add.69), channel_id=1, source_target_pairs={{0,2},{1,3},{2,0},{3,1},{4,6},{5,7},{6,4},{7,5},{8,10},{9,11},{10,... | collective-permute-start | bytes 393224 | tf_op jit(solution)/shard_map/ppermute | solution.py:205
  101.9 3.5 %collective-permute-start.15 = (f32[32,512]{1,0:T(8,128)S(1)}, f32[32,512]{1,0:T(8,128)S(1)}, u32[]{:S(2)}, u32[]{:S(2)}) collective-permute-start(f32[32,512]{1,0:T(8,128)S(1)} %add.58), channel_id=1, source_target_pairs={{0,64},{8,72},{16,80},{24,88},{32,96},{40,104},{48,112},{56,120},{... | collective-permute-start | bytes 196616 | tf_op jit(solution)/shard_map/ppermute | solution.py:205
  105.4 5.1 %collective-permute-start.16 = (f32[32,512]{1,0:T(8,128)S(1)}, f32[32,512]{1,0:T(8,128)S(1)}, u32[]{:S(2)}, u32[]{:S(2)}) collective-permute-start(f32[32,512]{1,0:T(8,128)S(1)} %add.59), channel_id=1, source_target_pairs={{0,192},{8,200},{16,208},{24,216},{32,224},{40,232},{48,240},{56,2... | collective-permute-start | bytes 196616 | tf_op jit(solution)/shard_map/ppermute | solution.py:205
  108.1 11.6 %collective-permute-start.28 = (f32[64,512]{1,0:T(8,128)S(1)}, f32[64,512]{1,0:T(8,128)S(1)}, u32[]{:S(2)}, u32[]{:S(2)}) collective-permute-start(f32[64,512]{1,0:T(8,128)S(1)} %add.70), channel_id=1, source_target_pairs={{0,4},{1,5},{2,6},{3,7},{4,0},{5,1},{6,2},{7,3},{8,12},{9,13},{10,... | collective-permute-start | bytes 393224 | tf_op jit(solution)/shard_map/ppermute | solution.py:205
  110.5 5.5 %collective-permute-start.17 = (f32[32,512]{1,0:T(8,128)S(1)}, f32[32,512]{1,0:T(8,128)S(1)}, u32[]{:S(2)}, u32[]{:S(2)}) collective-permute-start(f32[32,512]{1,0:T(8,128)S(1)} %add.60), channel_id=1, source_target_pairs={{0,1},{1,0},{2,3},{3,2},{4,5},{5,4},{6,7},{7,6},{8,9},{9,8},{10,11... | collective-permute-start | bytes 196616 | tf_op jit(solution)/shard_map/ppermute | solution.py:205
  116.1 5.6 %collective-permute-start.18 = (f32[32,512]{1,0:T(8,128)S(1)}, f32[32,512]{1,0:T(8,128)S(1)}, u32[]{:S(2)}, u32[]{:S(2)}) collective-permute-start(f32[32,512]{1,0:T(8,128)S(1)} %add.61), channel_id=1, source_target_pairs={{0,2},{1,3},{2,0},{3,1},{4,6},{5,7},{6,4},{7,5},{8,10},{9,11},{10,... | collective-permute-start | bytes 196616 | tf_op jit(solution)/shard_map/ppermute | solution.py:205
  119.6 13.3 %collective-permute-start.29 = (f32[64,512]{1,0:T(8,128)S(1)}, f32[64,512]{1,0:T(8,128)S(1)}, u32[]{:S(2)}, u32[]{:S(2)}) collective-permute-start(f32[64,512]{1,0:T(8,128)S(1)} %add.71), channel_id=1, source_target_pairs={{0,8},{8,0},{16,24},{24,16},{32,40},{40,32},{48,56},{56,48},{64,72... | collective-permute-start | bytes 393224 | tf_op jit(solution)/shard_map/ppermute | solution.py:205
  121.7 7.2 %collective-permute-start.19 = (f32[32,512]{1,0:T(8,128)S(1)}, f32[32,512]{1,0:T(8,128)S(1)}, u32[]{:S(2)}, u32[]{:S(2)}) collective-permute-start(f32[32,512]{1,0:T(8,128)S(1)} %add.62), channel_id=1, source_target_pairs={{0,4},{1,5},{2,6},{3,7},{4,0},{5,1},{6,2},{7,3},{8,12},{9,13},{10,... | collective-permute-start | bytes 196616 | tf_op jit(solution)/shard_map/ppermute | solution.py:205
  128.9 5.0 %collective-permute-start.20 = (f32[32,512]{1,0:T(8,128)S(1)}, f32[32,512]{1,0:T(8,128)S(1)}, u32[]{:S(2)}, u32[]{:S(2)}) collective-permute-start(f32[32,512]{1,0:T(8,128)S(1)} %add.63), channel_id=1, source_target_pairs={{0,8},{8,0},{16,24},{24,16},{32,40},{40,32},{48,56},{56,48},{64,72... | collective-permute-start | bytes 196616 | tf_op jit(solution)/shard_map/ppermute | solution.py:205
  (7 other events, 38.8 us)

commit v2 on v0

v2 whole, which is shorter than its diff:
```python
import functools

import jax
import jax.numpy as jnp
from jax import lax
from jax.experimental import pallas as pl
from jax.experimental.pallas import tpu as pltpu
from jax.sharding import PartitionSpec as P

L = 8
DT = 64
TB = 64
SLOTS = 768
PAIR_US = 0.4
Q = 256
F32 = jnp.float32
BF16 = jnp.bfloat16
VMEM_LIMIT = 8 * 2**20

NN = (((1,), (0,)), ((), ()))
NT = (((1,), (1,)), ((), ()))
TN = (((0,), (0,)), ((), ()))


def dot(a, b, dims):
    return lax.dot_general(a, b, dims, preferred_element_type=F32)


def sigmoid(value):
    return 0.5 * jnp.tanh(0.5 * value) + 0.5


def legendre(cosine):
    terms = [jnp.ones_like(cosine), cosine]
    for order in range(1, L - 1):
        terms.append(
            ((2 * order + 1) * cosine * terms[order] - order * terms[order - 1])
            * (1.0 / (order + 1))
        )
    return terms


def slot_kernel(
    ks_ref, counts_ref, in_ref, out_ref, cos_ref, in_to, out_to, valid_to, basis_to, core_to
):
    core_to[...] = jnp.full(core_to.shape, ks_ref[in_to.shape[0]], jnp.int32)
    lane = lax.broadcasted_iota(jnp.int32, (1, 2 * TB), 1)
    rows = []
    for p in range(in_to.shape[0]):
        k = ks_ref[p]
        in_to[p : p + 1, :] = in_ref[pl.ds(k, 1), :]
        out_to[p : p + 1, :] = out_ref[pl.ds(k, 1), :]
        rows.append(cos_ref[pl.ds(k, 1), :])
        for t in range(SLOTS // (2 * TB)):
            count = jnp.where(lane < TB, counts_ref[k, 2 * t], counts_ref[k, 2 * t + 1])
            valid_to[p : p + 1, t * 2 * TB : (t + 1) * 2 * TB] = (
                (lane & (TB - 1)) < count
            ).astype(F32)
    for l, term in enumerate(legendre(jnp.concatenate(rows, axis=0))):
        basis_to[l] = term


def one_hot(index):
    low = (index & (Q - 1)).astype(F32).astype(BF16)
    row = lax.broadcasted_iota(jnp.int32, (Q, 128), 0).astype(F32).astype(BF16)
    row = jnp.concatenate([row] * (SLOTS // 128), axis=1)
    return jnp.where(row == low, jnp.ones((), BF16), jnp.zeros((), BF16))


def stacked(table):
    parts = table.shape[1] // Q
    return jnp.concatenate([table[:, r * Q : (r + 1) * Q] for r in range(parts)], axis=0)


def pick(table, hot, high):
    parts = table.shape[1] // Q
    found = dot(stacked(table), hot, NN)
    total = found[:DT]
    for r in range(1, parts):
        total = jnp.where(high == r, found[r * DT : (r + 1) * DT], total)
    return total


def collect(values, hot, high, parts):
    low = values.astype(BF16)
    zero = jnp.zeros((), BF16)
    rows = [jnp.where(high == r, low, zero) for r in range(parts)]
    return dot(jnp.concatenate(rows, axis=0), hot, NT)


def expand(basis_ref, p, values):
    return jnp.concatenate(
        [(basis_ref[l, p : p + 1, :] * values).astype(BF16) for l in range(L)], axis=0
    )


def down_kernel(edge_ref, w_ref, down_ref, slope_ref):
    pre = dot(w_ref[...], edge_ref[...], NT)
    sig = sigmoid(pre)
    down_ref[...] = (pre * sig).astype(BF16)
    slope_ref[...] = sig * (1.0 + pre * (1.0 - sig))


def forward_kernel(places, base, rows, in_ref, out_ref, valid_ref, basis_ref, w_ref, *refs):
    n = len(places)
    sources = refs[:n]
    total_ref = refs[n] if base else None
    outs = refs[n + base :]
    trip_ref, feat_ref = outs[:2]
    w = w_ref[...]
    if rows:
        outs[2][...] = jnp.concatenate(
            [w[:, l * DT : (l + 1) * DT].astype(F32).T for l in range(L)], axis=1
        ).astype(BF16)
    parts = sources[0].shape[-1] // Q
    for i, p in enumerate(places):
        in_idx = in_ref[p : p + 1, :]
        out_idx = out_ref[p : p + 1, :]
        feat = pick(sources[i][...], one_hot(in_idx), in_idx // Q)
        feat_ref[i * DT : (i + 1) * DT, :] = feat.astype(BF16)
        message = dot(w, expand(basis_ref, p, feat), NN) * valid_ref[p : p + 1, :]
        part = collect(message, one_hot(out_idx), out_idx // Q, parts)
        if i == 0:
            trip_ref[...] = part + total_ref[...] if base else part
        else:
            trip_ref[...] += part


def middle_kernel(scale, cot_ref, trip_ref, w_ref, d_trip_ref, grad_ref, trip_b_ref):
    w = w_ref[...]
    for r in range(cot_ref.shape[0] // Q):
        trip = trip_ref[r * DT : (r + 1) * DT, :].astype(BF16)
        trip_b_ref[r * DT : (r + 1) * DT, :] = trip
        up_act = dot(trip, w, TN)
        sig = sigmoid(up_act)
        slope = sig * (1.0 + up_act * (1.0 - sig))
        d_act = (cot_ref[r * Q : (r + 1) * Q, :].astype(F32) * slope).astype(BF16)
        d_trip_ref[:, r * Q : (r + 1) * Q] = dot(w, d_act, NT).astype(BF16)
        part = dot(trip, d_act, NN) * scale
        grad_ref[...] = part if r == 0 else grad_ref[...] + part


def updated_kernel(after_ref, edge_ref, trip_ref, w_ref, updated_ref, token_ref):
    token_ref[...] = jnp.zeros_like(token_ref)
    rows = updated_ref.shape[0]
    base = pl.program_id(0) * rows
    for r in range(rows // Q):
        at = pl.multiple_of((base // Q + r) * DT, DT)
        up_act = dot(trip_ref[pl.ds(at, DT), :], w_ref[...], TN)
        edge = edge_ref[pl.ds(pl.multiple_of(base + r * Q, Q), Q), :].astype(F32)
        updated_ref[r * Q : (r + 1) * Q, :] = (edge + up_act * sigmoid(up_act)).astype(BF16)


def backward_kernel(
    places, base, scale, in_ref, out_ref, valid_ref, basis_ref, w_ref, d_trip_ref, *refs
):
    feat_refs = refs[: len(places)]
    grad_base = refs[len(places)] if base else None
    own_ref, pair_ref, grad_ref = refs[-3:]
    w_rows = w_ref[...]
    d_trip = d_trip_ref[...]
    parts = d_trip.shape[1] // Q
    total = grad_base[...] if base else None
    for i, p in enumerate(places):
        in_idx = in_ref[p : p + 1, :]
        out_idx = out_ref[p : p + 1, :]
        d_message = pick(d_trip, one_hot(out_idx), out_idx // Q) * valid_ref[p : p + 1, :]
        spread = expand(basis_ref, p, d_message)
        part = dot(feat_refs[i][...], spread, NT)
        total = part if total is None else total + part
        d_feat = dot(w_rows, spread, NN)
        d_source = collect(d_feat, one_hot(in_idx), in_idx // Q, parts).astype(BF16)
        for r in range(parts):
            at, piece = slice(r * Q, (r + 1) * Q), d_source[r * DT : (r + 1) * DT]
            if i == 0:
                own_ref[:, at] = piece
            else:
                pair_ref[i - 1, :, at] = piece
    if scale is None:
        grad_ref[...] = total
    else:
        total = total * scale
        for l in range(L):
            grad_ref[:, l * DT : (l + 1) * DT] = total[:, l * DT : (l + 1) * DT].T


def meet_kernel(own_ref, far_ref, near_ref, *out_refs):
    for i, out_ref in enumerate(out_refs):
        total = own_ref[i].astype(F32) + far_ref[i].astype(F32) + near_ref[i].astype(F32)
        out_ref[...] = total.astype(BF16)


def final_kernel(scale, after_ref, edge_ref, slope_ref, core_ref, bil_ref, up_ref, *refs):
    terms, (d_pre_ref, keep_ref, send_ref) = refs[:-3], refs[-3:]
    d_down = terms[0][...].astype(F32)
    for term in terms[1:]:
        d_down = d_down + term[...].astype(F32)
    d_pre = (d_down * slope_ref[...]).astype(BF16)
    d_pre_ref[...] = d_pre
    grad = dot(d_pre, edge_ref[...], NN) * scale
    even = core_ref[0:1, :] == 0
    half = DT // 2
    keep_ref[:half, :] = jnp.where(even, grad[:half], grad[half:])
    send_ref[:half, :] = jnp.where(even, grad[half:], grad[:half])
    bil, up = bil_ref[...], up_ref[...]
    keep_ref[half:, :] = jnp.where(even, bil, up)
    send_ref[half:, :] = jnp.where(even, up, bil)


def embed_kernel(after_ref, cot_ref, d_pre_ref, w_ref, grad_ref, token_ref):
    token_ref[...] = jnp.zeros_like(token_ref)
    rows = grad_ref.shape[0]
    base = pl.multiple_of(pl.program_id(0) * rows, rows)
    part = dot(d_pre_ref[:, pl.ds(base, rows)], w_ref[...], TN)
    grad_ref[...] = (cot_ref[pl.ds(base, rows), :].astype(F32) + part).astype(BF16)


def finish_kernel(core_ref, mine_ref, other_ref, down_ref, bil_ref, up_ref):
    even = core_ref[0:1, :] == 0
    half = DT // 2
    mine, other = mine_ref[...], other_ref[...]
    first, second = jnp.where(even, mine, other), jnp.where(even, other, mine)
    down_ref[:half, :] = first[:half]
    down_ref[half:, :] = second[:half]
    bil_ref[...] = first[half:]
    up_ref[...] = second[half:]


def cost(us):
    return pl.CostEstimate(
        flops=int(us * 1.0e9), bytes_accessed=int(us * 3.0e6), transcendentals=0
    )


VMEM = pl.BlockSpec(memory_space=pltpu.VMEM)


def call(kernel, outs, args, us, smem=(), after=None):
    scalar = pl.BlockSpec(memory_space=pltpu.SMEM)
    specs = [scalar if i in smem else VMEM for i in range(len(args))]
    return pl.pallas_call(
        kernel,
        out_shape=outs,
        in_specs=specs if after is None else [VMEM] + specs,
        out_specs=jax.tree.map(lambda _: VMEM, outs),
        compiler_params=pltpu.CompilerParams(vmem_limit_bytes=VMEM_LIMIT),
        cost_estimate=cost(us),
    )(*(() if after is None else (after,)), *args)


def tiled(kernel, steps, args, out, us, after, shape=(8, 128)):
    block = (out.shape[0] // steps, out.shape[1])
    return pl.pallas_call(
        kernel,
        grid=(steps,),
        out_shape=(out, jax.ShapeDtypeStruct(shape, F32)),
        in_specs=[VMEM] * (len(args) + 1),
        out_specs=(
            pl.BlockSpec(block, lambda r: (r, 0)),
            VMEM,
        ),
        compiler_params=pltpu.CompilerParams(vmem_limit_bytes=VMEM_LIMIT),
        cost_estimate=cost(us),
    )(after, *args)


def swap(x, axis, partner):
    return lax.ppermute(x, axis, [(i, partner(i)) for i in range(lax.axis_size(axis))])


def near(x, axis):
    return swap(x, axis, lambda i: i ^ 1)


def far(x, axis):
    n = lax.axis_size(axis)
    return swap(x, axis, lambda i: (i + 1) % n if i % 2 else (i - 1) % n)


SIDE = 4


def mirror(i, unit):
    return i + (SIDE - 1 - 2 * (i // unit % SIDE)) * unit


BOTH = ("gx", "gy")
SUM_STEPS = (
    (lambda i, j: (i ^ 2, j), lambda i, j: (i ^ 8, j), lambda i, j: (i ^ 10, j)),
    (
        lambda i, j: (mirror(i, 2), j),
        lambda i, j: (mirror(i, 8), j),
        lambda i, j: (mirror(mirror(i, 2), 8), j),
    ),
    (lambda i, j: (i, j ^ 1), lambda i, j: (i, j ^ 3), lambda i, j: (i, j ^ 2)),
    (lambda i, j: (i, 7 - j),),
)


def sum_step(x, *partners):
    nx, ny = (lax.axis_size(axis) for axis in BOTH)
    x = x.astype(BF16)
    got = []
    for partner in partners:
        pairs = []
        for i in range(nx):
            for j in range(ny):
                to = partner(i, j)
                pairs.append((i * ny + j, to[0] * ny + to[1]))
        got.append(lax.ppermute(x, BOTH, pairs).astype(F32))
    total = x.astype(F32) + got[0]
    return total + (got[1] + got[2]) if len(got) == 3 else total


def together(*values):
    return lax.optimization_barrier(values)


def shards(
    edge_embed, cotangent, w_down, w_bilinear, w_up, in_index, out_index, triplet_cos, block_counts
):
    edges, width = edge_embed.shape
    struct = jax.ShapeDtypeStruct
    table = struct((DT, edges), BF16)
    stack = struct((edges // Q * DT, Q), F32)
    wide = struct((DT, width), F32)
    scale = float(edges * lax.axis_size("gx") * lax.axis_size("gy")) ** (-0.5)
    steps = edges // Q
    row, whole = (lambda r: (r, 0)), (lambda r: (0, 0))
    column = lambda r: (0, r)
    w_down_t, w_bil_t = w_down.T, w_bilinear.T
    core = lax.rem(lax.axis_index("gx"), 2)

    near_a = 2 - 2 * core
    near_b = 2 - 2 * lax.rem(lax.axis_index("gy"), 2)
    far_a, far_b = 2 - near_a, 2 - near_b
    ks = [4, 3 + near_b, 3 + far_b, 3 * near_a + 1, 3 * far_a + 1]
    ks += [3 * a + b for a in (near_a, far_a) for b in (near_b, far_b)]
    ks = jnp.stack([jnp.asarray(k, jnp.int32) for k in ks + [core]])
    *slots, core = call(
        slot_kernel,
        (
            struct(in_index.shape, jnp.int32),
            struct(in_index.shape, jnp.int32),
            struct(in_index.shape, F32),
            struct((L,) + in_index.shape, F32),
            struct((8, width), jnp.int32),
        ),
        (ks, block_counts, in_index, out_index, triplet_cos),
        1,
        smem=(0, 1),
    )
    slots = tuple(slots)

    down, slope = call(
        down_kernel, (table, struct((DT, edges), F32)), (edge_embed, w_down_t), 1
    )
    source = {0: down, 1: near(down, "gy"), 2: far(down, "gy")}
    source[4], source[3] = far(down, "gx"), near(down, "gx")
    feats = {}
    trip = w_rows = None
    for places in ((0,), (3, 4), (1, 2), (5, 6), (7, 8)):
        if places == (1, 2):
            source[1], source[2], trip = together(source[1], source[2], trip)
            source[7], source[8] = far(source[1], "gx"), far(source[2], "gx")
            source[5], source[6] = near(source[1], "gx"), near(source[2], "gx")
        n = len(places)
        base = trip is not None
        args = slots + (w_bil_t,) + tuple(source[p] for p in places) + ((trip,) if base else ())
        outs = (stack, struct((n * DT, SLOTS), BF16))
        outs += () if base else (struct((DT, L * DT), BF16),)
        trip, feat, *rest = call(
            functools.partial(forward_kernel, places, base, not base),
            outs,
            args,
            n * PAIR_US,
        )
        w_rows = rest[0] if rest else w_rows
        for i, p in enumerate(places):
            feats[p] = feat[i * DT : (i + 1) * DT]

    d_trip, grad_up, trip = call(
        functools.partial(middle_kernel, scale),
        (table, wide, struct(stack.shape, BF16)),
        (cotangent, trip, w_up),
        2,
    )

    sent = []
    grad_bil = None
    for places in ((4, 7, 8), (3, 5, 6), (0, 1, 2)):
        n = len(places)
        base = grad_bil is not None
        args = slots + (w_rows, d_trip) + tuple(feats[p] for p in places)
        args += (grad_bil,) if base else ()
        last = scale if places[0] == 0 else None
        *out, grad_bil = call(
            functools.partial(backward_kernel, places, base, last),
            (table, struct((n - 1, DT, edges), BF16), wide),
            args,
            n * PAIR_US,
        )
        sent.append(out)
    far_pair, far_own = far(sent[0][1], "gx"), far(sent[0][0], "gx")
    near_own, near_pair = (near(x, "gx") for x in sent[1])
    own, pair = sent[2]
    to_near, to_far = call(meet_kernel, (table, table), (pair, far_pair, near_pair), 0.5)
    from_near, from_far = near(to_near, "gy"), far(to_far, "gy")
    result = struct((edges, width), BF16)
    updated, token = tiled(updated_kernel, 4, (edge_embed, trip, w_up), result, 2, after=to_near)
    share = struct((DT // 2 + DT, width), F32)
    d_pre, keep, send = call(
        functools.partial(final_kernel, scale),
        (table, share, share),
        (edge_embed, slope, core, grad_bil, grad_up)
        + (own, far_own, near_own, from_near, from_far),
        1,
        after=token,
    )
    sums = keep + near(send, "gx")
    sums = sum_step(sums, *SUM_STEPS[0])
    grad_embed, token = tiled(
        embed_kernel, 4, (cotangent, d_pre, w_down_t), result, 2, sums, sums.shape
    )
    sums = sum_step(sums, *SUM_STEPS[1]) + token
    for step in SUM_STEPS[2:]:
        sums = sum_step(sums, *step)
    grad_down, grad_bil, grad_up = call(
        finish_kernel,
        (wide, wide, wide),
        (core, sums, near(sums, "gx")),
        1,
    )
    return (updated, grad_embed, grad_down.T, grad_bil.T, grad_up)


def solution(mesh):
    both = P(("gx", "gy"), None)
    in_specs = (both, both, P(), P(), P(), both, both, both, both)
    out_specs = (both, both, P(), P(), P())
    return jax.shard_map(shards, mesh=mesh, in_specs=in_specs, out_specs=out_specs, check_vma=False)
```

time: 625 us -> 103 us (0.16)
  waiting for transfers between devices: 291 us -> 20.1 us
  matrix products: 146 us -> 0 us
  other arithmetic: 97.1 us -> 0.21 us
  local copies, waits for them, and re-layouts: 40.6 us -> 2.61 us
  Pallas kernels: 0 us -> 30.2 us
  starting transfers between devices: 30.7 us -> 49.2 us
  between operations: 14.2 us -> 0.97 us
    psum x1 -> x0, waiting for transfers between devices: 247 us -> none  [shards(): lax.psum((grad_down_local, grad_bil_local, grad_up_local), ('gx', 'gy'))]
    dot_general x78 -> x0, matrix products: 146 us -> none  [the longest x27 68.6 us: pick_rows(): return jnp.dot(selector, table, preferred_element_type=jnp.float32)]
    gather x19 -> x0, other arithmetic: 41.7 us -> none  [slot_mask(): jnp.repeat(counts, TB, total_repeat_length=SLOTS)]
    convert_element_type x20 -> x4, other arithmetic: 31.2 us -> 0.19 us  [sum_step(): x = x.astype(BF16)]
    pallas_call x0 -> x16, Pallas kernels: none -> 30.2 us  [the longest x14 24.6 us: call(): pl.pallas_call(kernel, out_shape=outs, in_specs=specs if after is None el...]
    ppermute x8 -> x26, waiting for transfers between devices: 43.9 us -> 20.1 us  [the longest x10 12.1 us: sum_step(): got.append(lax.ppermute(x, BOTH, pairs).astype(F32))]
    ppermute x8 -> x26, starting transfers between devices: 30.6 us -> 49.2 us  [the longest x16 35.9 us: swap(): lax.ppermute(x, axis, [(i, partner(i)) for i in range(lax.axis_size(axis))])]
    div x54 -> x0, other arithmetic: 14.4 us -> none  [legendre(): ((2 * order + 1) * cosine * terms[order] - order * terms[order - 1]) / (o...]
  transfers between devices with their start and end apart: 9 -> 26, of which waited for: 8 -> 10; matrix products, arithmetic and copies ran while one was open for 1% -> 0% of each run, Pallas kernels for 0% -> 19%
where the time goes in v2:
time: 103 us
  starting transfers between devices  49.2 us (48%)
  Pallas kernels  30.2 us (29%)
  waiting for transfers between devices  20.1 us (20%)
  local copies, waits for them, and re-layouts  2.61 us (3%)
    ppermute x16, starting transfers between devices, swap(): lax.ppermute(x, axis, [(i, partner(i)) for i in range(lax.axis_size(axis))])  35.9 us
    pallas_call x14, Pallas kernels, call(): pl.pallas_call(kernel, out_shape=outs, in_specs=specs if after is None el...  24.6 us
    ppermute x10, starting transfers between devices, sum_step(): got.append(lax.ppermute(x, BOTH, pairs).astype(F32))  13.4 us
    ppermute x10, waiting for transfers between devices, sum_step(): got.append(lax.ppermute(x, BOTH, pairs).astype(F32))  12.1 us
    ppermute x16, waiting for transfers between devices, swap(): lax.ppermute(x, axis, [(i, partner(i)) for i in range(lax.axis_size(axis))])  8.01 us
    pallas_call x2, Pallas kernels, tiled(): pl.pallas_call(kernel, grid=(steps,), out_shape=(out, jax.ShapeDtypeStruc...  5.59 us
    unnamed x22, local copies, waits for them, and re-layouts  2.47 us
  transfers between devices with their start and end apart: 26, of which 10 were waited for; matrix products, arithmetic and copies ran while one was open for 0% of the time, Pallas kernels for 19%

profile of v2, /device:TPU:1, one launch (start us, length us, event | category | flops | bytes accessed | tf_op | source)
XLA Modules:
  0.0 103.3 jit_solution(6104326877395976821)
XLA Ops:
  0.6 1.6 %copy-done = bf16[2048,512]{1,0:T(8,128)(2,1)S(1)} copy-done((bf16[2048,512]{1,0:T(8,128)(2,1)S(1)}, bf16[2048,512]{1,0:T(8,128)(2,1)}, u32[]{:S(2)}) %copy-start) | copy-done | bytes 2097176
  3.9 3.3 %collective-permute-start.2 = (bf16[64,2048]{1,0:T(8,128)(2,1)S(1)}, bf16[64,2048]{1,0:T(8,128)(2,1)S(1)}, u32[]{:S(2)}, u32[]{:S(2)}) collective-permute-start(bf16[64,2048]{1,0:T(8,128)(2,1)S(1)} %get-tuple-element.54.refs_0_), channel_id=1, source_target_pairs={{0,8},{8,0},{16,24},{24,16},{32,40},{40,32},{48,56},{56,48},{64,72... | collective-permute-start | bytes 786440 | tf_op jit(solution)/shard_map/ppermute | solution.py:268
  8.3 4.7 %collective-permute-start.1 = (bf16[64,2048]{1,0:T(8,128)(2,1)S(1)}, bf16[64,2048]{1,0:T(8,128)(2,1)S(1)}, u32[]{:S(2)}, u32[]{:S(2)}) collective-permute-start(bf16[64,2048]{1,0:T(8,128)(2,1)S(1)} %get-tuple-element.54.refs_0_), channel_id=1, source_target_pairs={{0,7},{1,2},{2,1},{3,4},{4,3},{5,6},{6,5},{7,0},{8,15},{9,10},{10,... | collective-permute-start | bytes 786440 | tf_op jit(solution)/shard_map/ppermute | solution.py:268
  13.9 1.2 %shard_map.130 = (f32[512,256]{1,0:T(8,128)S(1)}, bf16[64,768]{1,0:T(8,128)(2,1)S(1)}, bf16[64,512]{1,0:T(8,128)(2,1)S(1)}) custom-call(s32[9,768]{1,0:T(8,128)S(1)} %get-tuple-element.50.in_ref, s32[9,768]{1,0:T(8,128)S(1)} %get-tuple-element.51.out_ref, f32[9,768]{1,0:T(8,128)S(1)} %get-tuple-element.52.valid_ref, ...), custom_call_target="tpu_custom_call" | custom-call | flops 400000000 | bytes 1200000 | tf_op jit(solution)/shard_map/pallas_call | solution.py:241
  15.1 2.1 %shard_map.131 = (f32[512,256]{1,0:T(8,128)S(1)}, bf16[128,768]{1,0:T(8,128)(2,1)S(1)}) custom-call(s32[9,768]{1,0:T(8,128)S(1)} %get-tuple-element.50.in_ref, s32[9,768]{1,0:T(8,128)S(1)} %get-tuple-element.51.out_ref, f32[9,768]{1,0:T(8,128)S(1)} %get-tuple-element.52.valid_ref, f32[8,9,768]{2,1,0:T(8,128)S(1)} %get-tuple-element.53.basis_ref, ...), custom_call_target="tpu_custom_call" | custom-call | flops 800000000 | bytes 2400000 | tf_op jit(solution)/shard_map/pallas_call | solution.py:241
  17.2 4.8 %collective-permute-start.6 = (bf16[64,2048]{1,0:T(8,128)(2,1)S(1)}, bf16[64,2048]{1,0:T(8,128)(2,1)S(1)}, u32[]{:S(2)}, u32[]{:S(2)}) collective-permute-start(bf16[64,2048]{1,0:T(8,128)(2,1)S(1)} %collective-permute-done.refs_0_), channel_id=1, source_target_pairs={{0,8},{8,0},{16,24},{24,16},{32,40},{40,32},{48,56},{56,48},{64,72... | collective-permute-start | bytes 786440 | tf_op jit(solution)/shard_map/ppermute | solution.py:268
  22.1 1.7 %collective-permute-start.5 = (bf16[64,2048]{1,0:T(8,128)(2,1)S(1)}, bf16[64,2048]{1,0:T(8,128)(2,1)S(1)}, u32[]{:S(2)}, u32[]{:S(2)}) collective-permute-start(bf16[64,2048]{1,0:T(8,128)(2,1)S(1)} %collective-permute-done.1.refs_1_), channel_id=1, source_target_pairs={{0,248},{8,16},{16,8},{24,32},{32,24},{40,48},{48,40},{56,64},{64,... | collective-permute-start | bytes 786440 | tf_op jit(solution)/shard_map/ppermute | solution.py:268
  23.8 2.1 %shard_map.132 = (f32[512,256]{1,0:T(8,128)S(1)}, bf16[128,768]{1,0:T(8,128)(2,1)S(1)}) custom-call(s32[9,768]{1,0:T(8,128)S(1)} %get-tuple-element.50.in_ref, s32[9,768]{1,0:T(8,128)S(1)} %get-tuple-element.51.out_ref, f32[9,768]{1,0:T(8,128)S(1)} %get-tuple-element.52.valid_ref, f32[8,9,768]{2,1,0:T(8,128)S(1)} %get-tuple-element.53.basis_ref, ...), custom_call_target="tpu_custom_call" | custom-call | flops 800000000 | bytes 2400000 | tf_op jit(solution)/shard_map/pallas_call | solution.py:241
  25.9 2.1 %shard_map.133 = (f32[512,256]{1,0:T(8,128)S(1)}, bf16[128,768]{1,0:T(8,128)(2,1)S(1)}) custom-call(s32[9,768]{1,0:T(8,128)S(1)} %get-tuple-element.50.in_ref, s32[9,768]{1,0:T(8,128)S(1)} %get-tuple-element.51.out_ref, f32[9,768]{1,0:T(8,128)S(1)} %get-tuple-element.52.valid_ref, f32[8,9,768]{2,1,0:T(8,128)S(1)} %get-tuple-element.53.basis_ref, ...), custom_call_target="tpu_custom_call" | custom-call | flops 800000000 | bytes 2400000 | tf_op jit(solution)/shard_map/pallas_call | solution.py:241
  28.0 2.9 %collective-permute-done.5.refs_1_ = bf16[64,2048]{1,0:T(8,128)(2,1)S(1)} collective-permute-done((bf16[64,2048]{1,0:T(8,128)(2,1)S(1)}, bf16[64,2048]{1,0:T(8,128)(2,1)S(1)}, u32[]{:S(2)}, u32[]{:S(2)}) %collective-permute-start.5) | collective-permute-done | bytes 262176 | tf_op jit(solution)/shard_map/ppermute | solution.py:268
  31.0 2.1 %shard_map.134 = (f32[512,256]{1,0:T(8,128)S(1)}, bf16[128,768]{1,0:T(8,128)(2,1)S(1)}) custom-call(s32[9,768]{1,0:T(8,128)S(1)} %get-tuple-element.50.in_ref, s32[9,768]{1,0:T(8,128)S(1)} %get-tuple-element.51.out_ref, f32[9,768]{1,0:T(8,128)S(1)} %get-tuple-element.52.valid_ref, f32[8,9,768]{2,1,0:T(8,128)S(1)} %get-tuple-element.53.basis_ref, ...), custom_call_target="tpu_custom_call" | custom-call | flops 800000000 | bytes 2400000 | tf_op jit(solution)/shard_map/pallas_call | solution.py:241
  33.1 3.0 %shard_map.135 = (bf16[64,2048]{1,0:T(8,128)(2,1)S(1)}, f32[64,512]{1,0:T(8,128)S(1)}, bf16[512,256]{1,0:T(8,128)(2,1)S(1)}) custom-call(bf16[2048,512]{1,0:T(8,128)(2,1)S(1)} %copy-done.2, f32[512,256]{1,0:T(8,128)S(1)} %get-tuple-element.63.trip_ref, bf16[64,512]{1,0:T(8,128)(2,1)S(1)} %copy-done.4), custom_call_target="tpu_custom_call" | custom-call | flops 2000000000 | bytes 6000000 | tf_op jit(solution)/shard_map/pallas_call | solution.py:241
  36.1 3.0 %shard_map.136 = (bf16[64,2048]{1,0:T(8,128)(2,1)S(1)}, bf16[2,64,2048]{2,1,0:T(8,128)(2,1)S(1)}, f32[64,512]{1,0:T(8,128)S(1)}) custom-call(s32[9,768]{1,0:T(8,128)S(1)} %get-tuple-element.50.in_ref, s32[9,768]{1,0:T(8,128)S(1)} %get-tuple-element.51.out_ref, f32[9,768]{1,0:T(8,128)S(1)} %get-tuple-element.52.valid_ref, ...), custom_call_target="tpu_custom_call" | custom-call | flops 1200000000 | bytes 3600000 | tf_op jit(solution)/shard_map/pallas_call | solution.py:241
  39.4 3.1 %shard_map.137 = (bf16[64,2048]{1,0:T(8,128)(2,1)S(1)}, bf16[2,64,2048]{2,1,0:T(8,128)(2,1)S(1)}, f32[64,512]{1,0:T(8,128)S(1)}) custom-call(s32[9,768]{1,0:T(8,128)S(1)} %get-tuple-element.50.in_ref, s32[9,768]{1,0:T(8,128)S(1)} %get-tuple-element.51.out_ref, f32[9,768]{1,0:T(8,128)S(1)} %get-tuple-element.52.valid_ref, ...), custom_call_target="tpu_custom_call" | custom-call | flops 1200000000 | bytes 3600000 | tf_op jit(solution)/shard_map/pallas_call | solution.py:241
  42.5 5.8 %collective-permute-start.9 = (bf16[2,64,2048]{2,1,0:T(8,128)(2,1)S(1)}, bf16[2,64,2048]{2,1,0:T(8,128)(2,1)S(1)}, u32[]{:S(2)}, u32[]{:S(2)}) collective-permute-start(bf16[2,64,2048]{2,1,0:T(8,128)(2,1)S(1)} %get-tuple-element.74), channel_id=1, source_target_pairs={{0,8},{8,0},{16,24},{24,16},{32,40},{40,32},{48,56},{56,48},{64,72... | collective-permute-start | bytes 1572872 | tf_op jit(solution)/shard_map/ppermute | solution.py:268
  48.4 2.8 %collective-permute-start.11 = (bf16[64,2048]{1,0:T(8,128)(2,1)S(1)}, bf16[64,2048]{1,0:T(8,128)(2,1)S(1)}, u32[]{:S(2)}, u32[]{:S(2)}) collective-permute-start(bf16[64,2048]{1,0:T(8,128)(2,1)S(1)} %get-tuple-element.85), channel_id=1, source_target_pairs={{0,8},{8,0},{16,24},{24,16},{32,40},{40,32},{48,56},{56,48},{64,72... | collective-permute-start | bytes 786440 | tf_op jit(solution)/shard_map/ppermute | solution.py:268
  51.3 3.1 %shard_map.138 = (bf16[64,2048]{1,0:T(8,128)(2,1)S(1)}, bf16[2,64,2048]{2,1,0:T(8,128)(2,1)S(1)}, f32[64,512]{1,0:T(8,128)S(1)}) custom-call(s32[9,768]{1,0:T(8,128)S(1)} %get-tuple-element.50.in_ref, s32[9,768]{1,0:T(8,128)S(1)} %get-tuple-element.51.out_ref, f32[9,768]{1,0:T(8,128)S(1)} %get-tuple-element.52.valid_ref, ...), custom_call_target="tpu_custom_call" | custom-call | flops 1200000000 | bytes 3600000 | tf_op jit(solution)/shard_map/pallas_call | solution.py:241
  54.7 3.6 %collective-permute-start.13 = (bf16[64,2048]{1,0:T(8,128)(2,1)S(1)}, bf16[64,2048]{1,0:T(8,128)(2,1)S(1)}, u32[]{:S(2)}, u32[]{:S(2)}) collective-permute-start(bf16[64,2048]{1,0:T(8,128)(2,1)S(1)} %get-tuple-element.86), channel_id=1, source_target_pairs={{0,7},{1,2},{2,1},{3,4},{4,3},{5,6},{6,5},{7,0},{8,15},{9,10},{10,... | collective-permute-start | bytes 786440 | tf_op jit(solution)/shard_map/ppermute | solution.py:268
  58.2 3.0 %shard_map.140 = (bf16[2048,512]{1,0:T(8,128)(2,1)}, f32[8,128]{1,0:T(8,128)S(1)}) custom-call(bf16[64,2048]{1,0:T(8,128)(2,1)S(1)} %get-tuple-element.75.after_ref, bf16[2048,512]{1,0:T(8,128)(2,1)S(1)} %copy-done.1, bf16[512,256]{1,0:T(8,128)(2,1)S(1)} %get-tuple-element.76.trip_ref, bf16[64,512]{1,0:T(8,128)(2,1)S(1)} %copy-done.4), custom_call_target="tpu_custom_call" | custom-call | flops 2000000000 | bytes 6000000 | tf_op jit(solution)/shard_map/pallas_call | solution.py:253
  62.1 2.1 %collective-permute-done.13.refs_4_ = bf16[64,2048]{1,0:T(8,128)(2,1)S(1)} collective-permute-done((bf16[64,2048]{1,0:T(8,128)(2,1)S(1)}, bf16[64,2048]{1,0:T(8,128)(2,1)S(1)}, u32[]{:S(2)}, u32[]{:S(2)}) %collective-permute-start.13) | collective-permute-done | bytes 262176 | tf_op jit(solution)/shard_map/ppermute | solution.py:268
  64.7 1.4 %collective-permute-start.14 = (f32[96,512]{1,0:T(8,128)S(1)}, f32[96,512]{1,0:T(8,128)S(1)}, u32[]{:S(2)}, u32[]{:S(2)}) collective-permute-start(f32[96,512]{1,0:T(8,128)S(1)} %get-tuple-element.88), channel_id=1, source_target_pairs={{0,8},{8,0},{16,24},{24,16},{32,40},{40,32},{48,56},{56,48},{64,72... | collective-permute-start | bytes 589832 | tf_op jit(solution)/shard_map/ppermute | solution.py:268
  68.0 1.9 %collective-permute-start.15 = (bf16[96,512]{1,0:T(8,128)(2,1)S(1)}, bf16[96,512]{1,0:T(8,128)(2,1)S(1)}, u32[]{:S(2)}, u32[]{:S(2)}) collective-permute-start(bf16[96,512]{1,0:T(8,128)(2,1)S(1)} %add_convert_fusion.2), channel_id=1, source_target_pairs={{0,16},{1,17},{2,18},{3,19},{4,20},{5,21},{6,22},{7,23},{8,24},{9,... | collective-permute-start | bytes 294920 | tf_op jit(solution)/shard_map/ppermute | solution.py:310
  69.9 2.3 %collective-permute-done.17 = bf16[96,512]{1,0:T(8,128)(2,1)S(1)} collective-permute-done((bf16[96,512]{1,0:T(8,128)(2,1)S(1)}, bf16[96,512]{1,0:T(8,128)(2,1)S(1)}, u32[]{:S(2)}, u32[]{:S(2)}) %collective-permute-start.17) | collective-permute-done | bytes 98336 | tf_op jit(solution)/shard_map/ppermute | solution.py:310
  73.2 3.0 %collective-permute-start.20 = (bf16[96,512]{1,0:T(8,128)(2,1)S(1)}, bf16[96,512]{1,0:T(8,128)(2,1)S(1)}, u32[]{:S(2)}, u32[]{:S(2)}) collective-permute-start(bf16[96,512]{1,0:T(8,128)(2,1)S(1)} %get-tuple-element.95), channel_id=1, source_target_pairs={{0,240},{1,241},{2,242},{3,243},{4,244},{5,245},{6,246},{7,247},{8... | collective-permute-start | bytes 294920 | tf_op jit(solution)/shard_map/ppermute | solution.py:310
  76.2 2.2 %collective-permute-start.18 = (bf16[96,512]{1,0:T(8,128)(2,1)S(1)}, bf16[96,512]{1,0:T(8,128)(2,1)S(1)}, u32[]{:S(2)}, u32[]{:S(2)}) collective-permute-start(bf16[96,512]{1,0:T(8,128)(2,1)S(1)} %get-tuple-element.95), channel_id=1, source_target_pairs={{0,48},{1,49},{2,50},{3,51},{4,52},{5,53},{6,54},{7,55},{8,56},{9,... | collective-permute-start | bytes 294920 | tf_op jit(solution)/shard_map/ppermute | solution.py:310
  78.4 2.6 %shard_map.142 = (bf16[2048,512]{1,0:T(8,128)(2,1)}, f32[96,512]{1,0:T(8,128)S(1)}) custom-call(f32[96,512]{1,0:T(8,128)S(1)} %get-tuple-element.96.after_ref, bf16[2048,512]{1,0:T(8,128)(2,1)S(1)} %copy-done.2, bf16[64,2048]{1,0:T(8,128)(2,1)S(1)} %get-tuple-element.89.d_pre_ref, bf16[64,512]{1,0:T(8,128)(2,1)S(1)} %bitcast.19), custom_call_target="tpu_custom_call" | custom-call | flops 2000000000 | bytes 6000000 | tf_op jit(solution)/shard_map/pallas_call | solution.py:253
  80.9 1.6 %collective-permute-done.19 = bf16[96,512]{1,0:T(8,128)(2,1)S(1)} collective-permute-done((bf16[96,512]{1,0:T(8,128)(2,1)S(1)}, bf16[96,512]{1,0:T(8,128)(2,1)S(1)}, u32[]{:S(2)}, u32[]{:S(2)}) %collective-permute-start.19) | collective-permute-done | bytes 98336 | tf_op jit(solution)/shard_map/ppermute | solution.py:310
  82.6 1.7 %collective-permute-start.22 = (bf16[96,512]{1,0:T(8,128)(2,1)S(1)}, bf16[96,512]{1,0:T(8,128)(2,1)S(1)}, u32[]{:S(2)}, u32[]{:S(2)}) collective-permute-start(bf16[96,512]{1,0:T(8,128)(2,1)S(1)} %add_convert_fusion.1), channel_id=1, source_target_pairs={{0,3},{1,2},{2,1},{3,0},{4,7},{5,6},{6,5},{7,4},{8,11},{9,10},{10,... | collective-permute-start | bytes 294920 | tf_op jit(solution)/shard_map/ppermute | solution.py:310
  85.3 5.3 %collective-permute-done.23 = bf16[96,512]{1,0:T(8,128)(2,1)S(1)} collective-permute-done((bf16[96,512]{1,0:T(8,128)(2,1)S(1)}, bf16[96,512]{1,0:T(8,128)(2,1)S(1)}, u32[]{:S(2)}, u32[]{:S(2)}) %collective-permute-start.23) | collective-permute-done | bytes 98336 | tf_op jit(solution)/shard_map/ppermute | solution.py:310
  90.6 2.8 %collective-permute-start.24 = (bf16[96,512]{1,0:T(8,128)(2,1)S(1)}, bf16[96,512]{1,0:T(8,128)(2,1)S(1)}, u32[]{:S(2)}, u32[]{:S(2)}) collective-permute-start(bf16[96,512]{1,0:T(8,128)(2,1)S(1)} %add_convert_fusion), channel_id=1, source_target_pairs={{0,7},{1,6},{2,5},{3,4},{4,3},{5,2},{6,1},{7,0},{8,15},{9,14},{10,... | collective-permute-start | bytes 294920 | tf_op jit(solution)/shard_map/ppermute | solution.py:310
  93.3 2.0 %collective-permute-done.24 = bf16[96,512]{1,0:T(8,128)(2,1)S(1)} collective-permute-done((bf16[96,512]{1,0:T(8,128)(2,1)S(1)}, bf16[96,512]{1,0:T(8,128)(2,1)S(1)}, u32[]{:S(2)}, u32[]{:S(2)}) %collective-permute-start.24) | collective-permute-done | bytes 98336 | tf_op jit(solution)/shard_map/ppermute | solution.py:310
  95.4 6.1 %collective-permute-start.25 = (f32[96,512]{1,0:T(8,128)S(1)}, f32[96,512]{1,0:T(8,128)S(1)}, u32[]{:S(2)}, u32[]{:S(2)}) collective-permute-start(f32[96,512]{1,0:T(8,128)S(1)} %convert_add_fusion.mine_ref), channel_id=1, source_target_pairs={{0,8},{8,0},{16,24},{24,16},{32,40},{40,32},{48,56},{56,48},{64,72... | collective-permute-start | bytes 589832 | tf_op jit(solution)/shard_map/ppermute | solution.py:268
  (67 shorter events, 11.7 us)
Async XLA Ops:
  3.1 10.0 %copy-start.7 = (s32[9,768]{1,0:T(8,128)S(1)}, s32[9,768]{1,0:T(8,128)}, u32[]{:S(2)}) copy-start(s32[9,768]{1,0:T(8,128)} %in_ref.1) | copy-start | bytes 82948
  3.1 10.0 %copy-start.8 = (s32[9,768]{1,0:T(8,128)S(1)}, s32[9,768]{1,0:T(8,128)}, u32[]{:S(2)}) copy-start(s32[9,768]{1,0:T(8,128)} %out_ref.1) | copy-start | bytes 82948
  3.1 10.0 %copy-start.9 = (f32[9,768]{1,0:T(8,128)S(1)}, f32[9,768]{1,0:T(8,128)}, u32[]{:S(2)}) copy-start(f32[9,768]{1,0:T(8,128)} %cos_ref.1) | copy-start | bytes 82948
  3.1 10.0 %copy-start.10 = (s32[9,12]{1,0:T(8,128)S(1)}, s32[9,12]{1,0:T(8,128)}, u32[]{:S(2)}) copy-start(s32[9,12]{1,0:T(8,128)} %counts_ref.1) | copy-start | bytes 1300
  3.9 10.1 %copy-start.3 = (bf16[512,64]{0,1:T(8,128)(2,1)S(1)}, bf16[512,64]{0,1:T(8,128)(2,1)}, u32[]{:S(2)}) copy-start(bf16[512,64]{0,1:T(8,128)(2,1)} %param.12) | copy-start | bytes 196612
  3.9 11.2 %collective-permute-start.2 = (bf16[64,2048]{1,0:T(8,128)(2,1)S(1)}, bf16[64,2048]{1,0:T(8,128)(2,1)S(1)}, u32[]{:S(2)}, u32[]{:S(2)}) collective-permute-start(bf16[64,2048]{1,0:T(8,128)(2,1)S(1)} %get-tuple-element.54.refs_0_), channel_id=1, source_target_pairs={{0,8},{8,0},{16,24},{24,16},{32,40},{40,32},{48,56},{56,48},{64,72... | collective-permute-start | bytes 786440 | tf_op jit(solution)/shard_map/ppermute | solution.py:268
  7.2 7.9 %collective-permute-start.3 = (bf16[64,2048]{1,0:T(8,128)(2,1)S(1)}, bf16[64,2048]{1,0:T(8,128)(2,1)S(1)}, u32[]{:S(2)}, u32[]{:S(2)}) collective-permute-start(bf16[64,2048]{1,0:T(8,128)(2,1)S(1)} %get-tuple-element.54.refs_0_), channel_id=1, source_target_pairs={{0,248},{8,16},{16,8},{24,32},{32,24},{40,48},{48,40},{56,64},{64,... | collective-permute-start | bytes 786440 | tf_op jit(solution)/shard_map/ppermute | solution.py:268
  7.2 10.0 %collective-permute-start = (bf16[64,2048]{1,0:T(8,128)(2,1)S(1)}, bf16[64,2048]{1,0:T(8,128)(2,1)S(1)}, u32[]{:S(2)}, u32[]{:S(2)}) collective-permute-start(bf16[64,2048]{1,0:T(8,128)(2,1)S(1)} %get-tuple-element.54.refs_0_), channel_id=1, source_target_pairs={{0,1},{1,0},{2,3},{3,2},{4,5},{5,4},{6,7},{7,6},{8,9},{9,8},{10,11... | collective-permute-start | bytes 786440 | tf_op jit(solution)/shard_map/ppermute | solution.py:268
  8.3 8.9 %collective-permute-start.1 = (bf16[64,2048]{1,0:T(8,128)(2,1)S(1)}, bf16[64,2048]{1,0:T(8,128)(2,1)S(1)}, u32[]{:S(2)}, u32[]{:S(2)}) collective-permute-start(bf16[64,2048]{1,0:T(8,128)(2,1)S(1)} %get-tuple-element.54.refs_0_), channel_id=1, source_target_pairs={{0,7},{1,2},{2,1},{3,4},{4,3},{5,6},{6,5},{7,0},{8,15},{9,10},{10,... | collective-permute-start | bytes 786440 | tf_op jit(solution)/shard_map/ppermute | solution.py:268
  17.2 8.7 %collective-permute-start.6 = (bf16[64,2048]{1,0:T(8,128)(2,1)S(1)}, bf16[64,2048]{1,0:T(8,128)(2,1)S(1)}, u32[]{:S(2)}, u32[]{:S(2)}) collective-permute-start(bf16[64,2048]{1,0:T(8,128)(2,1)S(1)} %collective-permute-done.refs_0_), channel_id=1, source_target_pairs={{0,8},{8,0},{16,24},{24,16},{32,40},{40,32},{48,56},{56,48},{64,72... | collective-permute-start | bytes 786440 | tf_op jit(solution)/shard_map/ppermute | solution.py:268
  22.0 3.9 %collective-permute-start.7 = (bf16[64,2048]{1,0:T(8,128)(2,1)S(1)}, bf16[64,2048]{1,0:T(8,128)(2,1)S(1)}, u32[]{:S(2)}, u32[]{:S(2)}) collective-permute-start(bf16[64,2048]{1,0:T(8,128)(2,1)S(1)} %collective-permute-done.1.refs_1_), channel_id=1, source_target_pairs={{0,8},{8,0},{16,24},{24,16},{32,40},{40,32},{48,56},{56,48},{64,72... | collective-permute-start | bytes 786440 | tf_op jit(solution)/shard_map/ppermute | solution.py:268
  22.1 5.9 %collective-permute-start.4 = (bf16[64,2048]{1,0:T(8,128)(2,1)S(1)}, bf16[64,2048]{1,0:T(8,128)(2,1)S(1)}, u32[]{:S(2)}, u32[]{:S(2)}) collective-permute-start(bf16[64,2048]{1,0:T(8,128)(2,1)S(1)} %collective-permute-done.refs_0_), channel_id=1, source_target_pairs={{0,248},{8,16},{16,8},{24,32},{32,24},{40,48},{48,40},{56,64},{64,... | collective-permute-start | bytes 786440 | tf_op jit(solution)/shard_map/ppermute | solution.py:268
  22.1 8.9 %collective-permute-start.5 = (bf16[64,2048]{1,0:T(8,128)(2,1)S(1)}, bf16[64,2048]{1,0:T(8,128)(2,1)S(1)}, u32[]{:S(2)}, u32[]{:S(2)}) collective-permute-start(bf16[64,2048]{1,0:T(8,128)(2,1)S(1)} %collective-permute-done.1.refs_1_), channel_id=1, source_target_pairs={{0,248},{8,16},{16,8},{24,32},{32,24},{40,48},{48,40},{56,64},{64,... | collective-permute-start | bytes 786440 | tf_op jit(solution)/shard_map/ppermute | solution.py:268
  39.1 15.2 %collective-permute-start.8 = (bf16[2,64,2048]{2,1,0:T(8,128)(2,1)S(1)}, bf16[2,64,2048]{2,1,0:T(8,128)(2,1)S(1)}, u32[]{:S(2)}, u32[]{:S(2)}) collective-permute-start(bf16[2,64,2048]{2,1,0:T(8,128)(2,1)S(1)} %get-tuple-element.73), channel_id=1, source_target_pairs={{0,248},{8,16},{16,8},{24,32},{32,24},{40,48},{48,40},{56,64},{64,... | collective-permute-start | bytes 1572872 | tf_op jit(solution)/shard_map/ppermute | solution.py:268
  42.5 11.8 %collective-permute-start.9 = (bf16[2,64,2048]{2,1,0:T(8,128)(2,1)S(1)}, bf16[2,64,2048]{2,1,0:T(8,128)(2,1)S(1)}, u32[]{:S(2)}, u32[]{:S(2)}) collective-permute-start(bf16[2,64,2048]{2,1,0:T(8,128)(2,1)S(1)} %get-tuple-element.74), channel_id=1, source_target_pairs={{0,8},{8,0},{16,24},{24,16},{32,40},{40,32},{48,56},{56,48},{64,72... | collective-permute-start | bytes 1572872 | tf_op jit(solution)/shard_map/ppermute | solution.py:268
  48.3 12.9 %collective-permute-start.10 = (bf16[64,2048]{1,0:T(8,128)(2,1)S(1)}, bf16[64,2048]{1,0:T(8,128)(2,1)S(1)}, u32[]{:S(2)}, u32[]{:S(2)}) collective-permute-start(bf16[64,2048]{1,0:T(8,128)(2,1)S(1)} %get-tuple-element.84), channel_id=1, source_target_pairs={{0,248},{8,16},{16,8},{24,32},{32,24},{40,48},{48,40},{56,64},{64,... | collective-permute-start | bytes 786440 | tf_op jit(solution)/shard_map/ppermute | solution.py:268
  48.4 12.8 %collective-permute-start.11 = (bf16[64,2048]{1,0:T(8,128)(2,1)S(1)}, bf16[64,2048]{1,0:T(8,128)(2,1)S(1)}, u32[]{:S(2)}, u32[]{:S(2)}) collective-permute-start(bf16[64,2048]{1,0:T(8,128)(2,1)S(1)} %get-tuple-element.85), channel_id=1, source_target_pairs={{0,8},{8,0},{16,24},{24,16},{32,40},{40,32},{48,56},{56,48},{64,72... | collective-permute-start | bytes 786440 | tf_op jit(solution)/shard_map/ppermute | solution.py:268
  54.6 7.5 %collective-permute-start.12 = (bf16[64,2048]{1,0:T(8,128)(2,1)S(1)}, bf16[64,2048]{1,0:T(8,128)(2,1)S(1)}, u32[]{:S(2)}, u32[]{:S(2)}) collective-permute-start(bf16[64,2048]{1,0:T(8,128)(2,1)S(1)} %get-tuple-element.75.after_ref), channel_id=1, source_target_pairs={{0,1},{1,0},{2,3},{3,2},{4,5},{5,4},{6,7},{7,6},{8,9},{9,8},{10,11... | collective-permute-start | bytes 786440 | tf_op jit(solution)/shard_map/ppermute | solution.py:268
  54.7 9.5 %collective-permute-start.13 = (bf16[64,2048]{1,0:T(8,128)(2,1)S(1)}, bf16[64,2048]{1,0:T(8,128)(2,1)S(1)}, u32[]{:S(2)}, u32[]{:S(2)}) collective-permute-start(bf16[64,2048]{1,0:T(8,128)(2,1)S(1)} %get-tuple-element.86), channel_id=1, source_target_pairs={{0,7},{1,2},{2,1},{3,4},{4,3},{5,6},{6,5},{7,0},{8,15},{9,10},{10,... | collective-permute-start | bytes 786440 | tf_op jit(solution)/shard_map/ppermute | solution.py:268
  64.2 14.2 %copy-start.6 = (bf16[512,64]{0,1:T(8,128)(2,1)S(1)}, bf16[512,64]{0,1:T(8,128)(2,1)}, u32[]{:S(2)}) copy-start(bf16[512,64]{0,1:T(8,128)(2,1)} %param.11) | copy-start | bytes 196612
  64.7 2.5 %collective-permute-start.14 = (f32[96,512]{1,0:T(8,128)S(1)}, f32[96,512]{1,0:T(8,128)S(1)}, u32[]{:S(2)}, u32[]{:S(2)}) collective-permute-start(f32[96,512]{1,0:T(8,128)S(1)} %get-tuple-element.88), channel_id=1, source_target_pairs={{0,8},{8,0},{16,24},{24,16},{32,40},{40,32},{48,56},{56,48},{64,72... | collective-permute-start | bytes 589832 | tf_op jit(solution)/shard_map/ppermute | solution.py:268
  67.2 5.0 %collective-permute-start.17 = (bf16[96,512]{1,0:T(8,128)(2,1)S(1)}, bf16[96,512]{1,0:T(8,128)(2,1)S(1)}, u32[]{:S(2)}, u32[]{:S(2)}) collective-permute-start(bf16[96,512]{1,0:T(8,128)(2,1)S(1)} %add_convert_fusion.2), channel_id=1, source_target_pairs={{0,80},{1,81},{2,82},{3,83},{4,84},{5,85},{6,86},{7,87},{8,88},{9,... | collective-permute-start | bytes 294920 | tf_op jit(solution)/shard_map/ppermute | solution.py:310
  67.3 5.9 %collective-permute-start.16 = (bf16[96,512]{1,0:T(8,128)(2,1)S(1)}, bf16[96,512]{1,0:T(8,128)(2,1)S(1)}, u32[]{:S(2)}, u32[]{:S(2)}) collective-permute-start(bf16[96,512]{1,0:T(8,128)(2,1)S(1)} %add_convert_fusion.2), channel_id=1, source_target_pairs={{0,64},{1,65},{2,66},{3,67},{4,68},{5,69},{6,70},{7,71},{8,72},{9,... | collective-permute-start | bytes 294920 | tf_op jit(solution)/shard_map/ppermute | solution.py:310
  68.0 5.1 %collective-permute-start.15 = (bf16[96,512]{1,0:T(8,128)(2,1)S(1)}, bf16[96,512]{1,0:T(8,128)(2,1)S(1)}, u32[]{:S(2)}, u32[]{:S(2)}) collective-permute-start(bf16[96,512]{1,0:T(8,128)(2,1)S(1)} %add_convert_fusion.2), channel_id=1, source_target_pairs={{0,16},{1,17},{2,18},{3,19},{4,20},{5,21},{6,22},{7,23},{8,24},{9,... | collective-permute-start | bytes 294920 | tf_op jit(solution)/shard_map/ppermute | solution.py:310
  73.2 7.7 %collective-permute-start.20 = (bf16[96,512]{1,0:T(8,128)(2,1)S(1)}, bf16[96,512]{1,0:T(8,128)(2,1)S(1)}, u32[]{:S(2)}, u32[]{:S(2)}) collective-permute-start(bf16[96,512]{1,0:T(8,128)(2,1)S(1)} %get-tuple-element.95), channel_id=1, source_target_pairs={{0,240},{1,241},{2,242},{3,243},{4,244},{5,245},{6,246},{7,247},{8... | collective-permute-start | bytes 294920 | tf_op jit(solution)/shard_map/ppermute | solution.py:310
  76.2 6.3 %collective-permute-start.19 = (bf16[96,512]{1,0:T(8,128)(2,1)S(1)}, bf16[96,512]{1,0:T(8,128)(2,1)S(1)}, u32[]{:S(2)}, u32[]{:S(2)}) collective-permute-start(bf16[96,512]{1,0:T(8,128)(2,1)S(1)} %get-tuple-element.95), channel_id=1, source_target_pairs={{0,192},{1,193},{2,194},{3,195},{4,196},{5,197},{6,198},{7,199},{8... | collective-permute-start | bytes 294920 | tf_op jit(solution)/shard_map/ppermute | solution.py:310
  76.2 6.3 %collective-permute-start.18 = (bf16[96,512]{1,0:T(8,128)(2,1)S(1)}, bf16[96,512]{1,0:T(8,128)(2,1)S(1)}, u32[]{:S(2)}, u32[]{:S(2)}) collective-permute-start(bf16[96,512]{1,0:T(8,128)(2,1)S(1)} %get-tuple-element.95), channel_id=1, source_target_pairs={{0,48},{1,49},{2,50},{3,51},{4,52},{5,53},{6,54},{7,55},{8,56},{9,... | collective-permute-start | bytes 294920 | tf_op jit(solution)/shard_map/ppermute | solution.py:310
  82.5 8.0 %collective-permute-start.23 = (bf16[96,512]{1,0:T(8,128)(2,1)S(1)}, bf16[96,512]{1,0:T(8,128)(2,1)S(1)}, u32[]{:S(2)}, u32[]{:S(2)}) collective-permute-start(bf16[96,512]{1,0:T(8,128)(2,1)S(1)} %add_convert_fusion.1), channel_id=1, source_target_pairs={{0,2},{1,3},{2,0},{3,1},{4,6},{5,7},{6,4},{7,5},{8,10},{9,11},{10,... | collective-permute-start | bytes 294920 | tf_op jit(solution)/shard_map/ppermute | solution.py:310
  82.6 7.9 %collective-permute-start.22 = (bf16[96,512]{1,0:T(8,128)(2,1)S(1)}, bf16[96,512]{1,0:T(8,128)(2,1)S(1)}, u32[]{:S(2)}, u32[]{:S(2)}) collective-permute-start(bf16[96,512]{1,0:T(8,128)(2,1)S(1)} %add_convert_fusion.1), channel_id=1, source_target_pairs={{0,3},{1,2},{2,1},{3,0},{4,7},{5,6},{6,5},{7,4},{8,11},{9,10},{10,... | collective-permute-start | bytes 294920 | tf_op jit(solution)/shard_map/ppermute | solution.py:310
  84.4 6.2 %collective-permute-start.21 = (bf16[96,512]{1,0:T(8,128)(2,1)S(1)}, bf16[96,512]{1,0:T(8,128)(2,1)S(1)}, u32[]{:S(2)}, u32[]{:S(2)}) collective-permute-start(bf16[96,512]{1,0:T(8,128)(2,1)S(1)} %add_convert_fusion.1), channel_id=1, source_target_pairs={{0,1},{1,0},{2,3},{3,2},{4,5},{5,4},{6,7},{7,6},{8,9},{9,8},{10,11... | collective-permute-start | bytes 294920 | tf_op jit(solution)/shard_map/ppermute | solution.py:310
  90.6 4.8 %collective-permute-start.24 = (bf16[96,512]{1,0:T(8,128)(2,1)S(1)}, bf16[96,512]{1,0:T(8,128)(2,1)S(1)}, u32[]{:S(2)}, u32[]{:S(2)}) collective-permute-start(bf16[96,512]{1,0:T(8,128)(2,1)S(1)} %add_convert_fusion), channel_id=1, source_target_pairs={{0,7},{1,6},{2,5},{3,4},{4,3},{5,2},{6,1},{7,0},{8,15},{9,14},{10,... | collective-permute-start | bytes 294920 | tf_op jit(solution)/shard_map/ppermute | solution.py:310
  95.4 7.1 %collective-permute-start.25 = (f32[96,512]{1,0:T(8,128)S(1)}, f32[96,512]{1,0:T(8,128)S(1)}, u32[]{:S(2)}, u32[]{:S(2)}) collective-permute-start(f32[96,512]{1,0:T(8,128)S(1)} %convert_add_fusion.mine_ref), channel_id=1, source_target_pairs={{0,8},{8,0},{16,24},{24,16},{32,40},{40,32},{48,56},{56,48},{64,72... | collective-permute-start | bytes 589832 | tf_op jit(solution)/shard_map/ppermute | solution.py:268
  (5 other events, 19.6 us)

commit v3 on v2

--- a/solution.py
+++ b/solution.py
@@ -11,7 +11,8 @@
 DT = 64
 TB = 64
 SLOTS = 768
-PAIR_US = 0.4
+FORWARD_US = 0.04
+BACKWARD_US = 4
 Q = 256
 F32 = jnp.float32
 BF16 = jnp.bfloat16
@@ -40,9 +41,9 @@
     return terms
 
 
-def slot_kernel(
-    ks_ref, counts_ref, in_ref, out_ref, cos_ref, in_to, out_to, valid_to, basis_to, core_to
-):
+def slot_kernel(ks_ref, counts_ref, in_ref, out_ref, cos_ref, down_ref, *refs):
+    in_to, out_to, valid_to, basis_to, core_to, down_to = refs
+    down_to[...] = down_ref[...]
     core_to[...] = jnp.full(core_to.shape, ks_ref[in_to.shape[0]], jnp.int32)
     lane = lax.broadcasted_iota(jnp.int32, (1, 2 * TB), 1)
     rows = []
@@ -102,10 +103,8 @@
 
 
 def forward_kernel(places, base, rows, in_ref, out_ref, valid_ref, basis_ref, w_ref, *refs):
-    n = len(places)
-    sources = refs[:n]
-    total_ref = refs[n] if base else None
-    outs = refs[n + base :]
+    sources, refs = refs[: len(places)], refs[len(places) :]
+    total_ref, outs = refs[0] if base else None, refs[base:]
     trip_ref, feat_ref = outs[:2]
     w = w_ref[...]
     if rows:
@@ -156,7 +155,7 @@
 ):
     feat_refs = refs[: len(places)]
     grad_base = refs[len(places)] if base else None
-    own_ref, pair_ref, grad_ref = refs[-3:]
+    outs, grad_ref = refs[len(places) + base : -1], refs[-1]
     w_rows = w_ref[...]
     d_trip = d_trip_ref[...]
     parts = d_trip.shape[1] // Q
@@ -172,10 +171,12 @@
         d_source = collect(d_feat, one_hot(in_idx), in_idx // Q, parts).astype(BF16)
         for r in range(parts):
             at, piece = slice(r * Q, (r + 1) * Q), d_source[r * DT : (r + 1) * DT]
-            if i == 0:
-                own_ref[:, at] = piece
+            if len(outs) == 1:
+                outs[0][i, :, at] = piece
+            elif i == 0:
+                outs[0][:, at] = piece
             else:
-                pair_ref[i - 1, :, at] = piece
+                outs[1][i - 1, :, at] = piece
     if scale is None:
         grad_ref[...] = total
     else:
@@ -184,10 +185,13 @@
             grad_ref[:, l * DT : (l + 1) * DT] = total[:, l * DT : (l + 1) * DT].T
 
 
-def meet_kernel(own_ref, far_ref, near_ref, *out_refs):
-    for i, out_ref in enumerate(out_refs):
-        total = own_ref[i].astype(F32) + far_ref[i].astype(F32) + near_ref[i].astype(F32)
-        out_ref[...] = total.astype(BF16)
+def meet_kernel(own_ref, pair_ref, far_pair_ref, near_ref, far_own_ref, *refs):
+    *pair_to, own_to, far_own_to = refs
+    for i, out_ref in enumerate(pair_to):
+        total = pair_ref[i].astype(F32) + near_ref[i + 1].astype(F32)
+        out_ref[...] = (total + far_pair_ref[i].astype(F32)).astype(BF16)
+    own_to[...] = (own_ref[...].astype(F32) + near_ref[0].astype(F32)).astype(BF16)
+    far_own_to[...] = far_own_ref[...]
 
 
 def final_kernel(scale, after_ref, edge_ref, slope_ref, core_ref, bil_ref, up_ref, *refs):
@@ -312,10 +316,6 @@
     return total + (got[1] + got[2]) if len(got) == 3 else total
 
 
-def together(*values):
-    return lax.optimization_barrier(values)
-
-
 def shards(
     edge_embed, cotangent, w_down, w_bilinear, w_up, in_index, out_index, triplet_cos, block_counts
 ):
@@ -337,7 +337,13 @@
     ks = [4, 3 + near_b, 3 + far_b, 3 * near_a + 1, 3 * far_a + 1]
     ks += [3 * a + b for a in (near_a, far_a) for b in (near_b, far_b)]
     ks = jnp.stack([jnp.asarray(k, jnp.int32) for k in ks + [core]])
-    *slots, core = call(
+    down, slope = call(
+        down_kernel,
+        (table, struct((DT, edges), F32)),
+        (edge_embed, w_down_t),
+        1,
+    )
+    *slots, core, down_later = call(
         slot_kernel,
         (
             struct(in_index.shape, jnp.int32),
@@ -345,25 +351,21 @@
             struct(in_index.shape, F32),
             struct((L,) + in_index.shape, F32),
             struct((8, width), jnp.int32),
+            table,
         ),
-        (ks, block_counts, in_index, out_index, triplet_cos),
-        1,
+        (ks, block_counts, in_index, out_index, triplet_cos, down),
+        0.1,
         smem=(0, 1),
     )
     slots = tuple(slots)
 
-    down, slope = call(
-        down_kernel, (table, struct((DT, edges), F32)), (edge_embed, w_down_t), 1
-    )
     source = {0: down, 1: near(down, "gy"), 2: far(down, "gy")}
-    source[4], source[3] = far(down, "gx"), near(down, "gx")
+    source[4], source[3] = far(down_later, "gx"), near(down_later, "gx")
+    source[7], source[8] = far(source[1], "gx"), far(source[4], "gy")
+    source[5], source[6] = near(source[1], "gx"), near(source[2], "gx")
     feats = {}
     trip = w_rows = None
-    for places in ((0,), (3, 4), (1, 2), (5, 6), (7, 8)):
-        if places == (1, 2):
-            source[1], source[2], trip = together(source[1], source[2], trip)
-            source[7], source[8] = far(source[1], "gx"), far(source[2], "gx")
-            source[5], source[6] = near(source[1], "gx"), near(source[2], "gx")
+    for places in ((0, 3, 4), (1, 2, 5, 6), (7, 8)):
         n = len(places)
         base = trip is not None
         args = slots + (w_bil_t,) + tuple(source[p] for p in places) + ((trip,) if base else ())
@@ -373,7 +375,7 @@
             functools.partial(forward_kernel, places, base, not base),
             outs,
             args,
-            n * PAIR_US,
+            n * FORWARD_US,
         )
         w_rows = rest[0] if rest else w_rows
         for i, p in enumerate(places):
@@ -388,7 +390,7 @@
 
     sent = []
     grad_bil = None
-    for places in ((4, 7, 8), (3, 5, 6), (0, 1, 2)):
+    for places in ((7, 8), (4, 3, 5, 6), (0, 1, 2)):
         n = len(places)
         base = grad_bil is not None
         args = slots + (w_rows, d_trip) + tuple(feats[p] for p in places)
@@ -396,16 +398,20 @@
         last = scale if places[0] == 0 else None
         *out, grad_bil = call(
             functools.partial(backward_kernel, places, base, last),
-            (table, struct((n - 1, DT, edges), BF16), wide),
+            (struct((n, DT, edges), BF16), wide)
+            if places[0] == 7
+            else (table, struct((n - 1, DT, edges), BF16), wide),
             args,
-            n * PAIR_US,
+            n * BACKWARD_US,
         )
         sent.append(out)
-    far_pair, far_own = far(sent[0][1], "gx"), far(sent[0][0], "gx")
-    near_own, near_pair = (near(x, "gx") for x in sent[1])
-    own, pair = sent[2]
-    to_near, to_far = call(meet_kernel, (table, table), (pair, far_pair, near_pair), 0.5)
+    (far_pair,), (far_own, near_all), (own, pair) = sent
+    far_pair, near_all = far(far_pair, "gx"), near(near_all, "gx")
+    to_near, to_far, own, far_own = call(
+        meet_kernel, (table,) * 4, (own, pair, far_pair, near_all, far_own), 0.5
+    )
     from_near, from_far = near(to_near, "gy"), far(to_far, "gy")
+    far_own = far(far_own, "gx")
     result = struct((edges, width), BF16)
     updated, token = tiled(updated_kernel, 4, (edge_embed, trip, w_up), result, 2, after=to_near)
     share = struct((DT // 2 + DT, width), F32)
@@ -413,18 +419,18 @@
         functools.partial(final_kernel, scale),
         (table, share, share),
         (edge_embed, slope, core, grad_bil, grad_up)
-        + (own, far_own, near_own, from_near, from_far),
+        + (own, far_own, from_near, from_far),
         1,
         after=token,
     )
     sums = keep + near(send, "gx")
-    sums = sum_step(sums, *SUM_STEPS[0])
+    for step in SUM_STEPS[:2]:
+        sums = sum_step(sums, *step)
     grad_embed, token = tiled(
         embed_kernel, 4, (cotangent, d_pre, w_down_t), result, 2, sums, sums.shape
     )
-    sums = sum_step(sums, *SUM_STEPS[1]) + token
-    for step in SUM_STEPS[2:]:
-        sums = sum_step(sums, *step)
+    sums = sum_step(sums, *SUM_STEPS[2]) + token
+    sums = sum_step(sums, *SUM_STEPS[3])
     grad_down, grad_bil, grad_up = call(
         finish_kernel,
         (wide, wide, wide),

time: 103 us -> 101 us (0.981)
  waiting for transfers between devices: 20.1 us -> 17.9 us
  Pallas kernels: 30.2 us -> 28.8 us
    ppermute x16 -> x15, waiting for transfers between devices: 8.01 us -> 4.42 us  [swap(): lax.ppermute(x, axis, [(i, partner(i)) for i in range(lax.axis_size(axis))])]
    ppermute x16 -> x15, starting transfers between devices: 35.9 us -> 37.8 us  [swap(): lax.ppermute(x, axis, [(i, partner(i)) for i in range(lax.axis_size(axis))])]
    pallas_call x14 -> x12, Pallas kernels: 24.6 us -> 23.2 us  [call(): pl.pallas_call(kernel, out_shape=outs, in_specs=specs if after is None el...]
    ppermute x10, waiting for transfers between devices: 12.1 us -> 13.5 us  [sum_step(): got.append(lax.ppermute(x, BOTH, pairs).astype(F32))]
    ppermute x10, starting transfers between devices: 13.4 us -> 12.2 us  [sum_step(): got.append(lax.ppermute(x, BOTH, pairs).astype(F32))]
  transfers between devices with their start and end apart: 26 -> 25, of which waited for: 10 -> 10; matrix products, arithmetic and copies ran while one was open for 0% -> 0% of each run, Pallas kernels for 19% -> 19%
where the time goes in v3:
time: 101 us; the launch traced here: 100 us
  starting transfers between devices  49.9 us (49%)
  Pallas kernels  28.8 us (29%)
  waiting for transfers between devices  17.9 us (18%)
  local copies, waits for them, and re-layouts  2.62 us (3%)
    ppermute x15, starting transfers between devices, swap(): lax.ppermute(x, axis, [(i, partner(i)) for i in range(lax.axis_size(axis))])  37.8 us
    pallas_call x12, Pallas kernels, call(): pl.pallas_call(kernel, out_shape=outs, in_specs=specs if after is None el...  23.2 us
    ppermute x10, waiting for transfers between devices, sum_step(): got.append(lax.ppermute(x, BOTH, pairs).astype(F32))  13.5 us
    ppermute x10, starting transfers between devices, sum_step(): got.append(lax.ppermute(x, BOTH, pairs).astype(F32))  12.2 us
    pallas_call x2, Pallas kernels, tiled(): pl.pallas_call(kernel, grid=(steps,), out_shape=(out, jax.ShapeDtypeStruc...  5.6 us
    ppermute x15, waiting for transfers between devices, swap(): lax.ppermute(x, axis, [(i, partner(i)) for i in range(lax.axis_size(axis))])  4.42 us
    unnamed x22, local copies, waits for them, and re-layouts  2.47 us
  transfers between devices with their start and end apart: 25, of which 10 were waited for; matrix products, arithmetic and copies ran while one was open for 0% of the time, Pallas kernels for 19%

profile of v3, /device:TPU:1, one launch (start us, length us, event | category | flops | bytes accessed | tf_op | source)
XLA Modules:
  0.0 100.4 jit_solution(16317162955720913356)
XLA Ops:
  0.6 1.6 %copy-done = bf16[2048,512]{1,0:T(8,128)(2,1)S(1)} copy-done((bf16[2048,512]{1,0:T(8,128)(2,1)S(1)}, bf16[2048,512]{1,0:T(8,128)(2,1)}, u32[]{:S(2)}) %copy-start) | copy-done | bytes 2097176
  3.9 2.6 %collective-permute-start.2 = (bf16[64,2048]{1,0:T(8,128)(2,1)S(1)}, bf16[64,2048]{1,0:T(8,128)(2,1)S(1)}, u32[]{:S(2)}, u32[]{:S(2)}) collective-permute-start(bf16[64,2048]{1,0:T(8,128)(2,1)S(1)} %get-tuple-element.45.down_ref.refs_0_), channel_id=1, source_target_pairs={{0,1},{1,0},{2,3},{3,2},{4,5},{5,4},{6,7},{7,6},{8,9},{9,8},{10,11... | collective-permute-start | bytes 786440 | tf_op jit(solution)/shard_map/ppermute | solution.py:272
  6.4 4.7 %collective-permute-start.5 = (bf16[64,2048]{1,0:T(8,128)(2,1)S(1)}, bf16[64,2048]{1,0:T(8,128)(2,1)S(1)}, u32[]{:S(2)}, u32[]{:S(2)}) collective-permute-start(bf16[64,2048]{1,0:T(8,128)(2,1)S(1)} %get-tuple-element.45.down_ref.refs_0_), channel_id=1, source_target_pairs={{0,7},{1,2},{2,1},{3,4},{4,3},{5,6},{6,5},{7,0},{8,15},{9,10},{10,... | collective-permute-start | bytes 786440 | tf_op jit(solution)/shard_map/ppermute | solution.py:272
  12.1 2.4 %collective-permute-start.1 = (bf16[64,2048]{1,0:T(8,128)(2,1)S(1)}, bf16[64,2048]{1,0:T(8,128)(2,1)S(1)}, u32[]{:S(2)}, u32[]{:S(2)}) collective-permute-start(bf16[64,2048]{1,0:T(8,128)(2,1)S(1)} %get-tuple-element.50), channel_id=1, source_target_pairs={{0,248},{8,16},{16,8},{24,32},{32,24},{40,48},{48,40},{56,64},{64,... | collective-permute-start | bytes 786440 | tf_op jit(solution)/shard_map/ppermute | solution.py:272
  14.5 3.0 %collective-permute-start = (bf16[64,2048]{1,0:T(8,128)(2,1)S(1)}, bf16[64,2048]{1,0:T(8,128)(2,1)S(1)}, u32[]{:S(2)}, u32[]{:S(2)}) collective-permute-start(bf16[64,2048]{1,0:T(8,128)(2,1)S(1)} %get-tuple-element.50), channel_id=1, source_target_pairs={{0,8},{8,0},{16,24},{24,16},{32,40},{40,32},{48,56},{56,48},{64,72... | collective-permute-start | bytes 786440 | tf_op jit(solution)/shard_map/ppermute | solution.py:272
  18.4 1.1 %collective-permute-start.3 = (bf16[64,2048]{1,0:T(8,128)(2,1)S(1)}, bf16[64,2048]{1,0:T(8,128)(2,1)S(1)}, u32[]{:S(2)}, u32[]{:S(2)}) collective-permute-start(bf16[64,2048]{1,0:T(8,128)(2,1)S(1)} %collective-permute-done.2.refs_0_), channel_id=1, source_target_pairs={{0,248},{8,16},{16,8},{24,32},{32,24},{40,48},{48,40},{56,64},{64,... | collective-permute-start | bytes 786440 | tf_op jit(solution)/shard_map/ppermute | solution.py:272
  19.5 2.7 %collective-permute-start.4 = (bf16[64,2048]{1,0:T(8,128)(2,1)S(1)}, bf16[64,2048]{1,0:T(8,128)(2,1)S(1)}, u32[]{:S(2)}, u32[]{:S(2)}) collective-permute-start(bf16[64,2048]{1,0:T(8,128)(2,1)S(1)} %collective-permute-done.1.refs_2_), channel_id=1, source_target_pairs={{0,7},{1,2},{2,1},{3,4},{4,3},{5,6},{6,5},{7,0},{8,15},{9,10},{10,... | collective-permute-start | bytes 786440 | tf_op jit(solution)/shard_map/ppermute | solution.py:272
  22.1 2.6 %shard_map.130 = (f32[512,256]{1,0:T(8,128)S(1)}, bf16[192,768]{1,0:T(8,128)(2,1)S(1)}, bf16[64,512]{1,0:T(8,128)(2,1)S(1)}) custom-call(s32[9,768]{1,0:T(8,128)S(1)} %get-tuple-element.46.in_ref, s32[9,768]{1,0:T(8,128)S(1)} %get-tuple-element.47.out_ref, f32[9,768]{1,0:T(8,128)S(1)} %get-tuple-element.48.valid_ref, ...), custom_call_target="tpu_custom_call" | custom-call | flops 120000000 | bytes 360000 | tf_op jit(solution)/shard_map/pallas_call | solution.py:245
  24.8 3.1 %shard_map.131 = (f32[512,256]{1,0:T(8,128)S(1)}, bf16[256,768]{1,0:T(8,128)(2,1)S(1)}) custom-call(s32[9,768]{1,0:T(8,128)S(1)} %get-tuple-element.46.in_ref, s32[9,768]{1,0:T(8,128)S(1)} %get-tuple-element.47.out_ref, f32[9,768]{1,0:T(8,128)S(1)} %get-tuple-element.48.valid_ref, f32[8,9,768]{2,1,0:T(8,128)S(1)} %get-tuple-element.49.basis_ref, ...), custom_call_target="tpu_custom_call" | custom-call | flops 160000000 | bytes 480000 | tf_op jit(solution)/shard_map/pallas_call | solution.py:245
  28.0 2.1 %shard_map.132 = (f32[512,256]{1,0:T(8,128)S(1)}, bf16[128,768]{1,0:T(8,128)(2,1)S(1)}) custom-call(s32[9,768]{1,0:T(8,128)S(1)} %get-tuple-element.46.in_ref, s32[9,768]{1,0:T(8,128)S(1)} %get-tuple-element.47.out_ref, f32[9,768]{1,0:T(8,128)S(1)} %get-tuple-element.48.valid_ref, f32[8,9,768]{2,1,0:T(8,128)S(1)} %get-tuple-element.49.basis_ref, ...), custom_call_target="tpu_custom_call" | custom-call | flops 80000000 | bytes 240000 | tf_op jit(solution)/shard_map/pallas_call | solution.py:245
  30.1 3.0 %shard_map.133 = (bf16[64,2048]{1,0:T(8,128)(2,1)S(1)}, f32[64,512]{1,0:T(8,128)S(1)}, bf16[512,256]{1,0:T(8,128)(2,1)S(1)}) custom-call(bf16[2048,512]{1,0:T(8,128)(2,1)S(1)} %copy-done.7, f32[512,256]{1,0:T(8,128)S(1)} %get-tuple-element.54.trip_ref, bf16[64,512]{1,0:T(8,128)(2,1)S(1)} %copy-done.8), custom_call_target="tpu_custom_call" | custom-call | flops 2000000000 | bytes 6000000 | tf_op jit(solution)/shard_map/pallas_call | solution.py:245
  33.0 2.2 %shard_map.134 = (bf16[2,64,2048]{2,1,0:T(8,128)(2,1)S(1)}, f32[64,512]{1,0:T(8,128)S(1)}) custom-call(s32[9,768]{1,0:T(8,128)S(1)} %get-tuple-element.46.in_ref, s32[9,768]{1,0:T(8,128)S(1)} %get-tuple-element.47.out_ref, f32[9,768]{1,0:T(8,128)S(1)} %get-tuple-element.48.valid_ref, f32[8,9,768]{2,1,0:T(8,128)S(1)} %get-tuple-element.49.basis_ref, ...), custom_call_target="tpu_custom_call" | custom-call | flops 8000000000 | bytes 24000000 | tf_op jit(solution)/shard_map/pallas_call | solution.py:245
  35.2 2.9 %collective-permute-start.8 = (bf16[2,64,2048]{2,1,0:T(8,128)(2,1)S(1)}, bf16[2,64,2048]{2,1,0:T(8,128)(2,1)S(1)}, u32[]{:S(2)}, u32[]{:S(2)}) collective-permute-start(bf16[2,64,2048]{2,1,0:T(8,128)(2,1)S(1)} %get-tuple-element.63), channel_id=1, source_target_pairs={{0,248},{8,16},{16,8},{24,32},{32,24},{40,48},{48,40},{56,64},{64,... | collective-permute-start | bytes 1572872 | tf_op jit(solution)/shard_map/ppermute | solution.py:272
  38.1 4.0 %shard_map.135 = (bf16[64,2048]{1,0:T(8,128)(2,1)S(1)}, bf16[3,64,2048]{2,1,0:T(8,128)(2,1)S(1)}, f32[64,512]{1,0:T(8,128)S(1)}) custom-call(s32[9,768]{1,0:T(8,128)S(1)} %get-tuple-element.46.in_ref, s32[9,768]{1,0:T(8,128)S(1)} %get-tuple-element.47.out_ref, f32[9,768]{1,0:T(8,128)S(1)} %get-tuple-element.48.valid_ref, ...), custom_call_target="tpu_custom_call" | custom-call | flops 16000000000 | bytes 48000000 | tf_op jit(solution)/shard_map/pallas_call | solution.py:245
  42.1 3.9 %collective-permute-start.9 = (bf16[3,64,2048]{2,1,0:T(8,128)(2,1)S(1)}, bf16[3,64,2048]{2,1,0:T(8,128)(2,1)S(1)}, u32[]{:S(2)}, u32[]{:S(2)}) collective-permute-start(bf16[3,64,2048]{2,1,0:T(8,128)(2,1)S(1)} %get-tuple-element.64), channel_id=1, source_target_pairs={{0,8},{8,0},{16,24},{24,16},{32,40},{40,32},{48,56},{56,48},{64,72... | collective-permute-start | bytes 2359304 | tf_op jit(solution)/shard_map/ppermute | solution.py:272
  46.1 3.1 %shard_map.136 = (bf16[64,2048]{1,0:T(8,128)(2,1)S(1)}, bf16[2,64,2048]{2,1,0:T(8,128)(2,1)S(1)}, f32[64,512]{1,0:T(8,128)S(1)}) custom-call(s32[9,768]{1,0:T(8,128)S(1)} %get-tuple-element.46.in_ref, s32[9,768]{1,0:T(8,128)S(1)} %get-tuple-element.47.out_ref, f32[9,768]{1,0:T(8,128)S(1)} %get-tuple-element.48.valid_ref, ...), custom_call_target="tpu_custom_call" | custom-call | flops 12000000000 | bytes 36000000 | tf_op jit(solution)/shard_map/pallas_call | solution.py:245
  49.7 1.2 %collective-permute-start.12 = (bf16[64,2048]{1,0:T(8,128)(2,1)S(1)}, bf16[64,2048]{1,0:T(8,128)(2,1)S(1)}, u32[]{:S(2)}, u32[]{:S(2)}) collective-permute-start(bf16[64,2048]{1,0:T(8,128)(2,1)S(1)} %get-tuple-element.76), channel_id=1, source_target_pairs={{0,7},{1,2},{2,1},{3,4},{4,3},{5,6},{6,5},{7,0},{8,15},{9,10},{10,... | collective-permute-start | bytes 786440 | tf_op jit(solution)/shard_map/ppermute | solution.py:272
  50.9 3.0 %shard_map.138 = (bf16[2048,512]{1,0:T(8,128)(2,1)}, f32[8,128]{1,0:T(8,128)S(1)}) custom-call(bf16[64,2048]{1,0:T(8,128)(2,1)S(1)} %get-tuple-element.66.after_ref, bf16[2048,512]{1,0:T(8,128)(2,1)S(1)} %copy-done.1, bf16[512,256]{1,0:T(8,128)(2,1)S(1)} %get-tuple-element.67.trip_ref, bf16[64,512]{1,0:T(8,128)(2,1)S(1)} %copy-done.8), custom_call_target="tpu_custom_call" | custom-call | flops 2000000000 | bytes 6000000 | tf_op jit(solution)/shard_map/pallas_call | solution.py:257
  53.9 1.4 %collective-permute-done.10.refs_1_ = bf16[64,2048]{1,0:T(8,128)(2,1)S(1)} collective-permute-done((bf16[64,2048]{1,0:T(8,128)(2,1)S(1)}, bf16[64,2048]{1,0:T(8,128)(2,1)S(1)}, u32[]{:S(2)}, u32[]{:S(2)}) %collective-permute-start.10) | collective-permute-done | bytes 262176 | tf_op jit(solution)/shard_map/ppermute | solution.py:272
  56.7 5.7 %collective-permute-start.13 = (f32[96,512]{1,0:T(8,128)S(1)}, f32[96,512]{1,0:T(8,128)S(1)}, u32[]{:S(2)}, u32[]{:S(2)}) collective-permute-start(f32[96,512]{1,0:T(8,128)S(1)} %get-tuple-element.78), channel_id=1, source_target_pairs={{0,8},{8,0},{16,24},{24,16},{32,40},{40,32},{48,56},{56,48},{64,72... | collective-permute-start | bytes 589832 | tf_op jit(solution)/shard_map/ppermute | solution.py:272
  63.7 2.5 %collective-permute-start.14 = (bf16[96,512]{1,0:T(8,128)(2,1)S(1)}, bf16[96,512]{1,0:T(8,128)(2,1)S(1)}, u32[]{:S(2)}, u32[]{:S(2)}) collective-permute-start(bf16[96,512]{1,0:T(8,128)(2,1)S(1)} %add_convert_fusion.2), channel_id=1, source_target_pairs={{0,16},{1,17},{2,18},{3,19},{4,20},{5,21},{6,22},{7,23},{8,24},{9,... | collective-permute-start | bytes 294920 | tf_op jit(solution)/shard_map/ppermute | solution.py:314
  66.3 2.3 %collective-permute-done.16 = bf16[96,512]{1,0:T(8,128)(2,1)S(1)} collective-permute-done((bf16[96,512]{1,0:T(8,128)(2,1)S(1)}, bf16[96,512]{1,0:T(8,128)(2,1)S(1)}, u32[]{:S(2)}, u32[]{:S(2)}) %collective-permute-start.16) | collective-permute-done | bytes 98336 | tf_op jit(solution)/shard_map/ppermute | solution.py:314
  69.6 2.7 %collective-permute-start.19 = (bf16[96,512]{1,0:T(8,128)(2,1)S(1)}, bf16[96,512]{1,0:T(8,128)(2,1)S(1)}, u32[]{:S(2)}, u32[]{:S(2)}) collective-permute-start(bf16[96,512]{1,0:T(8,128)(2,1)S(1)} %add_convert_fusion.1), channel_id=1, source_target_pairs={{0,240},{1,241},{2,242},{3,243},{4,244},{5,245},{6,246},{7,247},{8... | collective-permute-start | bytes 294920 | tf_op jit(solution)/shard_map/ppermute | solution.py:314
  72.2 2.5 %collective-permute-start.17 = (bf16[96,512]{1,0:T(8,128)(2,1)S(1)}, bf16[96,512]{1,0:T(8,128)(2,1)S(1)}, u32[]{:S(2)}, u32[]{:S(2)}) collective-permute-start(bf16[96,512]{1,0:T(8,128)(2,1)S(1)} %add_convert_fusion.1), channel_id=1, source_target_pairs={{0,48},{1,49},{2,50},{3,51},{4,52},{5,53},{6,54},{7,55},{8,56},{9,... | collective-permute-start | bytes 294920 | tf_op jit(solution)/shard_map/ppermute | solution.py:314
  74.7 1.8 %collective-permute-done.19 = bf16[96,512]{1,0:T(8,128)(2,1)S(1)} collective-permute-done((bf16[96,512]{1,0:T(8,128)(2,1)S(1)}, bf16[96,512]{1,0:T(8,128)(2,1)S(1)}, u32[]{:S(2)}, u32[]{:S(2)}) %collective-permute-start.19) | collective-permute-done | bytes 98336 | tf_op jit(solution)/shard_map/ppermute | solution.py:314
  76.5 2.3 %collective-permute-done.18 = bf16[96,512]{1,0:T(8,128)(2,1)S(1)} collective-permute-done((bf16[96,512]{1,0:T(8,128)(2,1)S(1)}, bf16[96,512]{1,0:T(8,128)(2,1)S(1)}, u32[]{:S(2)}, u32[]{:S(2)}) %collective-permute-start.18) | collective-permute-done | bytes 98336 | tf_op jit(solution)/shard_map/ppermute | solution.py:314
  79.8 1.6 %collective-permute-start.21 = (bf16[96,512]{1,0:T(8,128)(2,1)S(1)}, bf16[96,512]{1,0:T(8,128)(2,1)S(1)}, u32[]{:S(2)}, u32[]{:S(2)}) collective-permute-start(bf16[96,512]{1,0:T(8,128)(2,1)S(1)} %get-tuple-element.85), channel_id=1, source_target_pairs={{0,3},{1,2},{2,1},{3,0},{4,7},{5,6},{6,5},{7,4},{8,11},{9,10},{10,... | collective-permute-start | bytes 294920 | tf_op jit(solution)/shard_map/ppermute | solution.py:314
  81.6 2.6 %shard_map.140 = (bf16[2048,512]{1,0:T(8,128)(2,1)}, f32[96,512]{1,0:T(8,128)S(1)}) custom-call(f32[96,512]{1,0:T(8,128)S(1)} %get-tuple-element.86.after_ref, bf16[2048,512]{1,0:T(8,128)(2,1)S(1)} %copy-done.7, bf16[64,2048]{1,0:T(8,128)(2,1)S(1)} %get-tuple-element.79.d_pre_ref, bf16[64,512]{1,0:T(8,128)(2,1)S(1)} %bitcast.17), custom_call_target="tpu_custom_call" | custom-call | flops 2000000000 | bytes 6000000 | tf_op jit(solution)/shard_map/pallas_call | solution.py:257
  84.2 2.9 %collective-permute-done.22 = bf16[96,512]{1,0:T(8,128)(2,1)S(1)} collective-permute-done((bf16[96,512]{1,0:T(8,128)(2,1)S(1)}, bf16[96,512]{1,0:T(8,128)(2,1)S(1)}, u32[]{:S(2)}, u32[]{:S(2)}) %collective-permute-start.22) | collective-permute-done | bytes 98336 | tf_op jit(solution)/shard_map/ppermute | solution.py:314
  87.2 1.5 %collective-permute-start.23 = (bf16[96,512]{1,0:T(8,128)(2,1)S(1)}, bf16[96,512]{1,0:T(8,128)(2,1)S(1)}, u32[]{:S(2)}, u32[]{:S(2)}) collective-permute-start(bf16[96,512]{1,0:T(8,128)(2,1)S(1)} %add_convert_fusion), channel_id=1, source_target_pairs={{0,7},{1,6},{2,5},{3,4},{4,3},{5,2},{6,1},{7,0},{8,15},{9,14},{10,... | collective-permute-start | bytes 294920 | tf_op jit(solution)/shard_map/ppermute | solution.py:314
  88.7 3.2 %collective-permute-done.23 = bf16[96,512]{1,0:T(8,128)(2,1)S(1)} collective-permute-done((bf16[96,512]{1,0:T(8,128)(2,1)S(1)}, bf16[96,512]{1,0:T(8,128)(2,1)S(1)}, u32[]{:S(2)}, u32[]{:S(2)}) %collective-permute-start.23) | collective-permute-done | bytes 98336 | tf_op jit(solution)/shard_map/ppermute | solution.py:314
  92.0 6.6 %collective-permute-start.24 = (f32[96,512]{1,0:T(8,128)S(1)}, f32[96,512]{1,0:T(8,128)S(1)}, u32[]{:S(2)}, u32[]{:S(2)}) collective-permute-start(f32[96,512]{1,0:T(8,128)S(1)} %convert_add_fusion.mine_ref), channel_id=1, source_target_pairs={{0,8},{8,0},{16,24},{24,16},{32,40},{40,32},{48,56},{56,48},{64,72... | collective-permute-start | bytes 589832 | tf_op jit(solution)/shard_map/ppermute | solution.py:272
  (63 shorter events, 10.7 us)
Async XLA Ops:
  3.1 8.1 %copy-start.3 = (s32[9,768]{1,0:T(8,128)S(1)}, s32[9,768]{1,0:T(8,128)}, u32[]{:S(2)}) copy-start(s32[9,768]{1,0:T(8,128)} %in_ref.1) | copy-start | bytes 82948
  3.1 8.1 %copy-start.4 = (s32[9,768]{1,0:T(8,128)S(1)}, s32[9,768]{1,0:T(8,128)}, u32[]{:S(2)}) copy-start(s32[9,768]{1,0:T(8,128)} %out_ref.1) | copy-start | bytes 82948
  3.1 8.1 %copy-start.5 = (f32[9,768]{1,0:T(8,128)S(1)}, f32[9,768]{1,0:T(8,128)}, u32[]{:S(2)}) copy-start(f32[9,768]{1,0:T(8,128)} %cos_ref.1) | copy-start | bytes 82948
  3.1 8.1 %copy-start.6 = (s32[9,12]{1,0:T(8,128)S(1)}, s32[9,12]{1,0:T(8,128)}, u32[]{:S(2)}) copy-start(s32[9,12]{1,0:T(8,128)} %counts_ref.1) | copy-start | bytes 1300
  3.1 19.1 %copy-start.2 = (bf16[512,64]{0,1:T(8,128)(2,1)S(1)}, bf16[512,64]{0,1:T(8,128)(2,1)}, u32[]{:S(2)}) copy-start(bf16[512,64]{0,1:T(8,128)(2,1)} %param.12) | copy-start | bytes 196612
  3.9 13.6 %collective-permute-start.2 = (bf16[64,2048]{1,0:T(8,128)(2,1)S(1)}, bf16[64,2048]{1,0:T(8,128)(2,1)S(1)}, u32[]{:S(2)}, u32[]{:S(2)}) collective-permute-start(bf16[64,2048]{1,0:T(8,128)(2,1)S(1)} %get-tuple-element.45.down_ref.refs_0_), channel_id=1, source_target_pairs={{0,1},{1,0},{2,3},{3,2},{4,5},{5,4},{6,7},{7,6},{8,9},{9,8},{10,11... | collective-permute-start | bytes 786440 | tf_op jit(solution)/shard_map/ppermute | solution.py:272
  6.4 11.0 %collective-permute-start.5 = (bf16[64,2048]{1,0:T(8,128)(2,1)S(1)}, bf16[64,2048]{1,0:T(8,128)(2,1)S(1)}, u32[]{:S(2)}, u32[]{:S(2)}) collective-permute-start(bf16[64,2048]{1,0:T(8,128)(2,1)S(1)} %get-tuple-element.45.down_ref.refs_0_), channel_id=1, source_target_pairs={{0,7},{1,2},{2,1},{3,4},{4,3},{5,6},{6,5},{7,0},{8,15},{9,10},{10,... | collective-permute-start | bytes 786440 | tf_op jit(solution)/shard_map/ppermute | solution.py:272
  12.1 7.4 %collective-permute-start.1 = (bf16[64,2048]{1,0:T(8,128)(2,1)S(1)}, bf16[64,2048]{1,0:T(8,128)(2,1)S(1)}, u32[]{:S(2)}, u32[]{:S(2)}) collective-permute-start(bf16[64,2048]{1,0:T(8,128)(2,1)S(1)} %get-tuple-element.50), channel_id=1, source_target_pairs={{0,248},{8,16},{16,8},{24,32},{32,24},{40,48},{48,40},{56,64},{64,... | collective-permute-start | bytes 786440 | tf_op jit(solution)/shard_map/ppermute | solution.py:272
  14.5 7.7 %collective-permute-start = (bf16[64,2048]{1,0:T(8,128)(2,1)S(1)}, bf16[64,2048]{1,0:T(8,128)(2,1)S(1)}, u32[]{:S(2)}, u32[]{:S(2)}) collective-permute-start(bf16[64,2048]{1,0:T(8,128)(2,1)S(1)} %get-tuple-element.50), channel_id=1, source_target_pairs={{0,8},{8,0},{16,24},{24,16},{32,40},{40,32},{48,56},{56,48},{64,72... | collective-permute-start | bytes 786440 | tf_op jit(solution)/shard_map/ppermute | solution.py:272
  17.5 7.3 %collective-permute-start.6 = (bf16[64,2048]{1,0:T(8,128)(2,1)S(1)}, bf16[64,2048]{1,0:T(8,128)(2,1)S(1)}, u32[]{:S(2)}, u32[]{:S(2)}) collective-permute-start(bf16[64,2048]{1,0:T(8,128)(2,1)S(1)} %collective-permute-done.2.refs_0_), channel_id=1, source_target_pairs={{0,8},{8,0},{16,24},{24,16},{32,40},{40,32},{48,56},{56,48},{64,72... | collective-permute-start | bytes 786440 | tf_op jit(solution)/shard_map/ppermute | solution.py:272
  17.5 7.3 %collective-permute-start.7 = (bf16[64,2048]{1,0:T(8,128)(2,1)S(1)}, bf16[64,2048]{1,0:T(8,128)(2,1)S(1)}, u32[]{:S(2)}, u32[]{:S(2)}) collective-permute-start(bf16[64,2048]{1,0:T(8,128)(2,1)S(1)} %collective-permute-done.5.refs_1_), channel_id=1, source_target_pairs={{0,8},{8,0},{16,24},{24,16},{32,40},{40,32},{48,56},{56,48},{64,72... | collective-permute-start | bytes 786440 | tf_op jit(solution)/shard_map/ppermute | solution.py:272
  18.4 9.6 %collective-permute-start.3 = (bf16[64,2048]{1,0:T(8,128)(2,1)S(1)}, bf16[64,2048]{1,0:T(8,128)(2,1)S(1)}, u32[]{:S(2)}, u32[]{:S(2)}) collective-permute-start(bf16[64,2048]{1,0:T(8,128)(2,1)S(1)} %collective-permute-done.2.refs_0_), channel_id=1, source_target_pairs={{0,248},{8,16},{16,8},{24,32},{32,24},{40,48},{48,40},{56,64},{64,... | collective-permute-start | bytes 786440 | tf_op jit(solution)/shard_map/ppermute | solution.py:272
  19.5 8.5 %collective-permute-start.4 = (bf16[64,2048]{1,0:T(8,128)(2,1)S(1)}, bf16[64,2048]{1,0:T(8,128)(2,1)S(1)}, u32[]{:S(2)}, u32[]{:S(2)}) collective-permute-start(bf16[64,2048]{1,0:T(8,128)(2,1)S(1)} %collective-permute-done.1.refs_2_), channel_id=1, source_target_pairs={{0,7},{1,2},{2,1},{3,4},{4,3},{5,6},{6,5},{7,0},{8,15},{9,10},{10,... | collective-permute-start | bytes 786440 | tf_op jit(solution)/shard_map/ppermute | solution.py:272
  24.8 5.2 %copy-start.7 = (bf16[2048,512]{1,0:T(8,128)(2,1)S(1)}, bf16[2048,512]{1,0:T(8,128)(2,1)}, u32[]{:S(2)}) copy-start(bf16[2048,512]{1,0:T(8,128)(2,1)} %cot_ref.3) | copy-start | bytes 6291460
  35.2 13.9 %collective-permute-start.8 = (bf16[2,64,2048]{2,1,0:T(8,128)(2,1)S(1)}, bf16[2,64,2048]{2,1,0:T(8,128)(2,1)S(1)}, u32[]{:S(2)}, u32[]{:S(2)}) collective-permute-start(bf16[2,64,2048]{2,1,0:T(8,128)(2,1)S(1)} %get-tuple-element.63), channel_id=1, source_target_pairs={{0,248},{8,16},{16,8},{24,32},{32,24},{40,48},{48,40},{56,64},{64,... | collective-permute-start | bytes 1572872 | tf_op jit(solution)/shard_map/ppermute | solution.py:272
  42.1 7.0 %collective-permute-start.9 = (bf16[3,64,2048]{2,1,0:T(8,128)(2,1)S(1)}, bf16[3,64,2048]{2,1,0:T(8,128)(2,1)S(1)}, u32[]{:S(2)}, u32[]{:S(2)}) collective-permute-start(bf16[3,64,2048]{2,1,0:T(8,128)(2,1)S(1)} %get-tuple-element.64), channel_id=1, source_target_pairs={{0,8},{8,0},{16,24},{24,16},{32,40},{40,32},{48,56},{56,48},{64,72... | collective-permute-start | bytes 2359304 | tf_op jit(solution)/shard_map/ppermute | solution.py:272
  49.5 5.9 %collective-permute-start.10 = (bf16[64,2048]{1,0:T(8,128)(2,1)S(1)}, bf16[64,2048]{1,0:T(8,128)(2,1)S(1)}, u32[]{:S(2)}, u32[]{:S(2)}) collective-permute-start(bf16[64,2048]{1,0:T(8,128)(2,1)S(1)} %get-tuple-element.75), channel_id=1, source_target_pairs={{0,248},{8,16},{16,8},{24,32},{32,24},{40,48},{48,40},{56,64},{64,... | collective-permute-start | bytes 786440 | tf_op jit(solution)/shard_map/ppermute | solution.py:272
  49.6 5.8 %collective-permute-start.11 = (bf16[64,2048]{1,0:T(8,128)(2,1)S(1)}, bf16[64,2048]{1,0:T(8,128)(2,1)S(1)}, u32[]{:S(2)}, u32[]{:S(2)}) collective-permute-start(bf16[64,2048]{1,0:T(8,128)(2,1)S(1)} %get-tuple-element.66.after_ref), channel_id=1, source_target_pairs={{0,1},{1,0},{2,3},{3,2},{4,5},{5,4},{6,7},{7,6},{8,9},{9,8},{10,11... | collective-permute-start | bytes 786440 | tf_op jit(solution)/shard_map/ppermute | solution.py:272
  49.7 6.5 %collective-permute-start.12 = (bf16[64,2048]{1,0:T(8,128)(2,1)S(1)}, bf16[64,2048]{1,0:T(8,128)(2,1)S(1)}, u32[]{:S(2)}, u32[]{:S(2)}) collective-permute-start(bf16[64,2048]{1,0:T(8,128)(2,1)S(1)} %get-tuple-element.76), channel_id=1, source_target_pairs={{0,7},{1,2},{2,1},{3,4},{4,3},{5,6},{6,5},{7,0},{8,15},{9,10},{10,... | collective-permute-start | bytes 786440 | tf_op jit(solution)/shard_map/ppermute | solution.py:272
  56.2 25.4 %copy-start.10 = (bf16[512,64]{0,1:T(8,128)(2,1)S(1)}, bf16[512,64]{0,1:T(8,128)(2,1)}, u32[]{:S(2)}) copy-start(bf16[512,64]{0,1:T(8,128)(2,1)} %param.11) | copy-start | bytes 196612
  56.7 6.8 %collective-permute-start.13 = (f32[96,512]{1,0:T(8,128)S(1)}, f32[96,512]{1,0:T(8,128)S(1)}, u32[]{:S(2)}, u32[]{:S(2)}) collective-permute-start(f32[96,512]{1,0:T(8,128)S(1)} %get-tuple-element.78), channel_id=1, source_target_pairs={{0,8},{8,0},{16,24},{24,16},{32,40},{40,32},{48,56},{56,48},{64,72... | collective-permute-start | bytes 589832 | tf_op jit(solution)/shard_map/ppermute | solution.py:272
  63.5 5.0 %collective-permute-start.16 = (bf16[96,512]{1,0:T(8,128)(2,1)S(1)}, bf16[96,512]{1,0:T(8,128)(2,1)S(1)}, u32[]{:S(2)}, u32[]{:S(2)}) collective-permute-start(bf16[96,512]{1,0:T(8,128)(2,1)S(1)} %add_convert_fusion.2), channel_id=1, source_target_pairs={{0,80},{1,81},{2,82},{3,83},{4,84},{5,85},{6,86},{7,87},{8,88},{9,... | collective-permute-start | bytes 294920 | tf_op jit(solution)/shard_map/ppermute | solution.py:314
  63.6 5.9 %collective-permute-start.15 = (bf16[96,512]{1,0:T(8,128)(2,1)S(1)}, bf16[96,512]{1,0:T(8,128)(2,1)S(1)}, u32[]{:S(2)}, u32[]{:S(2)}) collective-permute-start(bf16[96,512]{1,0:T(8,128)(2,1)S(1)} %add_convert_fusion.2), channel_id=1, source_target_pairs={{0,64},{1,65},{2,66},{3,67},{4,68},{5,69},{6,70},{7,71},{8,72},{9,... | collective-permute-start | bytes 294920 | tf_op jit(solution)/shard_map/ppermute | solution.py:314
  63.7 5.8 %collective-permute-start.14 = (bf16[96,512]{1,0:T(8,128)(2,1)S(1)}, bf16[96,512]{1,0:T(8,128)(2,1)S(1)}, u32[]{:S(2)}, u32[]{:S(2)}) collective-permute-start(bf16[96,512]{1,0:T(8,128)(2,1)S(1)} %add_convert_fusion.2), channel_id=1, source_target_pairs={{0,16},{1,17},{2,18},{3,19},{4,20},{5,21},{6,22},{7,23},{8,24},{9,... | collective-permute-start | bytes 294920 | tf_op jit(solution)/shard_map/ppermute | solution.py:314
  69.6 6.9 %collective-permute-start.19 = (bf16[96,512]{1,0:T(8,128)(2,1)S(1)}, bf16[96,512]{1,0:T(8,128)(2,1)S(1)}, u32[]{:S(2)}, u32[]{:S(2)}) collective-permute-start(bf16[96,512]{1,0:T(8,128)(2,1)S(1)} %add_convert_fusion.1), channel_id=1, source_target_pairs={{0,240},{1,241},{2,242},{3,243},{4,244},{5,245},{6,246},{7,247},{8... | collective-permute-start | bytes 294920 | tf_op jit(solution)/shard_map/ppermute | solution.py:314
  72.2 6.6 %collective-permute-start.18 = (bf16[96,512]{1,0:T(8,128)(2,1)S(1)}, bf16[96,512]{1,0:T(8,128)(2,1)S(1)}, u32[]{:S(2)}, u32[]{:S(2)}) collective-permute-start(bf16[96,512]{1,0:T(8,128)(2,1)S(1)} %add_convert_fusion.1), channel_id=1, source_target_pairs={{0,192},{1,193},{2,194},{3,195},{4,196},{5,197},{6,198},{7,199},{8... | collective-permute-start | bytes 294920 | tf_op jit(solution)/shard_map/ppermute | solution.py:314
  72.2 6.6 %collective-permute-start.17 = (bf16[96,512]{1,0:T(8,128)(2,1)S(1)}, bf16[96,512]{1,0:T(8,128)(2,1)S(1)}, u32[]{:S(2)}, u32[]{:S(2)}) collective-permute-start(bf16[96,512]{1,0:T(8,128)(2,1)S(1)} %add_convert_fusion.1), channel_id=1, source_target_pairs={{0,48},{1,49},{2,50},{3,51},{4,52},{5,53},{6,54},{7,55},{8,56},{9,... | collective-permute-start | bytes 294920 | tf_op jit(solution)/shard_map/ppermute | solution.py:314
  78.9 8.2 %collective-permute-start.22 = (bf16[96,512]{1,0:T(8,128)(2,1)S(1)}, bf16[96,512]{1,0:T(8,128)(2,1)S(1)}, u32[]{:S(2)}, u32[]{:S(2)}) collective-permute-start(bf16[96,512]{1,0:T(8,128)(2,1)S(1)} %get-tuple-element.85), channel_id=1, source_target_pairs={{0,2},{1,3},{2,0},{3,1},{4,6},{5,7},{6,4},{7,5},{8,10},{9,11},{10,... | collective-permute-start | bytes 294920 | tf_op jit(solution)/shard_map/ppermute | solution.py:314
  79.8 7.3 %collective-permute-start.21 = (bf16[96,512]{1,0:T(8,128)(2,1)S(1)}, bf16[96,512]{1,0:T(8,128)(2,1)S(1)}, u32[]{:S(2)}, u32[]{:S(2)}) collective-permute-start(bf16[96,512]{1,0:T(8,128)(2,1)S(1)} %get-tuple-element.85), channel_id=1, source_target_pairs={{0,3},{1,2},{2,1},{3,0},{4,7},{5,6},{6,5},{7,4},{8,11},{9,10},{10,... | collective-permute-start | bytes 294920 | tf_op jit(solution)/shard_map/ppermute | solution.py:314
  81.5 5.6 %collective-permute-start.20 = (bf16[96,512]{1,0:T(8,128)(2,1)S(1)}, bf16[96,512]{1,0:T(8,128)(2,1)S(1)}, u32[]{:S(2)}, u32[]{:S(2)}) collective-permute-start(bf16[96,512]{1,0:T(8,128)(2,1)S(1)} %get-tuple-element.85), channel_id=1, source_target_pairs={{0,1},{1,0},{2,3},{3,2},{4,5},{5,4},{6,7},{7,6},{8,9},{9,8},{10,11... | collective-permute-start | bytes 294920 | tf_op jit(solution)/shard_map/ppermute | solution.py:314
  87.2 4.8 %collective-permute-start.23 = (bf16[96,512]{1,0:T(8,128)(2,1)S(1)}, bf16[96,512]{1,0:T(8,128)(2,1)S(1)}, u32[]{:S(2)}, u32[]{:S(2)}) collective-permute-start(bf16[96,512]{1,0:T(8,128)(2,1)S(1)} %add_convert_fusion), channel_id=1, source_target_pairs={{0,7},{1,6},{2,5},{3,4},{4,3},{5,2},{6,1},{7,0},{8,15},{9,14},{10,... | collective-permute-start | bytes 294920 | tf_op jit(solution)/shard_map/ppermute | solution.py:314
  92.0 7.6 %collective-permute-start.24 = (f32[96,512]{1,0:T(8,128)S(1)}, f32[96,512]{1,0:T(8,128)S(1)}, u32[]{:S(2)}, u32[]{:S(2)}) collective-permute-start(f32[96,512]{1,0:T(8,128)S(1)} %convert_add_fusion.mine_ref), channel_id=1, source_target_pairs={{0,8},{8,0},{16,24},{24,16},{32,40},{40,32},{48,56},{56,48},{64,72... | collective-permute-start | bytes 589832 | tf_op jit(solution)/shard_map/ppermute | solution.py:272
  (4 other events, 9.4 us)

commit v4 on v3

--- a/solution.py
+++ b/solution.py
@@ -102,20 +102,25 @@
     slope_ref[...] = sig * (1.0 + pre * (1.0 - sig))
 
 
-def forward_kernel(places, base, rows, in_ref, out_ref, valid_ref, basis_ref, w_ref, *refs):
+def forward_kernel(places, base, rows, split, in_ref, out_ref, valid_ref, basis_ref, w_ref, *refs):
     sources, refs = refs[: len(places)], refs[len(places) :]
+    if split:
+        whole, rest = sources[0][...], sources[1][...]
+        sources = whole[:DT], jnp.concatenate([whole[DT:], rest], axis=0)
     total_ref, outs = refs[0] if base else None, refs[base:]
     trip_ref, feat_ref = outs[:2]
     w = w_ref[...]
     if rows:
+        outs[3][...] = sources[0][...]
         outs[2][...] = jnp.concatenate(
             [w[:, l * DT : (l + 1) * DT].astype(F32).T for l in range(L)], axis=1
         ).astype(BF16)
-    parts = sources[0].shape[-1] // Q
+    parts = trip_ref.shape[0] // DT
     for i, p in enumerate(places):
         in_idx = in_ref[p : p + 1, :]
         out_idx = out_ref[p : p + 1, :]
-        feat = pick(sources[i][...], one_hot(in_idx), in_idx // Q)
+        source = sources[i] if split else sources[i][...]
+        feat = pick(source, one_hot(in_idx), in_idx // Q)
         feat_ref[i * DT : (i + 1) * DT, :] = feat.astype(BF16)
         message = dot(w, expand(basis_ref, p, feat), NN) * valid_ref[p : p + 1, :]
         part = collect(message, one_hot(out_idx), out_idx // Q, parts)
@@ -360,24 +365,29 @@
     slots = tuple(slots)
 
     source = {0: down, 1: near(down, "gy"), 2: far(down, "gy")}
-    source[4], source[3] = far(down_later, "gx"), near(down_later, "gx")
-    source[7], source[8] = far(source[1], "gx"), far(source[4], "gy")
-    source[5], source[6] = near(source[1], "gx"), near(source[2], "gx")
     feats = {}
     trip = w_rows = None
-    for places in ((0, 3, 4), (1, 2, 5, 6), (7, 8)):
+    for places in ((0,), (3, 4), (1, 2, 5, 6), (7, 8)):
         n = len(places)
         base = trip is not None
-        args = slots + (w_bil_t,) + tuple(source[p] for p in places) + ((trip,) if base else ())
+        split = places == (7, 8)
+        blocks = (along_x, along_y) if split else tuple(source[p] for p in places)
+        args = slots + (w_bil_t,) + blocks + ((trip,) if base else ())
         outs = (stack, struct((n * DT, SLOTS), BF16))
-        outs += () if base else (struct((DT, L * DT), BF16),)
+        outs += () if base else (struct((DT, L * DT), BF16), table)
         trip, feat, *rest = call(
-            functools.partial(forward_kernel, places, base, not base),
+            functools.partial(forward_kernel, places, base, not base, split),
             outs,
             args,
             n * FORWARD_US,
         )
-        w_rows = rest[0] if rest else w_rows
+        if rest:
+            w_rows, down = rest
+            source[4], source[3] = far(down, "gx"), near(down, "gx")
+            half = DT // 2
+            along_x = far(jnp.concatenate([source[1], source[2][:half]], axis=0), "gx")
+            along_y = far(source[4][half:], "gy")
+            source[5], source[6] = near(source[1], "gx"), near(source[2], "gx")
         for i, p in enumerate(places):
             feats[p] = feat[i * DT : (i + 1) * DT]
 

time: 101 us -> 99.1 us (0.981)
  waiting for transfers between devices: 17.9 us -> 15.2 us
  Pallas kernels: 28.8 us -> 30 us
    ppermute x10, waiting for transfers between devices: 13.5 us -> 10.8 us  [sum_step(): got.append(lax.ppermute(x, BOTH, pairs).astype(F32))]
    pallas_call x12 -> x13, Pallas kernels: 23.2 us -> 24.4 us  [call(): pl.pallas_call(kernel, out_shape=outs, in_specs=specs if after is None el...]
  transfers between devices with their start and end apart: 25 -> 25, of which waited for: 10 -> 11; matrix products, arithmetic and copies ran while one was open for 0% -> 0% of each run, Pallas kernels for 19% -> 21%
where the time goes in v4:
time: 99.1 us; the launch traced here: 98.9 us
  starting transfers between devices  50 us (50%)
  Pallas kernels  30 us (30%)
  waiting for transfers between devices  15.2 us (15%)
  local copies, waits for them, and re-layouts  2.63 us (3%)
    ppermute x15, starting transfers between devices, swap(): lax.ppermute(x, axis, [(i, partner(i)) for i in range(lax.axis_size(axis))])  37.1 us
    pallas_call x13, Pallas kernels, call(): pl.pallas_call(kernel, out_shape=outs, in_specs=specs if after is None el...  24.4 us
    ppermute x10, starting transfers between devices, sum_step(): got.append(lax.ppermute(x, BOTH, pairs).astype(F32))  12.9 us
    ppermute x10, waiting for transfers between devices, sum_step(): got.append(lax.ppermute(x, BOTH, pairs).astype(F32))  10.8 us
    pallas_call x2, Pallas kernels, tiled(): pl.pallas_call(kernel, grid=(steps,), out_shape=(out, jax.ShapeDtypeStruc...  5.59 us
    ppermute x15, waiting for transfers between devices, swap(): lax.ppermute(x, axis, [(i, partner(i)) for i in range(lax.axis_size(axis))])  4.37 us
    unnamed x22, local copies, waits for them, and re-layouts  2.47 us
  transfers between devices with their start and end apart: 25, of which 11 were waited for; matrix products, arithmetic and copies ran while one was open for 0% of the time, Pallas kernels for 21%

profile of v4, /device:TPU:1, one launch (start us, length us, event | category | flops | bytes accessed | tf_op | source)
XLA Modules:
  0.0 98.9 jit_solution(10153526748234774742)
XLA Ops:
  0.6 1.6 %copy-done = bf16[2048,512]{1,0:T(8,128)(2,1)S(1)} copy-done((bf16[2048,512]{1,0:T(8,128)(2,1)S(1)}, bf16[2048,512]{1,0:T(8,128)(2,1)}, u32[]{:S(2)}) %copy-start) | copy-done | bytes 2097176
  3.9 6.5 %collective-permute-start.1 = (bf16[64,2048]{1,0:T(8,128)(2,1)S(1)}, bf16[64,2048]{1,0:T(8,128)(2,1)S(1)}, u32[]{:S(2)}, u32[]{:S(2)}) collective-permute-start(bf16[64,2048]{1,0:T(8,128)(2,1)S(1)} %get-tuple-element.47.down_ref.refs_0_), channel_id=1, source_target_pairs={{0,7},{1,2},{2,1},{3,4},{4,3},{5,6},{6,5},{7,0},{8,15},{9,10},{10,... | collective-permute-start | bytes 786440 | tf_op jit(solution)/shard_map/ppermute | solution.py:277
  10.5 1.5 %shard_map.129 = (s32[9,768]{1,0:T(8,128)S(1)}, s32[9,768]{1,0:T(8,128)S(1)}, f32[9,768]{1,0:T(8,128)S(1)}, f32[8,9,768]{2,1,0:T(8,128)S(1)}, s32[8,512]{1,0:T(8,128)S(1)}, /*index=5*/bf16[64,2048]{1,0:T(8,128)(2,1)}) custom-call(s32[10]{0:T(128)S(1)} %stack.39.ks_ref, s32[9,12]{1,0:T(8,128)S(1)} %copy-done.6, s32[9,768]{1,0:T(8,128)S(1)} %copy-done.3, ...), custom_call_target="tpu_custom_call" | custom-call | flops 100000000 | bytes 300000 | tf_op jit(solution)/shard_map/pallas_call | solution.py:250
  12.0 1.2 %shard_map.130 = (f32[512,256]{1,0:T(8,128)S(1)}, bf16[64,768]{1,0:T(8,128)(2,1)S(1)}, bf16[64,512]{1,0:T(8,128)(2,1)S(1)}, bf16[64,2048]{1,0:T(8,128)(2,1)S(1)}) custom-call(s32[9,768]{1,0:T(8,128)S(1)} %get-tuple-element.48.in_ref, s32[9,768]{1,0:T(8,128)S(1)} %get-tuple-element.49.out_ref, f32[9,768]{1,0:T(8,128)S(1)} %get-tuple-element.50.valid_ref, ...), custom_call_target="tpu_custom_call" | custom-call | flops 40000000 | bytes 120000 | tf_op jit(solution)/shard_map/pallas_call | solution.py:250
  13.1 2.1 %collective-permute-start.3 = (bf16[64,2048]{1,0:T(8,128)(2,1)S(1)}, bf16[64,2048]{1,0:T(8,128)(2,1)S(1)}, u32[]{:S(2)}, u32[]{:S(2)}) collective-permute-start(bf16[64,2048]{1,0:T(8,128)(2,1)S(1)} %get-tuple-element.53), channel_id=1, source_target_pairs={{0,248},{8,16},{16,8},{24,32},{32,24},{40,48},{48,40},{56,64},{64,... | collective-permute-start | bytes 786440 | tf_op jit(solution)/shard_map/ppermute | solution.py:277
  15.3 3.3 %collective-permute-start.7 = (bf16[64,2048]{1,0:T(8,128)(2,1)S(1)}, bf16[64,2048]{1,0:T(8,128)(2,1)S(1)}, u32[]{:S(2)}, u32[]{:S(2)}) collective-permute-start(bf16[64,2048]{1,0:T(8,128)(2,1)S(1)} %get-tuple-element.53), channel_id=1, source_target_pairs={{0,8},{8,0},{16,24},{24,16},{32,40},{40,32},{48,56},{56,48},{64,72... | collective-permute-start | bytes 786440 | tf_op jit(solution)/shard_map/ppermute | solution.py:277
  20.3 2.1 %collective-permute-start.4 = (bf16[32,2048]{1,0:T(8,128)(2,1)S(1)}, bf16[32,2048]{1,0:T(8,128)(2,1)S(1)}, u32[]{:S(2)}, u32[]{:S(2)}) collective-permute-start(bf16[32,2048]{1,0:T(8,128)(2,1)S(1)} %slice.41), channel_id=1, source_target_pairs={{0,7},{1,2},{2,1},{3,4},{4,3},{5,6},{6,5},{7,0},{8,15},{9,10},{10,... | collective-permute-start | bytes 393224 | tf_op jit(solution)/shard_map/ppermute | solution.py:277
  22.4 2.1 %shard_map.131 = (f32[512,256]{1,0:T(8,128)S(1)}, bf16[128,768]{1,0:T(8,128)(2,1)S(1)}) custom-call(s32[9,768]{1,0:T(8,128)S(1)} %get-tuple-element.48.in_ref, s32[9,768]{1,0:T(8,128)S(1)} %get-tuple-element.49.out_ref, f32[9,768]{1,0:T(8,128)S(1)} %get-tuple-element.50.valid_ref, f32[8,9,768]{2,1,0:T(8,128)S(1)} %get-tuple-element.51.basis_ref, ...), custom_call_target="tpu_custom_call" | custom-call | flops 80000000 | bytes 240000 | tf_op jit(solution)/shard_map/pallas_call | solution.py:250
  24.5 3.1 %shard_map.132 = (f32[512,256]{1,0:T(8,128)S(1)}, bf16[256,768]{1,0:T(8,128)(2,1)S(1)}) custom-call(s32[9,768]{1,0:T(8,128)S(1)} %get-tuple-element.48.in_ref, s32[9,768]{1,0:T(8,128)S(1)} %get-tuple-element.49.out_ref, f32[9,768]{1,0:T(8,128)S(1)} %get-tuple-element.50.valid_ref, f32[8,9,768]{2,1,0:T(8,128)S(1)} %get-tuple-element.51.basis_ref, ...), custom_call_target="tpu_custom_call" | custom-call | flops 160000000 | bytes 480000 | tf_op jit(solution)/shard_map/pallas_call | solution.py:250
  27.7 2.1 %shard_map.133 = (f32[512,256]{1,0:T(8,128)S(1)}, bf16[128,768]{1,0:T(8,128)(2,1)S(1)}) custom-call(s32[9,768]{1,0:T(8,128)S(1)} %get-tuple-element.48.in_ref, s32[9,768]{1,0:T(8,128)S(1)} %get-tuple-element.49.out_ref, f32[9,768]{1,0:T(8,128)S(1)} %get-tuple-element.50.valid_ref, f32[8,9,768]{2,1,0:T(8,128)S(1)} %get-tuple-element.51.basis_ref, ...), custom_call_target="tpu_custom_call" | custom-call | flops 80000000 | bytes 240000 | tf_op jit(solution)/shard_map/pallas_call | solution.py:250
  29.8 3.0 %shard_map.134 = (bf16[64,2048]{1,0:T(8,128)(2,1)S(1)}, f32[64,512]{1,0:T(8,128)S(1)}, bf16[512,256]{1,0:T(8,128)(2,1)S(1)}) custom-call(bf16[2048,512]{1,0:T(8,128)(2,1)S(1)} %copy-done.7, f32[512,256]{1,0:T(8,128)S(1)} %get-tuple-element.57.trip_ref, bf16[64,512]{1,0:T(8,128)(2,1)S(1)} %copy-done.8), custom_call_target="tpu_custom_call" | custom-call | flops 2000000000 | bytes 6000000 | tf_op jit(solution)/shard_map/pallas_call | solution.py:250
  32.8 2.2 %shard_map.135 = (bf16[2,64,2048]{2,1,0:T(8,128)(2,1)S(1)}, f32[64,512]{1,0:T(8,128)S(1)}) custom-call(s32[9,768]{1,0:T(8,128)S(1)} %get-tuple-element.48.in_ref, s32[9,768]{1,0:T(8,128)S(1)} %get-tuple-element.49.out_ref, f32[9,768]{1,0:T(8,128)S(1)} %get-tuple-element.50.valid_ref, f32[8,9,768]{2,1,0:T(8,128)S(1)} %get-tuple-element.51.basis_ref, ...), custom_call_target="tpu_custom_call" | custom-call | flops 8000000000 | bytes 24000000 | tf_op jit(solution)/shard_map/pallas_call | solution.py:250
  35.0 1.4 %collective-permute-start.8 = (bf16[2,64,2048]{2,1,0:T(8,128)(2,1)S(1)}, bf16[2,64,2048]{2,1,0:T(8,128)(2,1)S(1)}, u32[]{:S(2)}, u32[]{:S(2)}) collective-permute-start(bf16[2,64,2048]{2,1,0:T(8,128)(2,1)S(1)} %get-tuple-element.67), channel_id=1, source_target_pairs={{0,248},{8,16},{16,8},{24,32},{32,24},{40,48},{48,40},{56,64},{64,... | collective-permute-start | bytes 1572872 | tf_op jit(solution)/shard_map/ppermute | solution.py:277
  36.4 4.0 %shard_map.136 = (bf16[64,2048]{1,0:T(8,128)(2,1)S(1)}, bf16[3,64,2048]{2,1,0:T(8,128)(2,1)S(1)}, f32[64,512]{1,0:T(8,128)S(1)}) custom-call(s32[9,768]{1,0:T(8,128)S(1)} %get-tuple-element.48.in_ref, s32[9,768]{1,0:T(8,128)S(1)} %get-tuple-element.49.out_ref, f32[9,768]{1,0:T(8,128)S(1)} %get-tuple-element.50.valid_ref, ...), custom_call_target="tpu_custom_call" | custom-call | flops 16000000000 | bytes 48000000 | tf_op jit(solution)/shard_map/pallas_call | solution.py:250
  40.4 6.3 %collective-permute-start.9 = (bf16[3,64,2048]{2,1,0:T(8,128)(2,1)S(1)}, bf16[3,64,2048]{2,1,0:T(8,128)(2,1)S(1)}, u32[]{:S(2)}, u32[]{:S(2)}) collective-permute-start(bf16[3,64,2048]{2,1,0:T(8,128)(2,1)S(1)} %get-tuple-element.68), channel_id=1, source_target_pairs={{0,8},{8,0},{16,24},{24,16},{32,40},{40,32},{48,56},{56,48},{64,72... | collective-permute-start | bytes 2359304 | tf_op jit(solution)/shard_map/ppermute | solution.py:277
  46.8 3.1 %shard_map.137 = (bf16[64,2048]{1,0:T(8,128)(2,1)S(1)}, bf16[2,64,2048]{2,1,0:T(8,128)(2,1)S(1)}, f32[64,512]{1,0:T(8,128)S(1)}) custom-call(s32[9,768]{1,0:T(8,128)S(1)} %get-tuple-element.48.in_ref, s32[9,768]{1,0:T(8,128)S(1)} %get-tuple-element.49.out_ref, f32[9,768]{1,0:T(8,128)S(1)} %get-tuple-element.50.valid_ref, ...), custom_call_target="tpu_custom_call" | custom-call | flops 12000000000 | bytes 36000000 | tf_op jit(solution)/shard_map/pallas_call | solution.py:250
  50.7 1.2 %collective-permute-start.12 = (bf16[64,2048]{1,0:T(8,128)(2,1)S(1)}, bf16[64,2048]{1,0:T(8,128)(2,1)S(1)}, u32[]{:S(2)}, u32[]{:S(2)}) collective-permute-start(bf16[64,2048]{1,0:T(8,128)(2,1)S(1)} %get-tuple-element.80), channel_id=1, source_target_pairs={{0,7},{1,2},{2,1},{3,4},{4,3},{5,6},{6,5},{7,0},{8,15},{9,10},{10,... | collective-permute-start | bytes 786440 | tf_op jit(solution)/shard_map/ppermute | solution.py:277
  51.9 3.0 %shard_map.139 = (bf16[2048,512]{1,0:T(8,128)(2,1)}, f32[8,128]{1,0:T(8,128)S(1)}) custom-call(bf16[64,2048]{1,0:T(8,128)(2,1)S(1)} %get-tuple-element.70.after_ref, bf16[2048,512]{1,0:T(8,128)(2,1)S(1)} %copy-done.1, bf16[512,256]{1,0:T(8,128)(2,1)S(1)} %get-tuple-element.71.trip_ref, bf16[64,512]{1,0:T(8,128)(2,1)S(1)} %copy-done.8), custom_call_target="tpu_custom_call" | custom-call | flops 2000000000 | bytes 6000000 | tf_op jit(solution)/shard_map/pallas_call | solution.py:262
  54.9 1.1 %collective-permute-done.10.refs_1_ = bf16[64,2048]{1,0:T(8,128)(2,1)S(1)} collective-permute-done((bf16[64,2048]{1,0:T(8,128)(2,1)S(1)}, bf16[64,2048]{1,0:T(8,128)(2,1)S(1)}, u32[]{:S(2)}, u32[]{:S(2)}) %collective-permute-start.10) | collective-permute-done | bytes 262176 | tf_op jit(solution)/shard_map/ppermute | solution.py:277
  57.6 6.1 %collective-permute-start.13 = (f32[96,512]{1,0:T(8,128)S(1)}, f32[96,512]{1,0:T(8,128)S(1)}, u32[]{:S(2)}, u32[]{:S(2)}) collective-permute-start(f32[96,512]{1,0:T(8,128)S(1)} %get-tuple-element.82), channel_id=1, source_target_pairs={{0,8},{8,0},{16,24},{24,16},{32,40},{40,32},{48,56},{56,48},{64,72... | collective-permute-start | bytes 589832 | tf_op jit(solution)/shard_map/ppermute | solution.py:277
  65.0 2.5 %collective-permute-start.14 = (bf16[96,512]{1,0:T(8,128)(2,1)S(1)}, bf16[96,512]{1,0:T(8,128)(2,1)S(1)}, u32[]{:S(2)}, u32[]{:S(2)}) collective-permute-start(bf16[96,512]{1,0:T(8,128)(2,1)S(1)} %add_convert_fusion.2), channel_id=1, source_target_pairs={{0,16},{1,17},{2,18},{3,19},{4,20},{5,21},{6,22},{7,23},{8,24},{9,... | collective-permute-start | bytes 294920 | tf_op jit(solution)/shard_map/ppermute | solution.py:319
  67.6 2.3 %collective-permute-done.16 = bf16[96,512]{1,0:T(8,128)(2,1)S(1)} collective-permute-done((bf16[96,512]{1,0:T(8,128)(2,1)S(1)}, bf16[96,512]{1,0:T(8,128)(2,1)S(1)}, u32[]{:S(2)}, u32[]{:S(2)}) %collective-permute-start.16) | collective-permute-done | bytes 98336 | tf_op jit(solution)/shard_map/ppermute | solution.py:319
  70.9 1.6 %collective-permute-start.19 = (bf16[96,512]{1,0:T(8,128)(2,1)S(1)}, bf16[96,512]{1,0:T(8,128)(2,1)S(1)}, u32[]{:S(2)}, u32[]{:S(2)}) collective-permute-start(bf16[96,512]{1,0:T(8,128)(2,1)S(1)} %add_convert_fusion.1), channel_id=1, source_target_pairs={{0,240},{1,241},{2,242},{3,243},{4,244},{5,245},{6,246},{7,247},{8... | collective-permute-start | bytes 294920 | tf_op jit(solution)/shard_map/ppermute | solution.py:319
  72.5 3.6 %collective-permute-start.17 = (bf16[96,512]{1,0:T(8,128)(2,1)S(1)}, bf16[96,512]{1,0:T(8,128)(2,1)S(1)}, u32[]{:S(2)}, u32[]{:S(2)}) collective-permute-start(bf16[96,512]{1,0:T(8,128)(2,1)S(1)} %add_convert_fusion.1), channel_id=1, source_target_pairs={{0,48},{1,49},{2,50},{3,51},{4,52},{5,53},{6,54},{7,55},{8,56},{9,... | collective-permute-start | bytes 294920 | tf_op jit(solution)/shard_map/ppermute | solution.py:319
  76.0 1.8 %collective-permute-done.19 = bf16[96,512]{1,0:T(8,128)(2,1)S(1)} collective-permute-done((bf16[96,512]{1,0:T(8,128)(2,1)S(1)}, bf16[96,512]{1,0:T(8,128)(2,1)S(1)}, u32[]{:S(2)}, u32[]{:S(2)}) %collective-permute-start.19) | collective-permute-done | bytes 98336 | tf_op jit(solution)/shard_map/ppermute | solution.py:319
  78.8 1.5 %collective-permute-start.22 = (bf16[96,512]{1,0:T(8,128)(2,1)S(1)}, bf16[96,512]{1,0:T(8,128)(2,1)S(1)}, u32[]{:S(2)}, u32[]{:S(2)}) collective-permute-start(bf16[96,512]{1,0:T(8,128)(2,1)S(1)} %get-tuple-element.89), channel_id=1, source_target_pairs={{0,2},{1,3},{2,0},{3,1},{4,6},{5,7},{6,4},{7,5},{8,10},{9,11},{10,... | collective-permute-start | bytes 294920 | tf_op jit(solution)/shard_map/ppermute | solution.py:319
  80.3 1.5 %collective-permute-start.21 = (bf16[96,512]{1,0:T(8,128)(2,1)S(1)}, bf16[96,512]{1,0:T(8,128)(2,1)S(1)}, u32[]{:S(2)}, u32[]{:S(2)}) collective-permute-start(bf16[96,512]{1,0:T(8,128)(2,1)S(1)} %get-tuple-element.89), channel_id=1, source_target_pairs={{0,3},{1,2},{2,1},{3,0},{4,7},{5,6},{6,5},{7,4},{8,11},{9,10},{10,... | collective-permute-start | bytes 294920 | tf_op jit(solution)/shard_map/ppermute | solution.py:319
  81.8 2.6 %shard_map.141 = (bf16[2048,512]{1,0:T(8,128)(2,1)}, f32[96,512]{1,0:T(8,128)S(1)}) custom-call(f32[96,512]{1,0:T(8,128)S(1)} %get-tuple-element.90.after_ref, bf16[2048,512]{1,0:T(8,128)(2,1)S(1)} %copy-done.7, bf16[64,2048]{1,0:T(8,128)(2,1)S(1)} %get-tuple-element.83.d_pre_ref, bf16[64,512]{1,0:T(8,128)(2,1)S(1)} %bitcast.18), custom_call_target="tpu_custom_call" | custom-call | flops 2000000000 | bytes 6000000 | tf_op jit(solution)/shard_map/pallas_call | solution.py:262
  84.4 1.9 %collective-permute-done.21 = bf16[96,512]{1,0:T(8,128)(2,1)S(1)} collective-permute-done((bf16[96,512]{1,0:T(8,128)(2,1)S(1)}, bf16[96,512]{1,0:T(8,128)(2,1)S(1)}, u32[]{:S(2)}, u32[]{:S(2)}) %collective-permute-start.21) | collective-permute-done | bytes 98336 | tf_op jit(solution)/shard_map/ppermute | solution.py:319
  86.5 2.0 %collective-permute-start.23 = (bf16[96,512]{1,0:T(8,128)(2,1)S(1)}, bf16[96,512]{1,0:T(8,128)(2,1)S(1)}, u32[]{:S(2)}, u32[]{:S(2)}) collective-permute-start(bf16[96,512]{1,0:T(8,128)(2,1)S(1)} %add_convert_fusion), channel_id=1, source_target_pairs={{0,7},{1,6},{2,5},{3,4},{4,3},{5,2},{6,1},{7,0},{8,15},{9,14},{10,... | collective-permute-start | bytes 294920 | tf_op jit(solution)/shard_map/ppermute | solution.py:319
  88.5 2.8 %collective-permute-done.23 = bf16[96,512]{1,0:T(8,128)(2,1)S(1)} collective-permute-done((bf16[96,512]{1,0:T(8,128)(2,1)S(1)}, bf16[96,512]{1,0:T(8,128)(2,1)S(1)}, u32[]{:S(2)}, u32[]{:S(2)}) %collective-permute-start.23) | collective-permute-done | bytes 98336 | tf_op jit(solution)/shard_map/ppermute | solution.py:319
  91.3 5.8 %collective-permute-start.24 = (f32[96,512]{1,0:T(8,128)S(1)}, f32[96,512]{1,0:T(8,128)S(1)}, u32[]{:S(2)}, u32[]{:S(2)}) collective-permute-start(f32[96,512]{1,0:T(8,128)S(1)} %convert_add_fusion.mine_ref), channel_id=1, source_target_pairs={{0,8},{8,0},{16,24},{24,16},{32,40},{40,32},{48,56},{56,48},{64,72... | collective-permute-start | bytes 589832 | tf_op jit(solution)/shard_map/ppermute | solution.py:277
  (66 shorter events, 11.2 us)
Async XLA Ops:
  3.1 7.4 %copy-start.3 = (s32[9,768]{1,0:T(8,128)S(1)}, s32[9,768]{1,0:T(8,128)}, u32[]{:S(2)}) copy-start(s32[9,768]{1,0:T(8,128)} %in_ref.1) | copy-start | bytes 82948
  3.1 7.4 %copy-start.4 = (s32[9,768]{1,0:T(8,128)S(1)}, s32[9,768]{1,0:T(8,128)}, u32[]{:S(2)}) copy-start(s32[9,768]{1,0:T(8,128)} %out_ref.1) | copy-start | bytes 82948
  3.1 7.4 %copy-start.5 = (f32[9,768]{1,0:T(8,128)S(1)}, f32[9,768]{1,0:T(8,128)}, u32[]{:S(2)}) copy-start(f32[9,768]{1,0:T(8,128)} %cos_ref.1) | copy-start | bytes 82948
  3.1 7.4 %copy-start.6 = (s32[9,12]{1,0:T(8,128)S(1)}, s32[9,12]{1,0:T(8,128)}, u32[]{:S(2)}) copy-start(s32[9,12]{1,0:T(8,128)} %counts_ref.1) | copy-start | bytes 1300
  3.1 8.9 %copy-start.2 = (bf16[512,64]{0,1:T(8,128)(2,1)S(1)}, bf16[512,64]{0,1:T(8,128)(2,1)}, u32[]{:S(2)}) copy-start(bf16[512,64]{0,1:T(8,128)(2,1)} %param.12) | copy-start | bytes 196612
  3.9 14.7 %collective-permute-start.1 = (bf16[64,2048]{1,0:T(8,128)(2,1)S(1)}, bf16[64,2048]{1,0:T(8,128)(2,1)S(1)}, u32[]{:S(2)}, u32[]{:S(2)}) collective-permute-start(bf16[64,2048]{1,0:T(8,128)(2,1)S(1)} %get-tuple-element.47.down_ref.refs_0_), channel_id=1, source_target_pairs={{0,7},{1,2},{2,1},{3,4},{4,3},{5,6},{6,5},{7,0},{8,15},{9,10},{10,... | collective-permute-start | bytes 786440 | tf_op jit(solution)/shard_map/ppermute | solution.py:277
  10.4 8.3 %collective-permute-start = (bf16[64,2048]{1,0:T(8,128)(2,1)S(1)}, bf16[64,2048]{1,0:T(8,128)(2,1)S(1)}, u32[]{:S(2)}, u32[]{:S(2)}) collective-permute-start(bf16[64,2048]{1,0:T(8,128)(2,1)S(1)} %get-tuple-element.47.down_ref.refs_0_), channel_id=1, source_target_pairs={{0,1},{1,0},{2,3},{3,2},{4,5},{5,4},{6,7},{7,6},{8,9},{9,8},{10,11... | collective-permute-start | bytes 786440 | tf_op jit(solution)/shard_map/ppermute | solution.py:277
  13.1 7.2 %collective-permute-start.3 = (bf16[64,2048]{1,0:T(8,128)(2,1)S(1)}, bf16[64,2048]{1,0:T(8,128)(2,1)S(1)}, u32[]{:S(2)}, u32[]{:S(2)}) collective-permute-start(bf16[64,2048]{1,0:T(8,128)(2,1)S(1)} %get-tuple-element.53), channel_id=1, source_target_pairs={{0,248},{8,16},{16,8},{24,32},{32,24},{40,48},{48,40},{56,64},{64,... | collective-permute-start | bytes 786440 | tf_op jit(solution)/shard_map/ppermute | solution.py:277
  15.3 7.1 %collective-permute-start.7 = (bf16[64,2048]{1,0:T(8,128)(2,1)S(1)}, bf16[64,2048]{1,0:T(8,128)(2,1)S(1)}, u32[]{:S(2)}, u32[]{:S(2)}) collective-permute-start(bf16[64,2048]{1,0:T(8,128)(2,1)S(1)} %get-tuple-element.53), channel_id=1, source_target_pairs={{0,8},{8,0},{16,24},{24,16},{32,40},{40,32},{48,56},{56,48},{64,72... | collective-permute-start | bytes 786440 | tf_op jit(solution)/shard_map/ppermute | solution.py:277
  18.6 5.9 %collective-permute-start.6 = (bf16[64,2048]{1,0:T(8,128)(2,1)S(1)}, bf16[64,2048]{1,0:T(8,128)(2,1)S(1)}, u32[]{:S(2)}, u32[]{:S(2)}) collective-permute-start(bf16[64,2048]{1,0:T(8,128)(2,1)S(1)} %collective-permute-done.1.refs_1_), channel_id=1, source_target_pairs={{0,8},{8,0},{16,24},{24,16},{32,40},{40,32},{48,56},{56,48},{64,72... | collective-permute-start | bytes 786440 | tf_op jit(solution)/shard_map/ppermute | solution.py:277
  18.7 5.8 %collective-permute-start.5 = (bf16[64,2048]{1,0:T(8,128)(2,1)S(1)}, bf16[64,2048]{1,0:T(8,128)(2,1)S(1)}, u32[]{:S(2)}, u32[]{:S(2)}) collective-permute-start(bf16[64,2048]{1,0:T(8,128)(2,1)S(1)} %collective-permute-done.refs_0_), channel_id=1, source_target_pairs={{0,8},{8,0},{16,24},{24,16},{32,40},{40,32},{48,56},{56,48},{64,72... | collective-permute-start | bytes 786440 | tf_op jit(solution)/shard_map/ppermute | solution.py:277
  19.2 8.5 %collective-permute-start.2 = (bf16[96,2048]{1,0:T(8,128)(2,1)S(1)}, bf16[96,2048]{1,0:T(8,128)(2,1)S(1)}, u32[]{:S(2)}, u32[]{:S(2)}) collective-permute-start(bf16[96,2048]{1,0:T(8,128)(2,1)S(1)} %pad_maximum_fusion), channel_id=1, source_target_pairs={{0,248},{8,16},{16,8},{24,32},{32,24},{40,48},{48,40},{56,64},{64,... | collective-permute-start | bytes 1179656 | tf_op jit(solution)/shard_map/ppermute | solution.py:277
  20.3 7.3 %collective-permute-start.4 = (bf16[32,2048]{1,0:T(8,128)(2,1)S(1)}, bf16[32,2048]{1,0:T(8,128)(2,1)S(1)}, u32[]{:S(2)}, u32[]{:S(2)}) collective-permute-start(bf16[32,2048]{1,0:T(8,128)(2,1)S(1)} %slice.41), channel_id=1, source_target_pairs={{0,7},{1,2},{2,1},{3,4},{4,3},{5,6},{6,5},{7,0},{8,15},{9,10},{10,... | collective-permute-start | bytes 393224 | tf_op jit(solution)/shard_map/ppermute | solution.py:277
  27.6 2.2 %copy-start.7 = (bf16[2048,512]{1,0:T(8,128)(2,1)S(1)}, bf16[2048,512]{1,0:T(8,128)(2,1)}, u32[]{:S(2)}) copy-start(bf16[2048,512]{1,0:T(8,128)(2,1)} %cot_ref.3) | copy-start | bytes 6291460
  35.0 14.9 %collective-permute-start.8 = (bf16[2,64,2048]{2,1,0:T(8,128)(2,1)S(1)}, bf16[2,64,2048]{2,1,0:T(8,128)(2,1)S(1)}, u32[]{:S(2)}, u32[]{:S(2)}) collective-permute-start(bf16[2,64,2048]{2,1,0:T(8,128)(2,1)S(1)} %get-tuple-element.67), channel_id=1, source_target_pairs={{0,248},{8,16},{16,8},{24,32},{32,24},{40,48},{48,40},{56,64},{64,... | collective-permute-start | bytes 1572872 | tf_op jit(solution)/shard_map/ppermute | solution.py:277
  40.4 9.4 %collective-permute-start.9 = (bf16[3,64,2048]{2,1,0:T(8,128)(2,1)S(1)}, bf16[3,64,2048]{2,1,0:T(8,128)(2,1)S(1)}, u32[]{:S(2)}, u32[]{:S(2)}) collective-permute-start(bf16[3,64,2048]{2,1,0:T(8,128)(2,1)S(1)} %get-tuple-element.68), channel_id=1, source_target_pairs={{0,8},{8,0},{16,24},{24,16},{32,40},{40,32},{48,56},{56,48},{64,72... | collective-permute-start | bytes 2359304 | tf_op jit(solution)/shard_map/ppermute | solution.py:277
  50.2 5.9 %collective-permute-start.10 = (bf16[64,2048]{1,0:T(8,128)(2,1)S(1)}, bf16[64,2048]{1,0:T(8,128)(2,1)S(1)}, u32[]{:S(2)}, u32[]{:S(2)}) collective-permute-start(bf16[64,2048]{1,0:T(8,128)(2,1)S(1)} %get-tuple-element.79), channel_id=1, source_target_pairs={{0,248},{8,16},{16,8},{24,32},{32,24},{40,48},{48,40},{56,64},{64,... | collective-permute-start | bytes 786440 | tf_op jit(solution)/shard_map/ppermute | solution.py:277
  50.3 5.8 %collective-permute-start.11 = (bf16[64,2048]{1,0:T(8,128)(2,1)S(1)}, bf16[64,2048]{1,0:T(8,128)(2,1)S(1)}, u32[]{:S(2)}, u32[]{:S(2)}) collective-permute-start(bf16[64,2048]{1,0:T(8,128)(2,1)S(1)} %get-tuple-element.70.after_ref), channel_id=1, source_target_pairs={{0,1},{1,0},{2,3},{3,2},{4,5},{5,4},{6,7},{7,6},{8,9},{9,8},{10,11... | collective-permute-start | bytes 786440 | tf_op jit(solution)/shard_map/ppermute | solution.py:277
  50.7 6.4 %collective-permute-start.12 = (bf16[64,2048]{1,0:T(8,128)(2,1)S(1)}, bf16[64,2048]{1,0:T(8,128)(2,1)S(1)}, u32[]{:S(2)}, u32[]{:S(2)}) collective-permute-start(bf16[64,2048]{1,0:T(8,128)(2,1)S(1)} %get-tuple-element.80), channel_id=1, source_target_pairs={{0,7},{1,2},{2,1},{3,4},{4,3},{5,6},{6,5},{7,0},{8,15},{9,10},{10,... | collective-permute-start | bytes 786440 | tf_op jit(solution)/shard_map/ppermute | solution.py:277
  57.1 24.7 %copy-start.10 = (bf16[512,64]{0,1:T(8,128)(2,1)S(1)}, bf16[512,64]{0,1:T(8,128)(2,1)}, u32[]{:S(2)}) copy-start(bf16[512,64]{0,1:T(8,128)(2,1)} %param.11) | copy-start | bytes 196612
  57.6 7.2 %collective-permute-start.13 = (f32[96,512]{1,0:T(8,128)S(1)}, f32[96,512]{1,0:T(8,128)S(1)}, u32[]{:S(2)}, u32[]{:S(2)}) collective-permute-start(f32[96,512]{1,0:T(8,128)S(1)} %get-tuple-element.82), channel_id=1, source_target_pairs={{0,8},{8,0},{16,24},{24,16},{32,40},{40,32},{48,56},{56,48},{64,72... | collective-permute-start | bytes 589832 | tf_op jit(solution)/shard_map/ppermute | solution.py:277
  64.8 5.0 %collective-permute-start.16 = (bf16[96,512]{1,0:T(8,128)(2,1)S(1)}, bf16[96,512]{1,0:T(8,128)(2,1)S(1)}, u32[]{:S(2)}, u32[]{:S(2)}) collective-permute-start(bf16[96,512]{1,0:T(8,128)(2,1)S(1)} %add_convert_fusion.2), channel_id=1, source_target_pairs={{0,80},{1,81},{2,82},{3,83},{4,84},{5,85},{6,86},{7,87},{8,88},{9,... | collective-permute-start | bytes 294920 | tf_op jit(solution)/shard_map/ppermute | solution.py:319
  64.9 5.9 %collective-permute-start.15 = (bf16[96,512]{1,0:T(8,128)(2,1)S(1)}, bf16[96,512]{1,0:T(8,128)(2,1)S(1)}, u32[]{:S(2)}, u32[]{:S(2)}) collective-permute-start(bf16[96,512]{1,0:T(8,128)(2,1)S(1)} %add_convert_fusion.2), channel_id=1, source_target_pairs={{0,64},{1,65},{2,66},{3,67},{4,68},{5,69},{6,70},{7,71},{8,72},{9,... | collective-permute-start | bytes 294920 | tf_op jit(solution)/shard_map/ppermute | solution.py:319
  65.0 5.8 %collective-permute-start.14 = (bf16[96,512]{1,0:T(8,128)(2,1)S(1)}, bf16[96,512]{1,0:T(8,128)(2,1)S(1)}, u32[]{:S(2)}, u32[]{:S(2)}) collective-permute-start(bf16[96,512]{1,0:T(8,128)(2,1)S(1)} %add_convert_fusion.2), channel_id=1, source_target_pairs={{0,16},{1,17},{2,18},{3,19},{4,20},{5,21},{6,22},{7,23},{8,24},{9,... | collective-permute-start | bytes 294920 | tf_op jit(solution)/shard_map/ppermute | solution.py:319
  70.9 7.0 %collective-permute-start.19 = (bf16[96,512]{1,0:T(8,128)(2,1)S(1)}, bf16[96,512]{1,0:T(8,128)(2,1)S(1)}, u32[]{:S(2)}, u32[]{:S(2)}) collective-permute-start(bf16[96,512]{1,0:T(8,128)(2,1)S(1)} %add_convert_fusion.1), channel_id=1, source_target_pairs={{0,240},{1,241},{2,242},{3,243},{4,244},{5,245},{6,246},{7,247},{8... | collective-permute-start | bytes 294920 | tf_op jit(solution)/shard_map/ppermute | solution.py:319
  72.5 6.3 %collective-permute-start.18 = (bf16[96,512]{1,0:T(8,128)(2,1)S(1)}, bf16[96,512]{1,0:T(8,128)(2,1)S(1)}, u32[]{:S(2)}, u32[]{:S(2)}) collective-permute-start(bf16[96,512]{1,0:T(8,128)(2,1)S(1)} %add_convert_fusion.1), channel_id=1, source_target_pairs={{0,192},{1,193},{2,194},{3,195},{4,196},{5,197},{6,198},{7,199},{8... | collective-permute-start | bytes 294920 | tf_op jit(solution)/shard_map/ppermute | solution.py:319
  72.5 6.3 %collective-permute-start.17 = (bf16[96,512]{1,0:T(8,128)(2,1)S(1)}, bf16[96,512]{1,0:T(8,128)(2,1)S(1)}, u32[]{:S(2)}, u32[]{:S(2)}) collective-permute-start(bf16[96,512]{1,0:T(8,128)(2,1)S(1)} %add_convert_fusion.1), channel_id=1, source_target_pairs={{0,48},{1,49},{2,50},{3,51},{4,52},{5,53},{6,54},{7,55},{8,56},{9,... | collective-permute-start | bytes 294920 | tf_op jit(solution)/shard_map/ppermute | solution.py:319
  78.8 5.6 %collective-permute-start.22 = (bf16[96,512]{1,0:T(8,128)(2,1)S(1)}, bf16[96,512]{1,0:T(8,128)(2,1)S(1)}, u32[]{:S(2)}, u32[]{:S(2)}) collective-permute-start(bf16[96,512]{1,0:T(8,128)(2,1)S(1)} %get-tuple-element.89), channel_id=1, source_target_pairs={{0,2},{1,3},{2,0},{3,1},{4,6},{5,7},{6,4},{7,5},{8,10},{9,11},{10,... | collective-permute-start | bytes 294920 | tf_op jit(solution)/shard_map/ppermute | solution.py:319
  80.3 6.0 %collective-permute-start.21 = (bf16[96,512]{1,0:T(8,128)(2,1)S(1)}, bf16[96,512]{1,0:T(8,128)(2,1)S(1)}, u32[]{:S(2)}, u32[]{:S(2)}) collective-permute-start(bf16[96,512]{1,0:T(8,128)(2,1)S(1)} %get-tuple-element.89), channel_id=1, source_target_pairs={{0,3},{1,2},{2,1},{3,0},{4,7},{5,6},{6,5},{7,4},{8,11},{9,10},{10,... | collective-permute-start | bytes 294920 | tf_op jit(solution)/shard_map/ppermute | solution.py:319
  81.8 4.6 %collective-permute-start.20 = (bf16[96,512]{1,0:T(8,128)(2,1)S(1)}, bf16[96,512]{1,0:T(8,128)(2,1)S(1)}, u32[]{:S(2)}, u32[]{:S(2)}) collective-permute-start(bf16[96,512]{1,0:T(8,128)(2,1)S(1)} %get-tuple-element.89), channel_id=1, source_target_pairs={{0,1},{1,0},{2,3},{3,2},{4,5},{5,4},{6,7},{7,6},{8,9},{9,8},{10,11... | collective-permute-start | bytes 294920 | tf_op jit(solution)/shard_map/ppermute | solution.py:319
  86.5 4.8 %collective-permute-start.23 = (bf16[96,512]{1,0:T(8,128)(2,1)S(1)}, bf16[96,512]{1,0:T(8,128)(2,1)S(1)}, u32[]{:S(2)}, u32[]{:S(2)}) collective-permute-start(bf16[96,512]{1,0:T(8,128)(2,1)S(1)} %add_convert_fusion), channel_id=1, source_target_pairs={{0,7},{1,6},{2,5},{3,4},{4,3},{5,2},{6,1},{7,0},{8,15},{9,14},{10,... | collective-permute-start | bytes 294920 | tf_op jit(solution)/shard_map/ppermute | solution.py:319
  91.3 6.9 %collective-permute-start.24 = (f32[96,512]{1,0:T(8,128)S(1)}, f32[96,512]{1,0:T(8,128)S(1)}, u32[]{:S(2)}, u32[]{:S(2)}) collective-permute-start(f32[96,512]{1,0:T(8,128)S(1)} %convert_add_fusion.mine_ref), channel_id=1, source_target_pairs={{0,8},{8,0},{16,24},{24,16},{32,40},{40,32},{48,56},{56,48},{64,72... | collective-permute-start | bytes 589832 | tf_op jit(solution)/shard_map/ppermute | solution.py:277
  (4 other events, 6.6 us)

commit v5 on v4

--- a/solution.py
+++ b/solution.py
@@ -367,7 +367,7 @@
     source = {0: down, 1: near(down, "gy"), 2: far(down, "gy")}
     feats = {}
     trip = w_rows = None
-    for places in ((0,), (3, 4), (1, 2, 5, 6), (7, 8)):
+    for places in ((0,), (3, 4, 1, 2, 5, 6), (7, 8)):
         n = len(places)
         base = trip is not None
         split = places == (7, 8)

time: 99.1 us -> 100 us (level)
  waiting for transfers between devices: 15.2 us -> 16.7 us
    ppermute x10, waiting for transfers between devices: 10.8 us -> 12.3 us  [sum_step(): got.append(lax.ppermute(x, BOTH, pairs).astype(F32))]
    ppermute x15, starting transfers between devices: 37.1 us -> 38.3 us  [swap(): lax.ppermute(x, axis, [(i, partner(i)) for i in range(lax.axis_size(axis))])]
    pallas_call x13 -> x12, Pallas kernels: 24.4 us -> 23.8 us  [call(): pl.pallas_call(kernel, out_shape=outs, in_specs=specs if after is None el...]
  transfers between devices with their start and end apart: 25 -> 25, of which waited for: 11 -> 11; matrix products, arithmetic and copies ran while one was open for 0% -> 0% of each run, Pallas kernels for 21% -> 20%
where the time goes in v5:
time: 100 us
  starting transfers between devices  50.4 us (50%)
  Pallas kernels  29.4 us (29%)
  waiting for transfers between devices  16.7 us (17%)
  local copies, waits for them, and re-layouts  2.63 us (3%)
    ppermute x15, starting transfers between devices, swap(): lax.ppermute(x, axis, [(i, partner(i)) for i in range(lax.axis_size(axis))])  38.3 us
    pallas_call x12, Pallas kernels, call(): pl.pallas_call(kernel, out_shape=outs, in_specs=specs if after is None el...  23.8 us
    ppermute x10, waiting for transfers between devices, sum_step(): got.append(lax.ppermute(x, BOTH, pairs).astype(F32))  12.3 us
    ppermute x10, starting transfers between devices, sum_step(): got.append(lax.ppermute(x, BOTH, pairs).astype(F32))  12.2 us
    pallas_call x2, Pallas kernels, tiled(): pl.pallas_call(kernel, grid=(steps,), out_shape=(out, jax.ShapeDtypeStruc...  5.6 us
    ppermute x15, waiting for transfers between devices, swap(): lax.ppermute(x, axis, [(i, partner(i)) for i in range(lax.axis_size(axis))])  4.43 us
    unnamed x22, local copies, waits for them, and re-layouts  2.47 us
  transfers between devices with their start and end apart: 25, of which 11 were waited for; matrix products, arithmetic and copies ran while one was open for 0% of the time, Pallas kernels for 20%

profile of v5, /device:TPU:1, one launch (start us, length us, event | category | flops | bytes accessed | tf_op | source)
XLA Modules:
  0.0 100.3 jit_solution(1672694367780504394)
XLA Ops:
  0.6 1.6 %copy-done = bf16[2048,512]{1,0:T(8,128)(2,1)S(1)} copy-done((bf16[2048,512]{1,0:T(8,128)(2,1)S(1)}, bf16[2048,512]{1,0:T(8,128)(2,1)}, u32[]{:S(2)}) %copy-start) | copy-done | bytes 2097176
  3.9 6.5 %collective-permute-start.1 = (bf16[64,2048]{1,0:T(8,128)(2,1)S(1)}, bf16[64,2048]{1,0:T(8,128)(2,1)S(1)}, u32[]{:S(2)}, u32[]{:S(2)}) collective-permute-start(bf16[64,2048]{1,0:T(8,128)(2,1)S(1)} %get-tuple-element.45.down_ref.refs_0_), channel_id=1, source_target_pairs={{0,7},{1,2},{2,1},{3,4},{4,3},{5,6},{6,5},{7,0},{8,15},{9,10},{10,... | collective-permute-start | bytes 786440 | tf_op jit(solution)/shard_map/ppermute | solution.py:277
  10.5 1.5 %shard_map.129 = (s32[9,768]{1,0:T(8,128)S(1)}, s32[9,768]{1,0:T(8,128)S(1)}, f32[9,768]{1,0:T(8,128)S(1)}, f32[8,9,768]{2,1,0:T(8,128)S(1)}, s32[8,512]{1,0:T(8,128)S(1)}, /*index=5*/bf16[64,2048]{1,0:T(8,128)(2,1)}) custom-call(s32[10]{0:T(128)S(1)} %stack.39.ks_ref, s32[9,12]{1,0:T(8,128)S(1)} %copy-done.6, s32[9,768]{1,0:T(8,128)S(1)} %copy-done.3, ...), custom_call_target="tpu_custom_call" | custom-call | flops 100000000 | bytes 300000 | tf_op jit(solution)/shard_map/pallas_call | solution.py:250
  12.0 1.2 %shard_map.130 = (f32[512,256]{1,0:T(8,128)S(1)}, bf16[64,768]{1,0:T(8,128)(2,1)S(1)}, bf16[64,512]{1,0:T(8,128)(2,1)S(1)}, bf16[64,2048]{1,0:T(8,128)(2,1)S(1)}) custom-call(s32[9,768]{1,0:T(8,128)S(1)} %get-tuple-element.46.in_ref, s32[9,768]{1,0:T(8,128)S(1)} %get-tuple-element.47.out_ref, f32[9,768]{1,0:T(8,128)S(1)} %get-tuple-element.48.valid_ref, ...), custom_call_target="tpu_custom_call" | custom-call | flops 40000000 | bytes 120000 | tf_op jit(solution)/shard_map/pallas_call | solution.py:250
  13.1 2.1 %collective-permute-start.3 = (bf16[64,2048]{1,0:T(8,128)(2,1)S(1)}, bf16[64,2048]{1,0:T(8,128)(2,1)S(1)}, u32[]{:S(2)}, u32[]{:S(2)}) collective-permute-start(bf16[64,2048]{1,0:T(8,128)(2,1)S(1)} %get-tuple-element.51), channel_id=1, source_target_pairs={{0,248},{8,16},{16,8},{24,32},{32,24},{40,48},{48,40},{56,64},{64,... | collective-permute-start | bytes 786440 | tf_op jit(solution)/shard_map/ppermute | solution.py:277
  15.3 3.3 %collective-permute-start.5 = (bf16[64,2048]{1,0:T(8,128)(2,1)S(1)}, bf16[64,2048]{1,0:T(8,128)(2,1)S(1)}, u32[]{:S(2)}, u32[]{:S(2)}) collective-permute-start(bf16[64,2048]{1,0:T(8,128)(2,1)S(1)} %get-tuple-element.51), channel_id=1, source_target_pairs={{0,8},{8,0},{16,24},{24,16},{32,40},{40,32},{48,56},{56,48},{64,72... | collective-permute-start | bytes 786440 | tf_op jit(solution)/shard_map/ppermute | solution.py:277
  20.3 2.1 %collective-permute-start.4 = (bf16[32,2048]{1,0:T(8,128)(2,1)S(1)}, bf16[32,2048]{1,0:T(8,128)(2,1)S(1)}, u32[]{:S(2)}, u32[]{:S(2)}) collective-permute-start(bf16[32,2048]{1,0:T(8,128)(2,1)S(1)} %slice.41), channel_id=1, source_target_pairs={{0,7},{1,2},{2,1},{3,4},{4,3},{5,6},{6,5},{7,0},{8,15},{9,10},{10,... | collective-permute-start | bytes 393224 | tf_op jit(solution)/shard_map/ppermute | solution.py:277
  22.4 4.4 %shard_map.131 = (f32[512,256]{1,0:T(8,128)S(1)}, bf16[384,768]{1,0:T(8,128)(2,1)S(1)}) custom-call(s32[9,768]{1,0:T(8,128)S(1)} %get-tuple-element.46.in_ref, s32[9,768]{1,0:T(8,128)S(1)} %get-tuple-element.47.out_ref, f32[9,768]{1,0:T(8,128)S(1)} %get-tuple-element.48.valid_ref, f32[8,9,768]{2,1,0:T(8,128)S(1)} %get-tuple-element.49.basis_ref, ...), custom_call_target="tpu_custom_call" | custom-call | flops 240000000 | bytes 720000 | tf_op jit(solution)/shard_map/pallas_call | solution.py:250
  27.0 2.1 %shard_map.132 = (f32[512,256]{1,0:T(8,128)S(1)}, bf16[128,768]{1,0:T(8,128)(2,1)S(1)}) custom-call(s32[9,768]{1,0:T(8,128)S(1)} %get-tuple-element.46.in_ref, s32[9,768]{1,0:T(8,128)S(1)} %get-tuple-element.47.out_ref, f32[9,768]{1,0:T(8,128)S(1)} %get-tuple-element.48.valid_ref, f32[8,9,768]{2,1,0:T(8,128)S(1)} %get-tuple-element.49.basis_ref, ...), custom_call_target="tpu_custom_call" | custom-call | flops 80000000 | bytes 240000 | tf_op jit(solution)/shard_map/pallas_call | solution.py:250
  29.1 3.0 %shard_map.133 = (bf16[64,2048]{1,0:T(8,128)(2,1)S(1)}, f32[64,512]{1,0:T(8,128)S(1)}, bf16[512,256]{1,0:T(8,128)(2,1)S(1)}) custom-call(bf16[2048,512]{1,0:T(8,128)(2,1)S(1)} %copy-done.7, f32[512,256]{1,0:T(8,128)S(1)} %get-tuple-element.54.trip_ref, bf16[64,512]{1,0:T(8,128)(2,1)S(1)} %copy-done.8), custom_call_target="tpu_custom_call" | custom-call | flops 2000000000 | bytes 6000000 | tf_op jit(solution)/shard_map/pallas_call | solution.py:250
  32.1 2.2 %shard_map.134 = (bf16[2,64,2048]{2,1,0:T(8,128)(2,1)S(1)}, f32[64,512]{1,0:T(8,128)S(1)}) custom-call(s32[9,768]{1,0:T(8,128)S(1)} %get-tuple-element.46.in_ref, s32[9,768]{1,0:T(8,128)S(1)} %get-tuple-element.47.out_ref, f32[9,768]{1,0:T(8,128)S(1)} %get-tuple-element.48.valid_ref, f32[8,9,768]{2,1,0:T(8,128)S(1)} %get-tuple-element.49.basis_ref, ...), custom_call_target="tpu_custom_call" | custom-call | flops 8000000000 | bytes 24000000 | tf_op jit(solution)/shard_map/pallas_call | solution.py:250
  34.3 2.2 %collective-permute-start.8 = (bf16[2,64,2048]{2,1,0:T(8,128)(2,1)S(1)}, bf16[2,64,2048]{2,1,0:T(8,128)(2,1)S(1)}, u32[]{:S(2)}, u32[]{:S(2)}) collective-permute-start(bf16[2,64,2048]{2,1,0:T(8,128)(2,1)S(1)} %get-tuple-element.63), channel_id=1, source_target_pairs={{0,248},{8,16},{16,8},{24,32},{32,24},{40,48},{48,40},{56,64},{64,... | collective-permute-start | bytes 1572872 | tf_op jit(solution)/shard_map/ppermute | solution.py:277
  36.4 4.0 %shard_map.135 = (bf16[64,2048]{1,0:T(8,128)(2,1)S(1)}, bf16[3,64,2048]{2,1,0:T(8,128)(2,1)S(1)}, f32[64,512]{1,0:T(8,128)S(1)}) custom-call(s32[9,768]{1,0:T(8,128)S(1)} %get-tuple-element.46.in_ref, s32[9,768]{1,0:T(8,128)S(1)} %get-tuple-element.47.out_ref, f32[9,768]{1,0:T(8,128)S(1)} %get-tuple-element.48.valid_ref, ...), custom_call_target="tpu_custom_call" | custom-call | flops 16000000000 | bytes 48000000 | tf_op jit(solution)/shard_map/pallas_call | solution.py:250
  40.5 6.3 %collective-permute-start.9 = (bf16[3,64,2048]{2,1,0:T(8,128)(2,1)S(1)}, bf16[3,64,2048]{2,1,0:T(8,128)(2,1)S(1)}, u32[]{:S(2)}, u32[]{:S(2)}) collective-permute-start(bf16[3,64,2048]{2,1,0:T(8,128)(2,1)S(1)} %get-tuple-element.64), channel_id=1, source_target_pairs={{0,8},{8,0},{16,24},{24,16},{32,40},{40,32},{48,56},{56,48},{64,72... | collective-permute-start | bytes 2359304 | tf_op jit(solution)/shard_map/ppermute | solution.py:277
  46.8 3.1 %shard_map.136 = (bf16[64,2048]{1,0:T(8,128)(2,1)S(1)}, bf16[2,64,2048]{2,1,0:T(8,128)(2,1)S(1)}, f32[64,512]{1,0:T(8,128)S(1)}) custom-call(s32[9,768]{1,0:T(8,128)S(1)} %get-tuple-element.46.in_ref, s32[9,768]{1,0:T(8,128)S(1)} %get-tuple-element.47.out_ref, f32[9,768]{1,0:T(8,128)S(1)} %get-tuple-element.48.valid_ref, ...), custom_call_target="tpu_custom_call" | custom-call | flops 12000000000 | bytes 36000000 | tf_op jit(solution)/shard_map/pallas_call | solution.py:250
  50.4 1.5 %collective-permute-start.12 = (bf16[64,2048]{1,0:T(8,128)(2,1)S(1)}, bf16[64,2048]{1,0:T(8,128)(2,1)S(1)}, u32[]{:S(2)}, u32[]{:S(2)}) collective-permute-start(bf16[64,2048]{1,0:T(8,128)(2,1)S(1)} %get-tuple-element.76), channel_id=1, source_target_pairs={{0,7},{1,2},{2,1},{3,4},{4,3},{5,6},{6,5},{7,0},{8,15},{9,10},{10,... | collective-permute-start | bytes 786440 | tf_op jit(solution)/shard_map/ppermute | solution.py:277
  51.9 3.0 %shard_map.138 = (bf16[2048,512]{1,0:T(8,128)(2,1)}, f32[8,128]{1,0:T(8,128)S(1)}) custom-call(bf16[64,2048]{1,0:T(8,128)(2,1)S(1)} %get-tuple-element.66.after_ref, bf16[2048,512]{1,0:T(8,128)(2,1)S(1)} %copy-done.1, bf16[512,256]{1,0:T(8,128)(2,1)S(1)} %get-tuple-element.67.trip_ref, bf16[64,512]{1,0:T(8,128)(2,1)S(1)} %copy-done.8), custom_call_target="tpu_custom_call" | custom-call | flops 2000000000 | bytes 6000000 | tf_op jit(solution)/shard_map/pallas_call | solution.py:262
  54.9 1.1 %collective-permute-done.10.refs_1_ = bf16[64,2048]{1,0:T(8,128)(2,1)S(1)} collective-permute-done((bf16[64,2048]{1,0:T(8,128)(2,1)S(1)}, bf16[64,2048]{1,0:T(8,128)(2,1)S(1)}, u32[]{:S(2)}, u32[]{:S(2)}) %collective-permute-start.10) | collective-permute-done | bytes 262176 | tf_op jit(solution)/shard_map/ppermute | solution.py:277
  56.1 1.1 %collective-permute-done.12.refs_3_ = bf16[64,2048]{1,0:T(8,128)(2,1)S(1)} collective-permute-done((bf16[64,2048]{1,0:T(8,128)(2,1)S(1)}, bf16[64,2048]{1,0:T(8,128)(2,1)S(1)}, u32[]{:S(2)}, u32[]{:S(2)}) %collective-permute-start.12) | collective-permute-done | bytes 262176 | tf_op jit(solution)/shard_map/ppermute | solution.py:277
  57.7 5.7 %collective-permute-start.13 = (f32[96,512]{1,0:T(8,128)S(1)}, f32[96,512]{1,0:T(8,128)S(1)}, u32[]{:S(2)}, u32[]{:S(2)}) collective-permute-start(f32[96,512]{1,0:T(8,128)S(1)} %get-tuple-element.78), channel_id=1, source_target_pairs={{0,8},{8,0},{16,24},{24,16},{32,40},{40,32},{48,56},{56,48},{64,72... | collective-permute-start | bytes 589832 | tf_op jit(solution)/shard_map/ppermute | solution.py:277
  64.7 2.5 %collective-permute-start.14 = (bf16[96,512]{1,0:T(8,128)(2,1)S(1)}, bf16[96,512]{1,0:T(8,128)(2,1)S(1)}, u32[]{:S(2)}, u32[]{:S(2)}) collective-permute-start(bf16[96,512]{1,0:T(8,128)(2,1)S(1)} %add_convert_fusion.2), channel_id=1, source_target_pairs={{0,16},{1,17},{2,18},{3,19},{4,20},{5,21},{6,22},{7,23},{8,24},{9,... | collective-permute-start | bytes 294920 | tf_op jit(solution)/shard_map/ppermute | solution.py:319
  67.3 2.3 %collective-permute-done.16 = bf16[96,512]{1,0:T(8,128)(2,1)S(1)} collective-permute-done((bf16[96,512]{1,0:T(8,128)(2,1)S(1)}, bf16[96,512]{1,0:T(8,128)(2,1)S(1)}, u32[]{:S(2)}, u32[]{:S(2)}) %collective-permute-start.16) | collective-permute-done | bytes 98336 | tf_op jit(solution)/shard_map/ppermute | solution.py:319
  70.6 1.9 %collective-permute-start.19 = (bf16[96,512]{1,0:T(8,128)(2,1)S(1)}, bf16[96,512]{1,0:T(8,128)(2,1)S(1)}, u32[]{:S(2)}, u32[]{:S(2)}) collective-permute-start(bf16[96,512]{1,0:T(8,128)(2,1)S(1)} %add_convert_fusion.1), channel_id=1, source_target_pairs={{0,240},{1,241},{2,242},{3,243},{4,244},{5,245},{6,246},{7,247},{8... | collective-permute-start | bytes 294920 | tf_op jit(solution)/shard_map/ppermute | solution.py:319
  72.5 3.2 %collective-permute-start.17 = (bf16[96,512]{1,0:T(8,128)(2,1)S(1)}, bf16[96,512]{1,0:T(8,128)(2,1)S(1)}, u32[]{:S(2)}, u32[]{:S(2)}) collective-permute-start(bf16[96,512]{1,0:T(8,128)(2,1)S(1)} %add_convert_fusion.1), channel_id=1, source_target_pairs={{0,48},{1,49},{2,50},{3,51},{4,52},{5,53},{6,54},{7,55},{8,56},{9,... | collective-permute-start | bytes 294920 | tf_op jit(solution)/shard_map/ppermute | solution.py:319
  75.7 1.8 %collective-permute-done.19 = bf16[96,512]{1,0:T(8,128)(2,1)S(1)} collective-permute-done((bf16[96,512]{1,0:T(8,128)(2,1)S(1)}, bf16[96,512]{1,0:T(8,128)(2,1)S(1)}, u32[]{:S(2)}, u32[]{:S(2)}) %collective-permute-start.19) | collective-permute-done | bytes 98336 | tf_op jit(solution)/shard_map/ppermute | solution.py:319
  77.5 1.6 %collective-permute-done.18 = bf16[96,512]{1,0:T(8,128)(2,1)S(1)} collective-permute-done((bf16[96,512]{1,0:T(8,128)(2,1)S(1)}, bf16[96,512]{1,0:T(8,128)(2,1)S(1)}, u32[]{:S(2)}, u32[]{:S(2)}) %collective-permute-start.18) | collective-permute-done | bytes 98336 | tf_op jit(solution)/shard_map/ppermute | solution.py:319
  79.4 1.6 %collective-permute-start.21 = (bf16[96,512]{1,0:T(8,128)(2,1)S(1)}, bf16[96,512]{1,0:T(8,128)(2,1)S(1)}, u32[]{:S(2)}, u32[]{:S(2)}) collective-permute-start(bf16[96,512]{1,0:T(8,128)(2,1)S(1)} %get-tuple-element.85), channel_id=1, source_target_pairs={{0,3},{1,2},{2,1},{3,0},{4,7},{5,6},{6,5},{7,4},{8,11},{9,10},{10,... | collective-permute-start | bytes 294920 | tf_op jit(solution)/shard_map/ppermute | solution.py:319
  81.9 2.6 %shard_map.140 = (bf16[2048,512]{1,0:T(8,128)(2,1)}, f32[96,512]{1,0:T(8,128)S(1)}) custom-call(f32[96,512]{1,0:T(8,128)S(1)} %get-tuple-element.86.after_ref, bf16[2048,512]{1,0:T(8,128)(2,1)S(1)} %copy-done.7, bf16[64,2048]{1,0:T(8,128)(2,1)S(1)} %get-tuple-element.79.d_pre_ref, bf16[64,512]{1,0:T(8,128)(2,1)S(1)} %bitcast.17), custom_call_target="tpu_custom_call" | custom-call | flops 2000000000 | bytes 6000000 | tf_op jit(solution)/shard_map/pallas_call | solution.py:262
  84.5 1.5 %collective-permute-done.22 = bf16[96,512]{1,0:T(8,128)(2,1)S(1)} collective-permute-done((bf16[96,512]{1,0:T(8,128)(2,1)S(1)}, bf16[96,512]{1,0:T(8,128)(2,1)S(1)}, u32[]{:S(2)}, u32[]{:S(2)}) %collective-permute-start.22) | collective-permute-done | bytes 98336 | tf_op jit(solution)/shard_map/ppermute | solution.py:319
  87.0 1.5 %collective-permute-start.23 = (bf16[96,512]{1,0:T(8,128)(2,1)S(1)}, bf16[96,512]{1,0:T(8,128)(2,1)S(1)}, u32[]{:S(2)}, u32[]{:S(2)}) collective-permute-start(bf16[96,512]{1,0:T(8,128)(2,1)S(1)} %add_convert_fusion), channel_id=1, source_target_pairs={{0,7},{1,6},{2,5},{3,4},{4,3},{5,2},{6,1},{7,0},{8,15},{9,14},{10,... | collective-permute-start | bytes 294920 | tf_op jit(solution)/shard_map/ppermute | solution.py:319
  88.5 3.2 %collective-permute-done.23 = bf16[96,512]{1,0:T(8,128)(2,1)S(1)} collective-permute-done((bf16[96,512]{1,0:T(8,128)(2,1)S(1)}, bf16[96,512]{1,0:T(8,128)(2,1)S(1)}, u32[]{:S(2)}, u32[]{:S(2)}) %collective-permute-start.23) | collective-permute-done | bytes 98336 | tf_op jit(solution)/shard_map/ppermute | solution.py:319
  91.7 6.7 %collective-permute-start.24 = (f32[96,512]{1,0:T(8,128)S(1)}, f32[96,512]{1,0:T(8,128)S(1)}, u32[]{:S(2)}, u32[]{:S(2)}) collective-permute-start(f32[96,512]{1,0:T(8,128)S(1)} %convert_add_fusion.mine_ref), channel_id=1, source_target_pairs={{0,8},{8,0},{16,24},{24,16},{32,40},{40,32},{48,56},{56,48},{64,72... | collective-permute-start | bytes 589832 | tf_op jit(solution)/shard_map/ppermute | solution.py:277
  (65 shorter events, 10.9 us)
Async XLA Ops:
  3.1 7.4 %copy-start.3 = (s32[9,768]{1,0:T(8,128)S(1)}, s32[9,768]{1,0:T(8,128)}, u32[]{:S(2)}) copy-start(s32[9,768]{1,0:T(8,128)} %in_ref.1) | copy-start | bytes 82948
  3.1 7.4 %copy-start.4 = (s32[9,768]{1,0:T(8,128)S(1)}, s32[9,768]{1,0:T(8,128)}, u32[]{:S(2)}) copy-start(s32[9,768]{1,0:T(8,128)} %out_ref.1) | copy-start | bytes 82948
  3.1 7.4 %copy-start.5 = (f32[9,768]{1,0:T(8,128)S(1)}, f32[9,768]{1,0:T(8,128)}, u32[]{:S(2)}) copy-start(f32[9,768]{1,0:T(8,128)} %cos_ref.1) | copy-start | bytes 82948
  3.1 7.4 %copy-start.6 = (s32[9,12]{1,0:T(8,128)S(1)}, s32[9,12]{1,0:T(8,128)}, u32[]{:S(2)}) copy-start(s32[9,12]{1,0:T(8,128)} %counts_ref.1) | copy-start | bytes 1300
  3.1 8.9 %copy-start.2 = (bf16[512,64]{0,1:T(8,128)(2,1)S(1)}, bf16[512,64]{0,1:T(8,128)(2,1)}, u32[]{:S(2)}) copy-start(bf16[512,64]{0,1:T(8,128)(2,1)} %param.12) | copy-start | bytes 196612
  3.9 14.7 %collective-permute-start.1 = (bf16[64,2048]{1,0:T(8,128)(2,1)S(1)}, bf16[64,2048]{1,0:T(8,128)(2,1)S(1)}, u32[]{:S(2)}, u32[]{:S(2)}) collective-permute-start(bf16[64,2048]{1,0:T(8,128)(2,1)S(1)} %get-tuple-element.45.down_ref.refs_0_), channel_id=1, source_target_pairs={{0,7},{1,2},{2,1},{3,4},{4,3},{5,6},{6,5},{7,0},{8,15},{9,10},{10,... | collective-permute-start | bytes 786440 | tf_op jit(solution)/shard_map/ppermute | solution.py:277
  10.4 8.3 %collective-permute-start = (bf16[64,2048]{1,0:T(8,128)(2,1)S(1)}, bf16[64,2048]{1,0:T(8,128)(2,1)S(1)}, u32[]{:S(2)}, u32[]{:S(2)}) collective-permute-start(bf16[64,2048]{1,0:T(8,128)(2,1)S(1)} %get-tuple-element.45.down_ref.refs_0_), channel_id=1, source_target_pairs={{0,1},{1,0},{2,3},{3,2},{4,5},{5,4},{6,7},{7,6},{8,9},{9,8},{10,11... | collective-permute-start | bytes 786440 | tf_op jit(solution)/shard_map/ppermute | solution.py:277
  13.1 7.2 %collective-permute-start.3 = (bf16[64,2048]{1,0:T(8,128)(2,1)S(1)}, bf16[64,2048]{1,0:T(8,128)(2,1)S(1)}, u32[]{:S(2)}, u32[]{:S(2)}) collective-permute-start(bf16[64,2048]{1,0:T(8,128)(2,1)S(1)} %get-tuple-element.51), channel_id=1, source_target_pairs={{0,248},{8,16},{16,8},{24,32},{32,24},{40,48},{48,40},{56,64},{64,... | collective-permute-start | bytes 786440 | tf_op jit(solution)/shard_map/ppermute | solution.py:277
  15.3 7.1 %collective-permute-start.5 = (bf16[64,2048]{1,0:T(8,128)(2,1)S(1)}, bf16[64,2048]{1,0:T(8,128)(2,1)S(1)}, u32[]{:S(2)}, u32[]{:S(2)}) collective-permute-start(bf16[64,2048]{1,0:T(8,128)(2,1)S(1)} %get-tuple-element.51), channel_id=1, source_target_pairs={{0,8},{8,0},{16,24},{24,16},{32,40},{40,32},{48,56},{56,48},{64,72... | collective-permute-start | bytes 786440 | tf_op jit(solution)/shard_map/ppermute | solution.py:277
  18.6 3.9 %collective-permute-start.7 = (bf16[64,2048]{1,0:T(8,128)(2,1)S(1)}, bf16[64,2048]{1,0:T(8,128)(2,1)S(1)}, u32[]{:S(2)}, u32[]{:S(2)}) collective-permute-start(bf16[64,2048]{1,0:T(8,128)(2,1)S(1)} %collective-permute-done.1.refs_3_), channel_id=1, source_target_pairs={{0,8},{8,0},{16,24},{24,16},{32,40},{40,32},{48,56},{56,48},{64,72... | collective-permute-start | bytes 786440 | tf_op jit(solution)/shard_map/ppermute | solution.py:277
  18.7 3.7 %collective-permute-start.6 = (bf16[64,2048]{1,0:T(8,128)(2,1)S(1)}, bf16[64,2048]{1,0:T(8,128)(2,1)S(1)}, u32[]{:S(2)}, u32[]{:S(2)}) collective-permute-start(bf16[64,2048]{1,0:T(8,128)(2,1)S(1)} %collective-permute-done.refs_2_), channel_id=1, source_target_pairs={{0,8},{8,0},{16,24},{24,16},{32,40},{40,32},{48,56},{56,48},{64,72... | collective-permute-start | bytes 786440 | tf_op jit(solution)/shard_map/ppermute | solution.py:277
  19.2 7.8 %collective-permute-start.2 = (bf16[96,2048]{1,0:T(8,128)(2,1)S(1)}, bf16[96,2048]{1,0:T(8,128)(2,1)S(1)}, u32[]{:S(2)}, u32[]{:S(2)}) collective-permute-start(bf16[96,2048]{1,0:T(8,128)(2,1)S(1)} %pad_maximum_fusion), channel_id=1, source_target_pairs={{0,248},{8,16},{16,8},{24,32},{32,24},{40,48},{48,40},{56,64},{64,... | collective-permute-start | bytes 1179656 | tf_op jit(solution)/shard_map/ppermute | solution.py:277
  20.3 6.6 %collective-permute-start.4 = (bf16[32,2048]{1,0:T(8,128)(2,1)S(1)}, bf16[32,2048]{1,0:T(8,128)(2,1)S(1)}, u32[]{:S(2)}, u32[]{:S(2)}) collective-permute-start(bf16[32,2048]{1,0:T(8,128)(2,1)S(1)} %slice.41), channel_id=1, source_target_pairs={{0,7},{1,2},{2,1},{3,4},{4,3},{5,6},{6,5},{7,0},{8,15},{9,10},{10,... | collective-permute-start | bytes 393224 | tf_op jit(solution)/shard_map/ppermute | solution.py:277
  26.9 2.2 %copy-start.7 = (bf16[2048,512]{1,0:T(8,128)(2,1)S(1)}, bf16[2048,512]{1,0:T(8,128)(2,1)}, u32[]{:S(2)}) copy-start(bf16[2048,512]{1,0:T(8,128)(2,1)} %cot_ref.3) | copy-start | bytes 6291460
  34.3 15.6 %collective-permute-start.8 = (bf16[2,64,2048]{2,1,0:T(8,128)(2,1)S(1)}, bf16[2,64,2048]{2,1,0:T(8,128)(2,1)S(1)}, u32[]{:S(2)}, u32[]{:S(2)}) collective-permute-start(bf16[2,64,2048]{2,1,0:T(8,128)(2,1)S(1)} %get-tuple-element.63), channel_id=1, source_target_pairs={{0,248},{8,16},{16,8},{24,32},{32,24},{40,48},{48,40},{56,64},{64,... | collective-permute-start | bytes 1572872 | tf_op jit(solution)/shard_map/ppermute | solution.py:277
  40.5 9.4 %collective-permute-start.9 = (bf16[3,64,2048]{2,1,0:T(8,128)(2,1)S(1)}, bf16[3,64,2048]{2,1,0:T(8,128)(2,1)S(1)}, u32[]{:S(2)}, u32[]{:S(2)}) collective-permute-start(bf16[3,64,2048]{2,1,0:T(8,128)(2,1)S(1)} %get-tuple-element.64), channel_id=1, source_target_pairs={{0,8},{8,0},{16,24},{24,16},{32,40},{40,32},{48,56},{56,48},{64,72... | collective-permute-start | bytes 2359304 | tf_op jit(solution)/shard_map/ppermute | solution.py:277
  50.2 5.9 %collective-permute-start.10 = (bf16[64,2048]{1,0:T(8,128)(2,1)S(1)}, bf16[64,2048]{1,0:T(8,128)(2,1)S(1)}, u32[]{:S(2)}, u32[]{:S(2)}) collective-permute-start(bf16[64,2048]{1,0:T(8,128)(2,1)S(1)} %get-tuple-element.75), channel_id=1, source_target_pairs={{0,248},{8,16},{16,8},{24,32},{32,24},{40,48},{48,40},{56,64},{64,... | collective-permute-start | bytes 786440 | tf_op jit(solution)/shard_map/ppermute | solution.py:277
  50.3 5.8 %collective-permute-start.11 = (bf16[64,2048]{1,0:T(8,128)(2,1)S(1)}, bf16[64,2048]{1,0:T(8,128)(2,1)S(1)}, u32[]{:S(2)}, u32[]{:S(2)}) collective-permute-start(bf16[64,2048]{1,0:T(8,128)(2,1)S(1)} %get-tuple-element.66.after_ref), channel_id=1, source_target_pairs={{0,1},{1,0},{2,3},{3,2},{4,5},{5,4},{6,7},{7,6},{8,9},{9,8},{10,11... | collective-permute-start | bytes 786440 | tf_op jit(solution)/shard_map/ppermute | solution.py:277
  50.4 6.8 %collective-permute-start.12 = (bf16[64,2048]{1,0:T(8,128)(2,1)S(1)}, bf16[64,2048]{1,0:T(8,128)(2,1)S(1)}, u32[]{:S(2)}, u32[]{:S(2)}) collective-permute-start(bf16[64,2048]{1,0:T(8,128)(2,1)S(1)} %get-tuple-element.76), channel_id=1, source_target_pairs={{0,7},{1,2},{2,1},{3,4},{4,3},{5,6},{6,5},{7,0},{8,15},{9,10},{10,... | collective-permute-start | bytes 786440 | tf_op jit(solution)/shard_map/ppermute | solution.py:277
  57.2 24.7 %copy-start.10 = (bf16[512,64]{0,1:T(8,128)(2,1)S(1)}, bf16[512,64]{0,1:T(8,128)(2,1)}, u32[]{:S(2)}) copy-start(bf16[512,64]{0,1:T(8,128)(2,1)} %param.11) | copy-start | bytes 196612
  57.7 6.8 %collective-permute-start.13 = (f32[96,512]{1,0:T(8,128)S(1)}, f32[96,512]{1,0:T(8,128)S(1)}, u32[]{:S(2)}, u32[]{:S(2)}) collective-permute-start(f32[96,512]{1,0:T(8,128)S(1)} %get-tuple-element.78), channel_id=1, source_target_pairs={{0,8},{8,0},{16,24},{24,16},{32,40},{40,32},{48,56},{56,48},{64,72... | collective-permute-start | bytes 589832 | tf_op jit(solution)/shard_map/ppermute | solution.py:277
  64.5 5.0 %collective-permute-start.16 = (bf16[96,512]{1,0:T(8,128)(2,1)S(1)}, bf16[96,512]{1,0:T(8,128)(2,1)S(1)}, u32[]{:S(2)}, u32[]{:S(2)}) collective-permute-start(bf16[96,512]{1,0:T(8,128)(2,1)S(1)} %add_convert_fusion.2), channel_id=1, source_target_pairs={{0,80},{1,81},{2,82},{3,83},{4,84},{5,85},{6,86},{7,87},{8,88},{9,... | collective-permute-start | bytes 294920 | tf_op jit(solution)/shard_map/ppermute | solution.py:319
  64.6 5.9 %collective-permute-start.15 = (bf16[96,512]{1,0:T(8,128)(2,1)S(1)}, bf16[96,512]{1,0:T(8,128)(2,1)S(1)}, u32[]{:S(2)}, u32[]{:S(2)}) collective-permute-start(bf16[96,512]{1,0:T(8,128)(2,1)S(1)} %add_convert_fusion.2), channel_id=1, source_target_pairs={{0,64},{1,65},{2,66},{3,67},{4,68},{5,69},{6,70},{7,71},{8,72},{9,... | collective-permute-start | bytes 294920 | tf_op jit(solution)/shard_map/ppermute | solution.py:319
  64.7 5.8 %collective-permute-start.14 = (bf16[96,512]{1,0:T(8,128)(2,1)S(1)}, bf16[96,512]{1,0:T(8,128)(2,1)S(1)}, u32[]{:S(2)}, u32[]{:S(2)}) collective-permute-start(bf16[96,512]{1,0:T(8,128)(2,1)S(1)} %add_convert_fusion.2), channel_id=1, source_target_pairs={{0,16},{1,17},{2,18},{3,19},{4,20},{5,21},{6,22},{7,23},{8,24},{9,... | collective-permute-start | bytes 294920 | tf_op jit(solution)/shard_map/ppermute | solution.py:319
  70.6 7.0 %collective-permute-start.19 = (bf16[96,512]{1,0:T(8,128)(2,1)S(1)}, bf16[96,512]{1,0:T(8,128)(2,1)S(1)}, u32[]{:S(2)}, u32[]{:S(2)}) collective-permute-start(bf16[96,512]{1,0:T(8,128)(2,1)S(1)} %add_convert_fusion.1), channel_id=1, source_target_pairs={{0,240},{1,241},{2,242},{3,243},{4,244},{5,245},{6,246},{7,247},{8... | collective-permute-start | bytes 294920 | tf_op jit(solution)/shard_map/ppermute | solution.py:319
  72.5 6.7 %collective-permute-start.18 = (bf16[96,512]{1,0:T(8,128)(2,1)S(1)}, bf16[96,512]{1,0:T(8,128)(2,1)S(1)}, u32[]{:S(2)}, u32[]{:S(2)}) collective-permute-start(bf16[96,512]{1,0:T(8,128)(2,1)S(1)} %add_convert_fusion.1), channel_id=1, source_target_pairs={{0,192},{1,193},{2,194},{3,195},{4,196},{5,197},{6,198},{7,199},{8... | collective-permute-start | bytes 294920 | tf_op jit(solution)/shard_map/ppermute | solution.py:319
  72.5 6.7 %collective-permute-start.17 = (bf16[96,512]{1,0:T(8,128)(2,1)S(1)}, bf16[96,512]{1,0:T(8,128)(2,1)S(1)}, u32[]{:S(2)}, u32[]{:S(2)}) collective-permute-start(bf16[96,512]{1,0:T(8,128)(2,1)S(1)} %add_convert_fusion.1), channel_id=1, source_target_pairs={{0,48},{1,49},{2,50},{3,51},{4,52},{5,53},{6,54},{7,55},{8,56},{9,... | collective-permute-start | bytes 294920 | tf_op jit(solution)/shard_map/ppermute | solution.py:319
  79.2 6.8 %collective-permute-start.22 = (bf16[96,512]{1,0:T(8,128)(2,1)S(1)}, bf16[96,512]{1,0:T(8,128)(2,1)S(1)}, u32[]{:S(2)}, u32[]{:S(2)}) collective-permute-start(bf16[96,512]{1,0:T(8,128)(2,1)S(1)} %get-tuple-element.85), channel_id=1, source_target_pairs={{0,2},{1,3},{2,0},{3,1},{4,6},{5,7},{6,4},{7,5},{8,10},{9,11},{10,... | collective-permute-start | bytes 294920 | tf_op jit(solution)/shard_map/ppermute | solution.py:319
  79.4 6.5 %collective-permute-start.21 = (bf16[96,512]{1,0:T(8,128)(2,1)S(1)}, bf16[96,512]{1,0:T(8,128)(2,1)S(1)}, u32[]{:S(2)}, u32[]{:S(2)}) collective-permute-start(bf16[96,512]{1,0:T(8,128)(2,1)S(1)} %get-tuple-element.85), channel_id=1, source_target_pairs={{0,3},{1,2},{2,1},{3,0},{4,7},{5,6},{6,5},{7,4},{8,11},{9,10},{10,... | collective-permute-start | bytes 294920 | tf_op jit(solution)/shard_map/ppermute | solution.py:319
  81.1 5.8 %collective-permute-start.20 = (bf16[96,512]{1,0:T(8,128)(2,1)S(1)}, bf16[96,512]{1,0:T(8,128)(2,1)S(1)}, u32[]{:S(2)}, u32[]{:S(2)}) collective-permute-start(bf16[96,512]{1,0:T(8,128)(2,1)S(1)} %get-tuple-element.85), channel_id=1, source_target_pairs={{0,1},{1,0},{2,3},{3,2},{4,5},{5,4},{6,7},{7,6},{8,9},{9,8},{10,11... | collective-permute-start | bytes 294920 | tf_op jit(solution)/shard_map/ppermute | solution.py:319
  87.0 4.8 %collective-permute-start.23 = (bf16[96,512]{1,0:T(8,128)(2,1)S(1)}, bf16[96,512]{1,0:T(8,128)(2,1)S(1)}, u32[]{:S(2)}, u32[]{:S(2)}) collective-permute-start(bf16[96,512]{1,0:T(8,128)(2,1)S(1)} %add_convert_fusion), channel_id=1, source_target_pairs={{0,7},{1,6},{2,5},{3,4},{4,3},{5,2},{6,1},{7,0},{8,15},{9,14},{10,... | collective-permute-start | bytes 294920 | tf_op jit(solution)/shard_map/ppermute | solution.py:319
  91.7 7.8 %collective-permute-start.24 = (f32[96,512]{1,0:T(8,128)S(1)}, f32[96,512]{1,0:T(8,128)S(1)}, u32[]{:S(2)}, u32[]{:S(2)}) collective-permute-start(f32[96,512]{1,0:T(8,128)S(1)} %convert_add_fusion.mine_ref), channel_id=1, source_target_pairs={{0,8},{8,0},{16,24},{24,16},{32,40},{40,32},{48,56},{56,48},{64,72... | collective-permute-start | bytes 589832 | tf_op jit(solution)/shard_map/ppermute | solution.py:277
  (4 other events, 6.6 us)
